TPU v7x, 32 devices: a whole 2x2x4 slice. The times are simulated.
32 devices in a mesh: seg: 4 (over z), tok: 8 (over y, x, core).
Axes of the slice: x: 2, y: 2, z: 4, core: 2. Of those that a mesh axis runs over, the one named last changes fastest.
Arguments:
- layer_input: bfloat16 [8, 512, 1024], P('seg', 'tok'), may hold values from -6 to 6
- prev_rows: float32 [2, 8, 1024], P(None, 'seg'), may hold values from -6 to 6
- init_state: float32 [3, 8, 1024], P(None, 'seg'), may hold values from -5 to 12, as said below
- time_decay: float32 [1024], replicated, may hold values from -12 to -3
- time_first: float32 [1024], replicated, may hold values from 0 to 1.5
- mix_ratios: float32 [5, 1024], replicated, may hold values from 0.1 to 0.9
- norm_gain: float32 [2, 1024], replicated, may hold values from 0.5 to 1.5
- norm_bias: float32 [2, 1024], replicated, may hold values from -1.2 to 1.2
- att_weights: bfloat16 [3, 1024, 1024], replicated, may hold values from -0.1875 to 0.1875
- att_output: bfloat16 [1024, 1024], replicated, may hold values from -0.75 to 0.75
- ffn_receptance: bfloat16 [1024, 1024], replicated, may hold values from -0.1875 to 0.1875
- ffn_key: bfloat16 [1024, 4096], P(None, 'tok'), may hold values from -0.1875 to 0.1875
- ffn_value: bfloat16 [4096, 1024], P('tok'), may hold values from -0.09375 to 0.09375
- cotangent: bfloat16 [8, 512, 1024], P('seg', 'tok'), may hold values from -6 to 6
Outputs:
- layer_out: bfloat16 [8, 512, 1024], P('seg', 'tok')
- grad_input: float32 [8, 512, 1024], P('seg', 'tok')
- grad_prev_rows: float32 [2, 8, 1024], P(None, 'seg', 'tok')
- grad_init_state: float32 [3, 8, 1024], P(None, 'seg', 'tok')
- grad_time_decay: float32 [1024], P(('seg', 'tok'))
- grad_time_first: float32 [1024], P(('seg', 'tok'))
- grad_mix_ratios: float32 [5, 1024], P(None, ('seg', 'tok'))
- grad_norm_gain: float32 [2, 1024], P(None, ('seg', 'tok'))
- grad_norm_bias: float32 [2, 1024], P(None, ('seg', 'tok'))
- grad_att_weights: float32 [3, 1024, 1024], P(None, 'tok', 'seg')
- grad_att_output: float32 [1024, 1024], P('tok', 'seg')
- grad_ffn_receptance: float32 [1024, 1024], P('tok', 'seg')
- grad_ffn_key: float32 [1024, 4096], P('seg', 'tok')
- grad_ffn_value: float32 [4096, 1024], P('tok', 'seg')
Inputs may be any that keep to these rules, and one draw needn't show every extreme that they name: init_state[1] is positive.
All inputs are finite; a program needn't handle non-finite values.
Results may differ from a plain program's by a relative error of at most 0.025.
Values may be sent and summed in bfloat16 or wider, within the bound.
A program may use at most 192 MiB of HBM per device.

v0:
```python
import jax
import jax.numpy as jnp
from jax import lax
from jax.sharding import PartitionSpec as P

norm_eps = 1e-05
floor_exp = -1e30


def from_behind(shard, axis, by):
    size = lax.axis_size(axis)
    pairs = [(i, i + by) for i in range(size) if 0 <= i + by < size]
    return lax.ppermute(shard, axis, pairs)


def prefix(shard, axis, combine, identity):
    size, place = (lax.axis_size(axis), lax.axis_index(axis))
    everything = jax.tree.map(
        lambda part, kind: lax.all_gather(part.astype(kind), axis),
        shard,
        (jnp.bfloat16, jnp.bfloat16, jnp.bfloat16, jnp.bfloat16),
    )
    start = jax.tree.map(
        lambda part, zero: jnp.broadcast_to(jnp.asarray(zero, part.dtype), part.shape),
        shard,
        identity,
    )

    def prefix_turn(k, before):
        reached = k < place
        new = combine(
            before, jax.tree.map(lambda part, own: part[k].astype(own.dtype), everything, shard)
        )
        return jax.tree.map(lambda a, b: jnp.where(reached, a, b), new, before)

    return lax.fori_loop(0, size, prefix_turn, start)


def carried_in(value, axis, join, neutral):
    count, mine = (lax.axis_size(axis), lax.axis_index(axis))
    pieces = jax.tree.map(lambda part: lax.all_gather(part, axis), value)
    pieces = jax.tree.map(lambda part: part[::-1], pieces)
    mine = count - 1 - mine
    so_far = jax.tree.map(
        lambda part, zero: jnp.full_like(part, 0) + jnp.asarray(zero, part.dtype), value, neutral
    )

    def carried_turn(position, so_far):
        longer = join(so_far, jax.tree.map(lambda part: part[position], pieces))
        return jax.tree.map(lambda new, old: jnp.where(position < mine, new, old), longer, so_far)

    return lax.fori_loop(0, count - 1, carried_turn, so_far)


def layer_norm(rows_in, gain_row, bias_row):
    centred = rows_in - jnp.mean(rows_in, axis=-1, keepdims=True)
    inv_scale = lax.rsqrt(jnp.mean(centred * centred, axis=-1, keepdims=True) + norm_eps)
    normed = centred * inv_scale
    return (normed * gain_row + bias_row, normed, inv_scale)


def norm_back(grad_out, normed, inv_scale, gain_row):
    grad_norm = grad_out * gain_row
    grad_rows = inv_scale * (
        grad_norm
        - jnp.mean(grad_norm, axis=-1, keepdims=True)
        - normed * jnp.mean(grad_norm * normed, axis=-1, keepdims=True)
    )
    return (grad_rows, jnp.sum(grad_out * normed, axis=(0, 1)), jnp.sum(grad_out, axis=(0, 1)))


def project(rows_in, weight_mat):
    return jnp.einsum("std,de->ste", rows_in, weight_mat, preferred_element_type=jnp.float32)


def project_back(grads_in, weight_mat):
    return jnp.einsum("ste,de->std", grads_in, weight_mat, preferred_element_type=jnp.float32)


def outer_sum(rows_in, grads_in):
    return jnp.einsum("std,ste->de", rows_in, grads_in, preferred_element_type=jnp.float32)


def with_prior(rows_now, head_row):
    return jnp.concatenate([head_row[:, None, :], rows_now[:, :-1, :]], axis=1)


def from_next(grad_prior, right_row):
    return jnp.concatenate([grad_prior[:, 1:, :], right_row[:, None, :]], axis=1)


def combine_states(earlier, latter):
    lead_exp = earlier[2] + latter[3]
    peak_new = jnp.maximum(lead_exp, latter[2])
    early_weight = jnp.exp(lead_exp - peak_new)
    late_weight = jnp.exp(latter[2] - peak_new)
    return (
        earlier[0] * early_weight + latter[0] * late_weight,
        earlier[1] * early_weight + latter[1] * late_weight,
        peak_new,
        earlier[3] + latter[3],
    )


def jac_matrix(initial_memory_trio, summed):
    lead_exp = initial_memory_trio[2] + summed[3]
    peak_new = jnp.maximum(lead_exp, summed[2])
    early_weight = jnp.exp(lead_exp - peak_new)
    late_weight = jnp.exp(summed[2] - peak_new)
    end_num = initial_memory_trio[0] * early_weight + summed[0] * late_weight
    end_den = initial_memory_trio[1] * early_weight + summed[1] * late_weight
    picked = (lead_exp >= summed[2]).astype(jnp.float32)
    zero_rows = jnp.zeros_like(early_weight)
    return jnp.stack(
        [
            jnp.stack([early_weight, zero_rows, zero_rows]),
            jnp.stack([zero_rows, early_weight, zero_rows]),
            jnp.stack(
                [
                    initial_memory_trio[0] * early_weight - picked * end_num,
                    initial_memory_trio[1] * early_weight - picked * end_den,
                    picked,
                ]
            ),
        ]
    )


def combine_grads(earlier, latter):
    mat_new = jnp.sum(latter[0][:, :, None] * earlier[0][None, :, :], axis=1)
    vec_new = latter[1] + jnp.sum(latter[0] * earlier[1][None], axis=1)
    return (mat_new, vec_new)


def span_summary(lookup_line_pile, payload_line_pile, fading_rate_vector):
    span_len = lookup_line_pile.shape[1]
    offsets = jnp.arange(span_len, dtype=jnp.float32)
    tail_exp = (span_len - 1.0 - offsets)[None, :, None] * fading_rate_vector + lookup_line_pile
    peak_end = jnp.max(tail_exp, axis=1)
    tail_weight = jnp.exp(tail_exp - peak_end[:, None, :])
    span_decay = jnp.broadcast_to(span_len * fading_rate_vector, peak_end.shape)
    return (
        jnp.sum(tail_weight * payload_line_pile, axis=1),
        jnp.sum(tail_weight, axis=1),
        peak_end,
        span_decay,
    )


def averaged_pair_segment(
    prior_memory, layer_entry_lines, fading_rate_vector, initial_reward_summand
):
    num_in, den_in, prior_maximum = prior_memory
    lookup_segment, value_blk = layer_entry_lines
    block_len = lookup_segment.shape[1]
    offsets = jnp.arange(block_len, dtype=jnp.float32)
    later_position = offsets[:, None]
    earlier_position = offsets[None, :]
    gap_len = (later_position - 1.0 - earlier_position)[None, :, :, None]
    pairwise_exponent = gap_len * fading_rate_vector + lookup_segment[:, None, :, :]
    pairwise_exponent = jnp.where(
        (earlier_position < later_position)[None, :, :, None], pairwise_exponent, floor_exp
    )
    pairwise_exponent = jnp.where(
        (earlier_position == later_position)[None, :, :, None],
        initial_reward_summand + lookup_segment[:, :, None, :],
        pairwise_exponent,
    )
    carry_exp = prior_maximum[:, None, :] + offsets[None, :, None] * fading_rate_vector
    peak_row = jnp.maximum(jnp.max(pairwise_exponent, axis=2), carry_exp)
    pair_weight = jnp.exp(pairwise_exponent - peak_row[:, :, None, :])
    carry_weight = jnp.exp(carry_exp - peak_row)
    numerator = carry_weight * num_in[:, None, :] + jnp.sum(
        pair_weight * value_blk[:, None, :, :], axis=2
    )
    denominator = carry_weight * den_in[:, None, :] + jnp.sum(pair_weight, axis=2)
    tail_exp = (block_len - 1.0 - offsets)[None, :, None] * fading_rate_vector + lookup_segment
    ahead_exp = prior_maximum + block_len * fading_rate_vector
    peak_end = jnp.maximum(jnp.max(tail_exp, axis=1), ahead_exp)
    tail_weight = jnp.exp(tail_exp - peak_end[:, None, :])
    ahead_weight = jnp.exp(ahead_exp - peak_end)
    state_out = (
        ahead_weight * num_in + jnp.sum(tail_weight * value_blk, axis=1),
        ahead_weight * den_in + jnp.sum(tail_weight, axis=1),
        peak_end,
    )
    return (state_out, numerator / denominator)


def weighted_kv_range(
    initial_memory_trio,
    lookup_line_pile,
    payload_line_pile,
    fading_rate_vector,
    initial_reward_summand,
):
    seq_count, span_len, width_all = lookup_line_pile.shape
    block_len = max(16, span_len // 16)
    block_count = span_len // block_len

    def split_blocks(rows_in):
        return rows_in.reshape(seq_count, block_count, block_len, width_all).transpose(1, 0, 2, 3)

    def one_block(prior_memory, layer_entry_lines):
        return averaged_pair_segment(
            prior_memory, layer_entry_lines, fading_rate_vector, initial_reward_summand
        )

    end_state, mixed_out = lax.scan(
        jax.checkpoint(one_block),
        initial_memory_trio,
        (split_blocks(lookup_line_pile), split_blocks(payload_line_pile)),
    )
    mixed_out = mixed_out.transpose(1, 0, 2, 3).reshape(seq_count, span_len, width_all)
    return (mixed_out, end_state)


def on_device(
    layer_input,
    prev_rows,
    init_state,
    time_decay,
    time_first,
    mix_ratios,
    norm_gain,
    norm_bias,
    att_weights,
    att_output,
    ffn_receptance,
    ffn_key,
    ffn_value,
    cotangent,
):
    tok_first = lax.axis_index("tok") == 0
    inputs = layer_input.astype(jnp.float32)
    first_norm, normed_one, scale_one = layer_norm(inputs, norm_gain[0], norm_bias[0])
    from_left = from_behind(first_norm[:, -1, :], "tok", 1)
    prior_one = with_prior(first_norm, jnp.where(tok_first, prev_rows[0], from_left))
    mixed_in = [
        (first_norm * mix_ratios[member] + prior_one * (1.0 - mix_ratios[member])).astype(
            jnp.bfloat16
        )
        for member in range(3)
    ]
    lookup_line_pile = project(mixed_in[0], att_weights[0])
    payload_line_pile = project(mixed_in[1], att_weights[1])
    gate_pre = project(mixed_in[2], att_weights[2])
    fading_rate_vector = -jnp.exp(time_decay)
    local_sum = span_summary(lookup_line_pile, payload_line_pile, fading_rate_vector)
    zero_rows = jnp.zeros_like(local_sum[0])
    floor_rows = jnp.full_like(local_sum[0], floor_exp)
    before = prefix(
        (local_sum[0], local_sum[1], local_sum[2], local_sum[3]),
        "tok",
        combine_states,
        (zero_rows, zero_rows, floor_rows, zero_rows),
    )
    init_three = (init_state[0], init_state[1], init_state[2])
    start_full = combine_states((init_state[0], init_state[1], init_state[2], zero_rows), before)
    initial_memory_trio = (start_full[0], start_full[1], start_full[2])
    (wkv_out, end_unused), pull_fn = jax.vjp(
        weighted_kv_range,
        initial_memory_trio,
        lookup_line_pile,
        payload_line_pile,
        fading_rate_vector,
        time_first,
    )
    gate_sig = jax.nn.sigmoid(gate_pre)
    weighted = (gate_sig * wkv_out).astype(jnp.bfloat16)
    middle = inputs + project(weighted, att_output)
    second_norm, normed_two, scale_two = layer_norm(middle, norm_gain[1], norm_bias[1])
    from_left_two = from_behind(second_norm[:, -1, :], "tok", 1)
    prior_two = with_prior(second_norm, jnp.where(tok_first, prev_rows[1], from_left_two))
    mix_key_two = (second_norm * mix_ratios[3] + prior_two * (1.0 - mix_ratios[3])).astype(
        jnp.bfloat16
    )
    mix_gate_two = (second_norm * mix_ratios[4] + prior_two * (1.0 - mix_ratios[4])).astype(
        jnp.bfloat16
    )
    gate_two = project(mix_gate_two, ffn_receptance)
    gate_two_sig = jax.nn.sigmoid(gate_two)
    key_full, value_full = (ffn_key, ffn_value)
    rows_all = lax.all_gather(mix_key_two, "tok", axis=1, tiled=True)
    hidden_pre = project(rows_all, key_full)
    relu_part = jnp.maximum(hidden_pre, 0.0)
    hidden = (relu_part * relu_part).astype(jnp.bfloat16)
    partial_out = project(hidden, value_full)
    value_two = lax.psum_scatter(partial_out, "tok", scatter_dimension=1, tiled=True)
    layer_out = (middle + gate_two_sig * value_two).astype(jnp.bfloat16)
    grad_top = cotangent.astype(jnp.float32)
    grad_value_two = (grad_top * gate_two_sig).astype(jnp.bfloat16)
    grad_gate_two = (grad_top * value_two * gate_two_sig * (1.0 - gate_two_sig)).astype(
        jnp.bfloat16
    )
    grads_all = lax.all_gather(grad_value_two, "tok", axis=1, tiled=True)
    grad_hidden = project_back(grads_all, value_full)
    grad_hidden_pre = (grad_hidden * 2.0 * relu_part).astype(jnp.bfloat16)
    grad_value_w = outer_sum(hidden, grads_all)
    grad_key_w = outer_sum(rows_all, grad_hidden_pre)
    grad_mix_key_all = project_back(grad_hidden_pre, key_full)
    grad_mix_key_two = lax.psum_scatter(grad_mix_key_all, "tok", scatter_dimension=1, tiled=True)
    grad_mix_gate_two = project_back(grad_gate_two, ffn_receptance)
    grad_recept_w = outer_sum(mix_gate_two, grad_gate_two)
    step_two = second_norm - prior_two
    grad_prior_two = grad_mix_key_two * (1.0 - mix_ratios[3]) + grad_mix_gate_two * (
        1.0 - mix_ratios[4]
    )
    from_right_two = from_behind(grad_prior_two[:, 0, :], "tok", -1)
    grad_second = (
        grad_mix_key_two * mix_ratios[3]
        + grad_mix_gate_two * mix_ratios[4]
        + from_next(grad_prior_two, from_right_two)
    )
    prev_grad_two = jnp.where(tok_first, grad_prior_two[:, 0, :], 0.0)
    ratio_three = jnp.sum(step_two * grad_mix_key_two, axis=(0, 1))
    ratio_four = jnp.sum(step_two * grad_mix_gate_two, axis=(0, 1))
    grad_mid_norm, gain_grad_two, bias_grad_two = norm_back(
        grad_second, normed_two, scale_two, norm_gain[1]
    )
    grad_middle = grad_top + grad_mid_norm
    grad_branch = grad_middle.astype(jnp.bfloat16)
    grad_weighted = project_back(grad_branch, att_output)
    grad_out_w = outer_sum(weighted, grad_branch)
    grad_wkv = grad_weighted * gate_sig
    grad_gate_pre = (grad_weighted * wkv_out * gate_sig * (1.0 - gate_sig)).astype(jnp.bfloat16)
    plain_outcome = pull_fn((grad_wkv, (zero_rows, zero_rows, zero_rows)))
    direct_vec = jnp.stack([plain_outcome[0][0], plain_outcome[0][1], plain_outcome[0][2]])
    local_jac = jac_matrix(initial_memory_trio, local_sum)
    eye_mat = jnp.broadcast_to(jnp.eye(3, dtype=jnp.float32)[:, :, None, None], local_jac.shape)
    after_scan = carried_in(
        (local_jac, direct_vec), "tok", combine_grads, (eye_mat, jnp.zeros_like(direct_vec))
    )
    next_grad = after_scan[1]
    running_memory = pull_fn((jnp.zeros_like(wkv_out), (next_grad[0], next_grad[1], next_grad[2])))
    grad_keys = (plain_outcome[1] + running_memory[1]).astype(jnp.bfloat16)
    grad_values = (plain_outcome[2] + running_memory[2]).astype(jnp.bfloat16)
    grad_decay = (plain_outcome[3] + running_memory[3]) * fading_rate_vector
    reward_cotangent = plain_outcome[4] + running_memory[4]
    init_term = jnp.sum(jac_matrix(init_three, before) * direct_vec[None], axis=1)
    grad_mix_one = [
        project_back(grad_keys, att_weights[0]),
        project_back(grad_values, att_weights[1]),
        project_back(grad_gate_pre, att_weights[2]),
    ]
    grad_att_w = jnp.stack(
        [
            outer_sum(mixed_in[0], grad_keys),
            outer_sum(mixed_in[1], grad_values),
            outer_sum(mixed_in[2], grad_gate_pre),
        ]
    )
    step_one = first_norm - prior_one
    grad_first_in = sum((grad_mix_one[member] * mix_ratios[member] for member in range(3)))
    grad_prior_one = sum((grad_mix_one[member] * (1.0 - mix_ratios[member]) for member in range(3)))
    ratio_low = [jnp.sum(step_one * grad_mix_one[member], axis=(0, 1)) for member in range(3)]
    from_right_one = from_behind(grad_prior_one[:, 0, :], "tok", -1)
    grad_first = grad_first_in + from_next(grad_prior_one, from_right_one)
    prev_grad_one = jnp.where(tok_first, grad_prior_one[:, 0, :], 0.0)
    grad_in_norm, gain_grad_one, bias_grad_one = norm_back(
        grad_first, normed_one, scale_one, norm_gain[0]
    )
    grad_input = grad_middle + grad_in_norm
    grad_ratios = jnp.stack([ratio_low[0], ratio_low[1], ratio_low[2], ratio_three, ratio_four])
    grad_gains = jnp.stack([gain_grad_one, gain_grad_two])
    grad_biases = jnp.stack([bias_grad_one, bias_grad_two])
    prev_term = jnp.stack([prev_grad_one, prev_grad_two])
    seg_sums = (
        lax.psum_scatter(
            grad_att_w.astype(jnp.bfloat16), "seg", scatter_dimension=2, tiled=True
        ).astype(jnp.float32),
        lax.psum_scatter(
            grad_out_w.astype(jnp.bfloat16), "seg", scatter_dimension=1, tiled=True
        ).astype(jnp.float32),
        lax.psum_scatter(
            grad_recept_w.astype(jnp.bfloat16), "seg", scatter_dimension=1, tiled=True
        ).astype(jnp.float32),
        lax.psum_scatter(
            grad_decay.astype(jnp.bfloat16), "seg", scatter_dimension=0, tiled=True
        ).astype(jnp.float32),
        lax.psum_scatter(
            reward_cotangent.astype(jnp.bfloat16), "seg", scatter_dimension=0, tiled=True
        ).astype(jnp.float32),
        lax.psum_scatter(
            grad_ratios.astype(jnp.bfloat16), "seg", scatter_dimension=1, tiled=True
        ).astype(jnp.float32),
        lax.psum_scatter(
            grad_gains.astype(jnp.bfloat16), "seg", scatter_dimension=1, tiled=True
        ).astype(jnp.float32),
        lax.psum_scatter(
            grad_biases.astype(jnp.bfloat16), "seg", scatter_dimension=1, tiled=True
        ).astype(jnp.float32),
        lax.psum_scatter(
            grad_key_w.astype(jnp.bfloat16), "seg", scatter_dimension=0, tiled=True
        ).astype(jnp.float32),
        lax.psum_scatter(
            grad_value_w.astype(jnp.bfloat16), "seg", scatter_dimension=1, tiled=True
        ).astype(jnp.float32),
    )
    tok_sums = (
        lax.psum_scatter(seg_sums[0], "tok", scatter_dimension=1, tiled=True),
        lax.psum_scatter(seg_sums[1], "tok", scatter_dimension=0, tiled=True),
        lax.psum_scatter(seg_sums[2], "tok", scatter_dimension=0, tiled=True),
        lax.psum_scatter(seg_sums[3], "tok", scatter_dimension=0, tiled=True),
        lax.psum_scatter(seg_sums[4], "tok", scatter_dimension=0, tiled=True),
        lax.psum_scatter(seg_sums[5], "tok", scatter_dimension=1, tiled=True),
        lax.psum_scatter(seg_sums[6], "tok", scatter_dimension=1, tiled=True),
        lax.psum_scatter(seg_sums[7], "tok", scatter_dimension=1, tiled=True),
        lax.psum_scatter(init_term, "tok", scatter_dimension=2, tiled=True),
        lax.psum_scatter(prev_term, "tok", scatter_dimension=2, tiled=True),
    )
    key_grad_out = seg_sums[8]
    value_grad_out = seg_sums[9]
    return (
        layer_out,
        grad_input,
        tok_sums[9],
        tok_sums[8],
        tok_sums[3],
        tok_sums[4],
        tok_sums[5],
        tok_sums[6],
        tok_sums[7],
        tok_sums[0],
        tok_sums[1],
        tok_sums[2],
        key_grad_out,
        value_grad_out,
    )


def solution(mesh):
    return jax.shard_map(
        on_device,
        mesh=mesh,
        in_specs=(
            P("seg", "tok", None),
            P(None, "seg", None),
            P(None, "seg", None),
            P(),
            P(),
            P(),
            P(),
            P(),
            P(),
            P(),
            P(),
            P(None, "tok"),
            P("tok", None),
            P("seg", "tok", None),
        ),
        out_specs=(
            P("seg", "tok", None),
            P("seg", "tok", None),
            P(None, "seg", "tok"),
            P(None, "seg", "tok"),
            P(("seg", "tok")),
            P(("seg", "tok")),
            P(None, ("seg", "tok")),
            P(None, ("seg", "tok")),
            P(None, ("seg", "tok")),
            P(None, "tok", "seg"),
            P("tok", "seg"),
            P("tok", "seg"),
            P("seg", "tok"),
            P("tok", "seg"),
        ),
        check_vma=False,
    )
```

profile of v0, /device:TPU:0, one launch (start us, length us, event | category | flops | bytes accessed | tf_op | source)
XLA Modules:
  0.0 1044.4 jit_solution(227998358096725049)
XLA Ops:
  12.5 2.4 collective-permute-start
  17.4 10.0 all-gather
  28.1 2.1 add_convert_fusion.5
  30.2 2.2 add_reduce_fusion.3
  32.6 9.1 all-gather.6
  41.7 2.1 fusion.137
  44.0 8.1 all-gather.7
  52.0 9.1 all-gather.8
  65.5 19.5 %while.117 = (s32[]{:T(128)}, f32[2,1024]{1,0:T(2,128)S(1)}, f32[2,1024]{1,0:T(2,128)S(1)}, f32[2,1024]{1,0:T(2,128)S(1)}, f32[4,2,16,1024]{3,2,1,0:T(8,128)}, /...) while((s32[]{:T(128)}, f32[2,1024]{1,0:T(2,128)S(1)}, ...), condition=%wide.region_14.15_spmd.clone.clone, body=%wide.region_7.14_spmd.clone.clone.sunk | while | flops 6563842 | bytes 6666497 | solution.py:209
  86.4 3.2 fusion.133
  90.6 2.2 collective-permute-start.1
  94.9 30.2 %all-gather.12.cloned.1.call-done = bf16[2,512,1024]{2,1,0:T(8,128)(2,1)} async-done(((bf16[2,64,1024]{2,1,0:T(8,128)(2,1)}), bf16[2,512,1024]{2,1,0:T(8,128)(2,1)}) %all-gather.12.cloned.1.call-update) | async-done | bytes 2097168 | tf_op jit(solution)/shard_map/all_gather | solution.py:284
  125.1 3.2 fusion.114
  129.7 3.2 fusion.110
  133.0 51.4 %reduce-scatter.33.cloned.1.call-done = f32[2,64,1024]{2,1,0:T(8,128)} async-done(((f32[2,512,1024]{2,1,0:T(8,128)}), f32[2,64,1024]{2,1,0:T(8,128)}) %reduce-scatter.33.cloned.1.call-update) | async-done | bytes 524304 | tf_op jit(solution)/shard_map/reduce_scatter | solution.py:289
  184.4 2.6 fusion.132
  187.3 27.8 %all-gather.14.cloned.1.call-done = bf16[2,512,1024]{2,1,0:T(8,128)(2,1)} async-done(((bf16[2,64,1024]{2,1,0:T(8,128)(2,1)}), bf16[2,512,1024]{2,1,0:T(8,128)(2,1)}) %all-gather.14.cloned.1.call-update) | async-done | bytes 2097168 | tf_op jit(solution)/shard_map/all_gather | solution.py:296
  215.1 3.9 multiply_convert_fusion
  220.0 3.2 fusion.112
  224.6 50.1 %reduce-scatter.35.cloned.1.call-done = f32[2,64,1024]{2,1,0:T(8,128)} async-done(((f32[2,512,1024]{2,1,0:T(8,128)}), f32[2,64,1024]{2,1,0:T(8,128)}) %reduce-scatter.35.cloned.1.call-update) | async-done | bytes 524304 | tf_op jit(solution)/shard_map/reduce_scatter | solution.py:302
  274.7 3.7 multiply_reduce_fusion.15
  280.5 11.6 %all-gather.5 = f32[24,3,2,1024]{3,2,1,0:T(2,128)S(1)} all-gather(f32[3,3,2,1024]{3,2,1,0:T(2,128)S(1)} %pad_maximum_fusion.3), channel_id=8, replica_groups=mesh['seg'=4,'tok'=8] {'tok'}, dimensions={0}, use_global_device_ids=true | all-gather | bytes 663552 | tf_op jit(solution)/shard_map/all_gather | solution.py:41
  298.6 35.4 %while.114 = (s32[]{:T(128)}, f32[1024]{0:T(1024)S(1)}, f32[1024]{0:T(1024)S(1)}, f32[2,1024]{1,0:T(2,128)S(1)}, f32[2,1024]{1,0:T(2,128)S(1)}, /*index=5*/f32[2...) while((s32[]{:T(128)}, f32[1024]{0:T(1024)S(1)}, ...), condition=%wide.region_44.45_spmd.clone, body=%wide.region_21.44_spmd.clone.sunk | while | flops 24124196 | bytes 18094132 | solution.py:209
  302.0 1.9 fusion.221
  304.0 2.2 select_reduce_fusion.6
  310.8 1.9 fusion.221
  312.9 2.2 select_reduce_fusion.6
  321.7 2.2 select_reduce_fusion.6
  330.6 2.2 select_reduce_fusion.6
  334.1 8.5 all-gather.4
  342.6 7.2 while.115
  351.5 35.3 %while.116 = (s32[]{:T(128)}, f32[1024]{0:T(1024)S(1)}, f32[1024]{0:T(1024)S(1)}, f32[2,1024]{1,0:T(2,128)S(1)}, f32[2,1024]{1,0:T(2,128)S(1)}, /*index=5*/f32[2...) while((s32[]{:T(128)}, f32[1024]{0:T(1024)S(1)}, ...), condition=%wide.region_71.72_spmd.clone, body=%wide.region_48.71_spmd.clone.sunk | while | flops 24118052 | bytes 17930280 | solution.py:209
  356.8 2.2 select_reduce_fusion.7
  365.7 2.2 select_reduce_fusion.7
  374.5 2.2 select_reduce_fusion.7
  383.3 2.2 select_reduce_fusion.7
  388.0 2.5 fusion.65
  390.7 2.5 fusion.61
  393.4 2.5 multiply_add_fusion.10
  403.1 3.1 bitcast_convert_fusion
  406.4 2.1 bitcast_convert_fusion.1
  412.1 3.1 pad_maximum_fusion
  416.8 3.9 bitcast_convert_fusion.5
  420.8 4.1 bitcast_convert_fusion.6
  426.9 17.7 %reduce-scatter.61.cloned.1.call-done = bf16[256,2]{1,0:T(8,128)(2,1)} async-done(((bf16[1024,2]{1,0:T(8,128)(2,1)}), bf16[256,2]{1,0:T(8,128)(2,1)}) %reduce-scatter.61.cloned.1.call-update) | async-done | bytes 1040
  448.5 16.1 %reduce-scatter.37.cloned.1.call-done = bf16[5,256]{1,0:T(8,128)(2,1)} async-done(((bf16[5,1024]{1,0:T(8,128)(2,1)}), bf16[5,256]{1,0:T(8,128)(2,1)}) %reduce-scatter.37.cloned.1.call-update) | async-done | bytes 2576 | tf_op jit(solution)/shard_map/reduce_scatter | solution.py:384
  468.7 40.4 %reduce-scatter.47.cloned.1.call-done = bf16[1024,256]{1,0:T(8,128)(2,1)} async-done(((bf16[1024,1024]{1,0:T(8,128)(2,1)}), bf16[1024,256]{1,0:T(8,128)(2,1)}) %reduce-scatter.47.cloned.1.call-update) | async-done | bytes 524304 | tf_op jit(solution)/shard_map/reduce_scatter | solution.py:375
  509.0 2.1 convert_element_type.279
  511.2 43.3 %reduce-scatter.43.cloned.1.call-done = bf16[1024,256]{1,0:T(8,128)(2,1)} async-done(((bf16[1024,1024]{1,0:T(8,128)(2,1)}), bf16[1024,256]{1,0:T(8,128)(2,1)}) %reduce-scatter.43.cloned.1.call-update) | async-done | bytes 524304 | tf_op jit(solution)/shard_map/reduce_scatter | solution.py:372
  554.6 2.1 convert_element_type.277
  556.7 110.2 %reduce-scatter.39.cloned.1.call-done = bf16[3,1024,256]{2,1,0:T(8,128)(2,1)} async-done(((bf16[3,1024,1024]{2,1,0:T(8,128)(2,1)}), bf16[3,1024,256]{2,1,0:T(8,128)(2,1)}) %reduce-scatter.39.cloned.1.call-update) | async-done | bytes 1572880 | tf_op jit(solution)/shard_map/reduce_scatter | solution.py:369
  666.9 3.3 convert_element_type.275
  673.5 23.5 %reduce-scatter.53.cloned.1.call-done = bf16[512,256]{1,0:T(8,128)(2,1)} async-done(((bf16[512,1024]{1,0:T(8,128)(2,1)}), bf16[512,256]{1,0:T(8,128)(2,1)}) %reduce-scatter.53.cloned.1.call-update) | async-done | bytes 262160 | tf_op jit(solution)/shard_map/reduce_scatter | solution.py:396
  698.8 26.2 %reduce-scatter.51.cloned.1.call-done = bf16[256,512]{1,0:T(8,128)(2,1)} async-done(((bf16[1024,512]{1,0:T(8,128)(2,1)}), bf16[256,512]{1,0:T(8,128)(2,1)}) %reduce-scatter.51.cloned.1.call-update) | async-done | bytes 262160 | tf_op jit(solution)/shard_map/reduce_scatter | solution.py:393
  726.8 9.4 all-reduce.7
  736.4 11.8 %all-reduce.6 = (f32[256]{0:T(256)S(1)}, f32[256]{0:T(256)S(1)}) all-reduce(f32[256]{0:T(256)S(1)} %dynamic-slice_convert_fusion.1, f32[256]{0:T(256)S(1)} %dynamic-slice_convert_fusion), channel_id=14, replica_groups=mesh['seg'=4,'tok'=8] {'tok'}, use_global_device_ids=true, to_apply=%region_78.79.clone | all-reduce | flops 512 | bytes 4096
  750.4 9.9 reduce-scatter.67.cloned.1.call-done
  761.7 34.9 %reduce-scatter.63.cloned.1.call-done = f32[32,2]{1,0:T(8,128)} async-done(((f32[256,2]{1,0:T(8,128)}), f32[32,2]{1,0:T(8,128)}) %reduce-scatter.63.cloned.1.call-update) | async-done | bytes 272
  797.9 36.1 %reduce-scatter.55.cloned.1.call-done = f32[128,4]{1,0:T(8,128)} async-done(((f32[1024,4]{1,0:T(8,128)}), f32[128,4]{1,0:T(8,128)}) %reduce-scatter.55.cloned.1.call-update) | async-done | bytes 2064
  835.6 34.6 %reduce-scatter.59.cloned.1.call-done = f32[32,5]{1,0:T(8,128)} async-done(((f32[256,5]{1,0:T(8,128)}), f32[32,5]{1,0:T(8,128)}) %reduce-scatter.59.cloned.1.call-update) | async-done | bytes 656
  871.6 36.0 %reduce-scatter.57.cloned.1.call-done = f32[128,6]{1,0:T(8,128)} async-done(((f32[1024,6]{1,0:T(8,128)}), f32[128,6]{1,0:T(8,128)}) %reduce-scatter.57.cloned.1.call-update) | async-done | bytes 3088
  909.3 38.0 %reduce-scatter.49.cloned.1.call-done = f32[128,256]{1,0:T(8,128)} async-done(((f32[1024,256]{1,0:T(8,128)}), f32[128,256]{1,0:T(8,128)}) %reduce-scatter.49.cloned.1.call-update) | async-done | bytes 131088 | tf_op jit(solution)/shard_map/reduce_scatter | solution.py:403
  947.3 39.8 %reduce-scatter.45.cloned.1.call-done = f32[128,256]{1,0:T(8,128)} async-done(((f32[1024,256]{1,0:T(8,128)}), f32[128,256]{1,0:T(8,128)}) %reduce-scatter.45.cloned.1.call-update) | async-done | bytes 131088 | tf_op jit(solution)/shard_map/reduce_scatter | solution.py:402
  987.0 50.1 %reduce-scatter.41.cloned.1.call-done = f32[3,128,256]{2,1,0:T(8,128)} async-done(((f32[3,1024,256]{2,1,0:T(8,128)}), f32[3,128,256]{2,1,0:T(8,128)}) %reduce-scatter.41.cloned.1.call-update) | async-done | bytes 393232 | tf_op jit(solution)/shard_map/reduce_scatter | solution.py:401
  (756 shorter events, 144.1 us)
Async XLA Ops:
  7.2 177.2 %copy-start = (bf16[1024,1024]{1,0:T(8,128)(2,1)S(1)}, bf16[1024,1024]{1,0:T(8,128)(2,1)}, u32[]{:S(2)}) copy-start(bf16[1024,1024]{1,0:T(8,128)(2,1)} %param.34) | copy-start | bytes 6291460
  7.2 117.9 %all-gather.12.cloned.1.call-start = ((), (), s32[]{:S(2)}) async-start(), calls=%async_computation.18 | async-start | bytes 2359296 | tf_op jit(solution)/shard_map/all_gather | solution.py:284
  8.5 24.0 %copy-start.60 = (f32[2,64]{1,0:T(2,128)}, f32[2,64]{1,0:T(2,128)S(1)}, u32[]{:S(2)}) copy-start(f32[2,64]{1,0:T(2,128)S(1)} %broadcast_multiply_fusion.14) | copy-start | bytes 1540
  9.6 22.9 %copy-start.82 = (f32[2,64]{1,0:T(2,128)}, f32[2,64]{1,0:T(2,128)S(1)}, u32[]{:S(2)}) copy-start(f32[2,64]{1,0:T(2,128)S(1)} %add_rsqrt_fusion.1) | copy-start | bytes 1540
  10.4 22.1 %copy-start.41 = (f32[1,1024]{1,0:T(1,128)}, f32[1,1024]{1,0:T(1,128)S(1)}, u32[]{:S(2)}) copy-start(f32[1,1024]{1,0:T(1,128)S(1)} %get-tuple-element.1686) | copy-start | bytes 12292
  10.4 83.2 %copy-start.43 = (f32[1,1024]{1,0:T(1,128)}, f32[1,1024]{1,0:T(1,128)S(1)}, u32[]{:S(2)}) copy-start(f32[1,1024]{1,0:T(1,128)S(1)} %get-tuple-element.1685) | copy-start | bytes 12292
  11.2 21.3 %copy-start.50 = (f32[1,1024]{1,0:T(1,128)}, f32[1,1024]{1,0:T(1,128)S(1)}, u32[]{:S(2)}) copy-start(f32[1,1024]{1,0:T(1,128)S(1)} %get-tuple-element.1688) | copy-start | bytes 12292
  12.4 20.1 %copy-start.10 = (f32[2,64,1024]{2,1,0:T(8,128)}, f32[2,64,1024]{2,1,0:T(8,128)S(1)}, u32[]{:S(2)}) copy-start(f32[2,64,1024]{2,1,0:T(8,128)S(1)} %fusion.122) | copy-start | bytes 1572868
  12.5 14.9 %collective-permute-start = (f32[2,1024]{1,0:T(2,128)S(1)}, f32[2,1024]{1,0:T(2,128)S(1)}, u32[]{:S(2)}, u32[]{:S(2)}) collective-permute-start(f32[2,1024]{1,0:T(2,128)S(1)} %bitcast.519), channel_id=1, source_target_pairs={{0,1},{1,2},{2,3},{3,4},{4,5},{5,6},{6,7},{8,9},{9,10},{10,11},{11... | collective-permute-start | bytes 24584 | tf_op jit(solution)/shard_map/ppermute | solution.py:13
  15.7 47.4 %copy-start.70 = (f32[1024]{0:T(1024)}, f32[1024]{0:T(1024)S(1)}, u32[]{:S(2)}) copy-start(f32[1024]{0:T(1024)S(1)} %get-tuple-element.1689) | copy-start | bytes 12292
  16.6 15.9 %copy-start.52 = (f32[1,1024]{1,0:T(1,128)}, f32[1,1024]{1,0:T(1,128)S(1)}, u32[]{:S(2)}) copy-start(f32[1,1024]{1,0:T(1,128)S(1)} %get-tuple-element.1674) | copy-start | bytes 12292
  16.6 15.9 %copy-start.54 = (f32[1,1024]{1,0:T(1,128)}, f32[1,1024]{1,0:T(1,128)S(1)}, u32[]{:S(2)}) copy-start(f32[1,1024]{1,0:T(1,128)S(1)} %get-tuple-element.1672) | copy-start | bytes 12292
  16.7 15.9 %copy-start.56 = (f32[1,1024]{1,0:T(1,128)}, f32[1,1024]{1,0:T(1,128)S(1)}, u32[]{:S(2)}) copy-start(f32[1,1024]{1,0:T(1,128)S(1)} %get-tuple-element.1673) | copy-start | bytes 12292
  16.7 77.0 %copy-start.58 = (f32[1,1024]{1,0:T(1,128)}, f32[1,1024]{1,0:T(1,128)S(1)}, u32[]{:S(2)}) copy-start(f32[1,1024]{1,0:T(1,128)S(1)} %get-tuple-element.1671) | copy-start | bytes 12292
  16.7 77.0 %copy-start.59 = (f32[1,1024]{1,0:T(1,128)}, f32[1,1024]{1,0:T(1,128)S(1)}, u32[]{:S(2)}) copy-start(f32[1,1024]{1,0:T(1,128)S(1)} %get-tuple-element.1675) | copy-start | bytes 12292
  16.7 15.9 %copy-start.64 = (f32[1024]{0:T(1024)}, f32[1024]{0:T(1024)S(1)}, u32[]{:S(2)}) copy-start(f32[1024]{0:T(1024)S(1)} %broadcast_subtract_fusion.4) | copy-start | bytes 12292
  16.7 15.9 %copy-start.66 = (f32[1024]{0:T(1024)}, f32[1024]{0:T(1024)S(1)}, u32[]{:S(2)}) copy-start(f32[1024]{0:T(1024)S(1)} %get-tuple-element.1704) | copy-start | bytes 12292
  16.7 15.9 %copy-start.68 = (f32[1024]{0:T(1024)}, f32[1024]{0:T(1024)S(1)}, u32[]{:S(2)}) copy-start(f32[1024]{0:T(1024)S(1)} %get-tuple-element.1705) | copy-start | bytes 12292
  30.2 13.6 %copy-start.22 = (bf16[2,64,1024]{2,1,0:T(8,128)(2,1)}, bf16[2,64,1024]{2,1,0:T(8,128)(2,1)S(1)}, u32[]{:S(2)}) copy-start(bf16[2,64,1024]{2,1,0:T(8,128)(2,1)S(1)} %get-tuple-element.1664) | copy-start | bytes 786436
  30.2 13.6 %copy-start.24 = (bf16[2,64,1024]{2,1,0:T(8,128)(2,1)}, bf16[2,64,1024]{2,1,0:T(8,128)(2,1)S(1)}, u32[]{:S(2)}) copy-start(bf16[2,64,1024]{2,1,0:T(8,128)(2,1)S(1)} %get-tuple-element.1663) | copy-start | bytes 786436
  32.6 11.3 %copy-start.36 = (f32[2,64,1024]{2,1,0:T(8,128)}, f32[2,64,1024]{2,1,0:T(8,128)S(1)}, u32[]{:S(2)}) copy-start(f32[2,64,1024]{2,1,0:T(8,128)S(1)} %get-tuple-element.1694) | copy-start | bytes 1572868
  43.8 17.3 %copy-start.78 = (f32[2,1024]{1,0:T(2,128)}, f32[2,1024]{1,0:T(2,128)S(1)}, u32[]{:S(2)}) copy-start(f32[2,1024]{1,0:T(2,128)S(1)} %get-tuple-element.1442) | copy-start | bytes 24580
  43.9 17.9 %copy-start.76 = (f32[2,1024]{1,0:T(2,128)}, f32[2,1024]{1,0:T(2,128)S(1)}, u32[]{:S(2)}) copy-start(f32[2,1024]{1,0:T(2,128)S(1)} %get-tuple-element.1441) | copy-start | bytes 24580
  43.9 21.7 %copy-start.34 = (f32[1024]{0:T(1024)S(1)}, f32[1024]{0:T(1024)}, u32[]{:S(2)}) copy-start(f32[1024]{0:T(1024)} %param.28) | copy-start | bytes 12292
  43.9 21.7 %copy-start.89 = (f32[16]{0:T(128)S(1)}, f32[16]{0:T(128)}, u32[]{:S(2)}) copy-start(f32[16]{0:T(128)} %iota_subtract_fusion.5) | copy-start | bytes 196
  90.1 38.2 %copy-start.62 = (f32[2,64]{1,0:T(2,128)}, f32[2,64]{1,0:T(2,128)S(1)}, u32[]{:S(2)}) copy-start(f32[2,64]{1,0:T(2,128)S(1)} %broadcast_multiply_fusion.13) | copy-start | bytes 1540
  90.3 38.0 %copy-start.85 = (f32[2,64]{1,0:T(2,128)}, f32[2,64]{1,0:T(2,128)S(1)}, u32[]{:S(2)}) copy-start(f32[2,64]{1,0:T(2,128)S(1)} %add_rsqrt_fusion) | copy-start | bytes 1540
  90.6 3.0 collective-permute-start.1
  92.8 35.5 %copy-start.74 = (f32[1024]{0:T(1024)}, f32[1024]{0:T(1024)S(1)}, u32[]{:S(2)}) copy-start(f32[1024]{0:T(1024)S(1)} %get-tuple-element.1708) | copy-start | bytes 12292
  92.8 35.5 %copy-start.75 = (f32[1024]{0:T(1024)}, f32[1024]{0:T(1024)S(1)}, u32[]{:S(2)}) copy-start(f32[1024]{0:T(1024)S(1)} %get-tuple-element.1709) | copy-start | bytes 12292
  93.6 34.7 %copy-start.49 = (f32[2,1,1024]{2,1,0:T(1,128)}, f32[2,1,1024]{2,1,0:T(1,128)S(1)}, u32[]{:S(2)}) copy-start(f32[2,1,1024]{2,1,0:T(1,128)S(1)} %broadcast_in_dim.450) | copy-start | bytes 24580
  94.8 89.6 %reduce-scatter.33.cloned.1.call-start = ((), (), s32[]{:S(2)}) async-start(), calls=%async_computation.19 | async-start | bytes 4718592 | tf_op jit(solution)/shard_map/reduce_scatter | solution.py:289
  132.9 82.2 %all-gather.14.cloned.1.call-start = ((), (), s32[]{:S(2)}) async-start(), calls=%async_computation.20 | async-start | bytes 2359296 | tf_op jit(solution)/shard_map/all_gather | solution.py:296
  187.1 87.6 %reduce-scatter.35.cloned.1.call-start = ((), (), s32[]{:S(2)}) async-start(), calls=%async_computation.21 | async-start | bytes 4718592 | tf_op jit(solution)/shard_map/reduce_scatter | solution.py:302
  223.2 201.8 %reduce-scatter.65.cloned.1.call-start = ((), (), s32[]{:S(2)}) async-start(), calls=%async_computation.36 | async-start | bytes 327680
  279.2 13.8 %collective-permute-start.2 = (f32[2,1024]{1,0:T(2,128)S(1)}, f32[2,1024]{1,0:T(2,128)S(1)}, u32[]{:S(2)}, u32[]{:S(2)}) collective-permute-start(f32[2,1024]{1,0:T(2,128)S(1)} %bitcast.522), channel_id=1, source_target_pairs={{1,0},{2,1},{3,2},{4,3},{5,4},{6,5},{7,6},{9,8},{10,9},{11,10},{12... | collective-permute-start | bytes 24584 | tf_op jit(solution)/shard_map/ppermute | solution.py:13
  280.5 12.5 %copy-start.14 = (f32[2,64,1024]{2,1,0:T(8,128)S(1)}, f32[2,64,1024]{2,1,0:T(8,128)}, u32[]{:S(2)}) copy-start(f32[2,64,1024]{2,1,0:T(8,128)} %copy-done.13) | copy-start | bytes 1572868
  351.5 35.3 %copy-start.19 = (f32[4,2,16,1024]{3,2,0,1:T(8,128)S(1)}, f32[4,2,16,1024]{3,2,0,1:T(8,128)}, u32[]{:S(2)}) copy-start(f32[4,2,16,1024]{3,2,0,1:T(8,128)} %get-tuple-element.1072) | copy-start | bytes 1572868
  395.9 3.1 collective-permute-start.3
  401.3 43.3 %reduce-scatter.61.cloned.1.call-start = ((), (), s32[]{:S(2)}) async-start(), calls=%async_computation.34 | async-start | bytes 327680
  402.2 62.3 %reduce-scatter.37.cloned.1.call-start = ((), (), s32[]{:S(2)}) async-start(), calls=%async_computation.22 | async-start | bytes 20480 | tf_op jit(solution)/shard_map/reduce_scatter | solution.py:384
  403.1 105.9 %reduce-scatter.47.cloned.1.call-start = ((), (), s32[]{:S(2)}) async-start(), calls=%async_computation.27 | async-start | bytes 2621440 | tf_op jit(solution)/shard_map/reduce_scatter | solution.py:375
  406.3 148.3 %reduce-scatter.43.cloned.1.call-start = ((), (), s32[]{:S(2)}) async-start(), calls=%async_computation.25 | async-start | bytes 2621440 | tf_op jit(solution)/shard_map/reduce_scatter | solution.py:372
  408.5 258.5 %reduce-scatter.39.cloned.1.call-start = ((), (), s32[]{:S(2)}) async-start(), calls=%async_computation.23 | async-start | bytes 7864320 | tf_op jit(solution)/shard_map/reduce_scatter | solution.py:369
  415.2 281.8 %reduce-scatter.53.cloned.1.call-start = ((), (), s32[]{:S(2)}) async-start(), calls=%async_computation.30 | async-start | bytes 1310720 | tf_op jit(solution)/shard_map/reduce_scatter | solution.py:396
  420.8 25.6 %copy-start.81 = (f32[1,2,1024]{2,0,1:T(1,128)S(1)}, f32[1,2,1024]{2,0,1:T(1,128)}, u32[]{:S(2)}) copy-start(f32[1,2,1024]{2,0,1:T(1,128)} %get-tuple-element.1669) | copy-start | bytes 24580
  420.8 304.2 %reduce-scatter.51.cloned.1.call-start = ((), (), s32[]{:S(2)}) async-start(), calls=%async_computation.29 | async-start | bytes 1310720 | tf_op jit(solution)/shard_map/reduce_scatter | solution.py:393
  425.0 23.5 %copy-start.79 = (f32[1,2,1024]{2,1,0:T(2,128)S(1)}, f32[1,2,1024]{2,1,0:T(2,128)}, u32[]{:S(2)}) copy-start(f32[1,2,1024]{2,1,0:T(2,128)} %get-tuple-element.1611) | copy-start | bytes 24580
  425.0 23.5 %copy-start.80 = (f32[1,2,1024]{2,1,0:T(2,128)S(1)}, f32[1,2,1024]{2,1,0:T(2,128)}, u32[]{:S(2)}) copy-start(f32[1,2,1024]{2,1,0:T(2,128)} %get-tuple-element.1683) | copy-start | bytes 24580
  425.0 335.3 %reduce-scatter.67.cloned.1.call-start = ((), (), s32[]{:S(2)}) async-start(), calls=%async_computation.37 | async-start | bytes 147456
  425.1 41.0 %copy-start.45 = (f32[1,3,2,1024]{3,2,1,0:T(2,128)S(1)}, f32[1,3,2,1024]{3,2,1,0:T(2,128)}, u32[]{:S(2)}) copy-start(f32[1,3,2,1024]{3,2,1,0:T(2,128)} %get-tuple-element.1679) | copy-start | bytes 73732
  425.1 41.0 %copy-start.46 = (f32[1,3,2,1024]{3,2,1,0:T(2,128)S(1)}, f32[1,3,2,1024]{3,2,1,0:T(2,128)}, u32[]{:S(2)}) copy-start(f32[1,3,2,1024]{3,2,1,0:T(2,128)} %get-tuple-element.1680) | copy-start | bytes 73732
  426.8 369.7 %reduce-scatter.63.cloned.1.call-start = ((), (), s32[]{:S(2)}) async-start(), calls=%async_computation.35 | async-start | bytes 147456
  446.3 387.7 %reduce-scatter.55.cloned.1.call-start = ((), (), s32[]{:S(2)}) async-start(), calls=%async_computation.31 | async-start | bytes 589824
  448.4 421.8 %reduce-scatter.59.cloned.1.call-start = ((), (), s32[]{:S(2)}) async-start(), calls=%async_computation.33 | async-start | bytes 147456
  466.0 441.6 %reduce-scatter.57.cloned.1.call-start = ((), (), s32[]{:S(2)}) async-start(), calls=%async_computation.32 | async-start | bytes 589824
  468.6 478.6 %reduce-scatter.49.cloned.1.call-start = ((), (), s32[]{:S(2)}) async-start(), calls=%async_computation.28 | async-start | bytes 1179648 | tf_op jit(solution)/shard_map/reduce_scatter | solution.py:403
  511.2 475.9 %reduce-scatter.45.cloned.1.call-start = ((), (), s32[]{:S(2)}) async-start(), calls=%async_computation.26 | async-start | bytes 1179648 | tf_op jit(solution)/shard_map/reduce_scatter | solution.py:402
  556.7 480.4 %reduce-scatter.41.cloned.1.call-start = ((), (), s32[]{:S(2)}) async-start(), calls=%async_computation.24 | async-start | bytes 3538944 | tf_op jit(solution)/shard_map/reduce_scatter | solution.py:401
  670.3 56.5 %copy-start.88 = (f32[1024]{0:T(1024)S(1)}, f32[1024]{0:T(1024)}, u32[]{:S(2)}) copy-start(f32[1024]{0:T(1024)} %param.27) | copy-start | bytes 12292
  670.3 79.0 %copy-start.93 = (f32[2,64]{1,0:T(2,128)S(1)}, f32[2,64]{1,0:T(2,128)}, u32[]{:S(2)}) copy-start(f32[2,64]{1,0:T(2,128)} %get-tuple-element.1444) | copy-start | bytes 1540
  670.3 79.1 %copy-start.92 = (f32[2,64]{1,0:T(2,128)S(1)}, f32[2,64]{1,0:T(2,128)}, u32[]{:S(2)}) copy-start(f32[2,64]{1,0:T(2,128)} %get-tuple-element.1445) | copy-start | bytes 1540
  670.3 79.0 %copy-start.84 = (f32[2,64]{1,0:T(2,128)S(1)}, f32[2,64]{1,0:T(2,128)}, u32[]{:S(2)}) copy-start(f32[2,64]{1,0:T(2,128)} %copy-done.82) | copy-start | bytes 1540
  672.7 364.4 %copy-start.1 = (bf16[1024,1024]{1,0:T(8,128)(2,1)S(1)}, bf16[1024,1024]{1,0:T(8,128)(2,1)}, u32[]{:S(2)}) copy-start(bf16[1024,1024]{1,0:T(8,128)(2,1)} %param.34) | copy-start | bytes 6291460
  (56 other events, 170.4 us)
Sparse Core Ops, SparseCore 0:
  95.0 30.0 all-gather.11
  133.1 51.3 reduce-scatter.32
  187.2 27.8 all-gather.13
  223.3 51.3 reduce-scatter.34
  401.4 22.4 reduce-scatter.64
  426.7 17.8 reduce-scatter.60
  447.4 17.1 reduce-scatter.36
  467.0 41.9 reduce-scatter.46
  511.3 43.1 reduce-scatter.42
  556.8 110.0 reduce-scatter.38
  669.3 27.6 reduce-scatter.52
  699.2 25.7 reduce-scatter.50
  728.3 32.0 reduce-scatter.66
  763.2 33.3 reduce-scatter.62
  799.8 34.1 reduce-scatter.54
  836.8 33.3 reduce-scatter.58
  873.4 34.1 reduce-scatter.56
  911.2 35.9 reduce-scatter.48
  951.0 35.9 reduce-scatter.44
  990.8 46.2 reduce-scatter.40
where the time goes:
time: 1050 us; the launch traced here: 1040 us
  waiting for transfers between devices  719 us (68%)
  other arithmetic  124 us (12%)
  blocking collectives  77.5 us (7%)
  matrix products  53.4 us (5%)
  local copies, waits for them, and re-layouts  41.9 us (4%)
  between operations  18.1 us (2%)
    unnamed x27, waiting for transfers between devices  170 us
    reduce_scatter x1, waiting for transfers between devices, on_device(): lax.psum_scatter(grad_att_w.astype(jnp.bfloat16), 'seg', scatter_dimensio...  110 us
    reduce_scatter x1, waiting for transfers between devices, on_device(): lax.psum_scatter(partial_out, 'tok', scatter_dimension=1, tiled=True)  51.4 us
    reduce_scatter x1, waiting for transfers between devices, on_device(): lax.psum_scatter(seg_sums[0], 'tok', scatter_dimension=1, tiled=True)  50.1 us
    reduce_scatter x1, waiting for transfers between devices, on_device(): lax.psum_scatter(grad_mix_key_all, 'tok', scatter_dimension=1, tiled=True)  50.1 us
    reduce_scatter x1, waiting for transfers between devices, on_device(): lax.psum_scatter(grad_out_w.astype(jnp.bfloat16), 'seg', scatter_dimensio...  43.3 us
    reduce_scatter x1, waiting for transfers between devices, on_device(): lax.psum_scatter(grad_recept_w.astype(jnp.bfloat16), 'seg', scatter_dimen...  40.4 us
    reduce_scatter x1, waiting for transfers between devices, on_device(): lax.psum_scatter(seg_sums[1], 'tok', scatter_dimension=0, tiled=True)  39.8 us
  transfers between devices with their start and end apart: 24, of which 21 were waited for; matrix products, arithmetic and copies ran while one was open for 5% of the time, Pallas kernels for 0%

commit v1 on v0

--- a/solution.py
+++ b/solution.py
@@ -1,6 +1,10 @@
+import types
+
 import jax
 import jax.numpy as jnp
 from jax import lax
+from jax.experimental import pallas as pl
+from jax.experimental.pallas import tpu as pltpu
 from jax.sharding import PartitionSpec as P
 
 norm_eps = 1e-05
@@ -429,9 +433,1036 @@
     )
 
 
+BF16 = jnp.bfloat16
+F32 = jnp.float32
+LOW = floor_exp
+MESH = pl.DeviceIdType.MESH
+ROWS = 128
+SPAN = 64
+TILE = 256
+HALF = 512
+
+
+def dot_nn(a, b):
+    return lax.dot_general(a, b, (((1,), (0,)), ((), ())), preferred_element_type=F32)
+
+
+def dot_nt(a, b):
+    return lax.dot_general(a, b, (((1,), (1,)), ((), ())), preferred_element_type=F32)
+
+
+def dot_tn(a, b):
+    return lax.dot_general(a, b, (((0,), (0,)), ((), ())), preferred_element_type=F32)
+
+
+def each(count, step):
+    def turn(i, carry):
+        step(i)
+        return carry
+
+    lax.fori_loop(0, count, turn, 0)
+
+
+def tile_of(i, size):
+    if isinstance(i, int):
+        return pl.ds(i * size, size)
+    return pl.ds(pl.multiple_of(i * size, size), size)
+
+
+def normalise(rows):
+    centred = rows - jnp.mean(rows, axis=-1, keepdims=True)
+    scale = lax.rsqrt(jnp.mean(centred * centred, axis=-1, keepdims=True) + norm_eps)
+    return centred * scale, scale
+
+
+def unnormalise(grad, normed, scale, gain):
+    dn = grad * gain
+    return scale * (
+        dn
+        - jnp.mean(dn, axis=-1, keepdims=True)
+        - normed * jnp.mean(dn * normed, axis=-1, keepdims=True)
+    )
+
+
+def swap_matrix():
+    row = lax.broadcasted_iota(jnp.int32, (ROWS, ROWS), 0)
+    col = lax.broadcasted_iota(jnp.int32, (ROWS, ROWS), 1)
+    source = (row & 64) | ((row & 7) << 3) | ((row >> 3) & 7)
+    return jnp.where(col == source, 1.0, 0.0).astype(BF16)
+
+
+def swap_exact(matrix, rows):
+    high = rows.astype(BF16)
+    rest = rows - high.astype(F32)
+    mid = rest.astype(BF16)
+    low = (rest - mid.astype(F32)).astype(BF16)
+    return dot_nn(matrix, high) + (dot_nn(matrix, mid) + dot_nn(matrix, low))
+
+
+def join(a, b, p, a2, b2, p2):
+    peak = jnp.maximum(p, p2)
+    e1 = jnp.exp(p - peak)
+    e2 = jnp.exp(p2 - peak)
+    return e1 * a + e2 * a2, e1 * b + e2 * b2, peak
+
+
+SCRATCH = dict(
+    watt=((3, 1024, 1024), BF16),
+    wout=((1024, 1024), BF16),
+    wrec=((1024, 1024), BF16),
+    wkey=((1024, 1024), BF16),
+    wval=((1024, 1024), BF16),
+    xp=((ROWS, 1024), BF16),
+    cg=((4, ROWS, 1024), BF16),
+    n1=((ROWS, 1024), F32),
+    r1=((ROWS, 128), F32),
+    fn=((2, 72, 1024), F32),
+    hs1=((2, 1, 1024), F32),
+    hr1=((2, 1, 1024), F32),
+    xs=((5, 2 * ROWS, 1024), BF16),
+    gs=((5, 2 * ROWS, 1024), BF16),
+    kb=((ROWS, 1024), F32),
+    vb=((ROWS, 1024), F32),
+    sr=((ROWS, 1024), F32),
+    ou=((ROWS, 1024), F32),
+    rd=((ROWS, 1024), F32),
+    qq=((ROWS, 1024), F32),
+    sa=((ROWS, 1024), F32),
+    sb=((ROWS, 1024), F32),
+    sp=((ROWS, 1024), F32),
+    ea=((2, 8, 1024), F32),
+    eb=((2, 8, 1024), F32),
+    ep=((2, 8, 1024), F32),
+    ws=((3, 2, 1024), F32),
+    wr=((8, 3, 2, 1024), F32),
+    bs=((3, 2, 1024), F32),
+    br=((8, 3, 2, 1024), F32),
+    dev=((3, 2, 1024), F32),
+    mid=((ROWS, 1024), F32),
+    n2=((ROWS, 1024), F32),
+    r2=((ROWS, 128), F32),
+    sng=((4, ROWS, 1024), BF16),
+    hs2=((2, 1, 1024), F32),
+    hr2=((4, 2, 1, 1024), F32),
+    sf=((2, 72, 1024), F32),
+    mk=((4 * ROWS, 1024), BF16),
+    mg=((ROWS, 1024), BF16),
+    gv=((4 * ROWS, 1024), BF16),
+    hid=((4 * ROWS, 1024), BF16),
+    ghp=((4 * ROWS, 1024), BF16),
+    rl=((ROWS, 1024), F32),
+    cc=((ROWS, 1024), F32),
+    gg=((ROWS, 1024), BF16),
+    ab=((ROWS, 1024), F32),
+    bb=((2, 72, 1024), F32),
+    pvs=((4, ROWS, 1024), BF16),
+    pvr=((3, ROWS, 1024), BF16),
+    gss=((4, ROWS, 1024), BF16),
+    gsr=((3, ROWS, 1024), BF16),
+    bts=((4, 2, 1, 1024), F32),
+    btr=((4, 2, 1, 1024), F32),
+    bsum=((2, 1, 1024), F32),
+    fks=((1024, 512), BF16),
+    fkr=((1024, 512), BF16),
+    fkz=((1024, 512), BF16),
+    fkt=((3, 256, 512), BF16),
+    fvs=((4, 512, 256), BF16),
+    fvr=((4, 512, 256), BF16),
+    fvz=((4, 512, 256), BF16),
+    fvt=((3, 512, 256), BF16),
+    arecv=((5, 3, ROWS, 1024), BF16),
+    zsend=((5, 4, ROWS, 256), BF16),
+    zrecv=((5, 3, ROWS, 256), BF16),
+    hs3=((2, 1, 1024), F32),
+    hr3=((2, 1, 1024), F32),
+    acc=((6, 8, 1024), F32),
+    vec=((16, 1024), F32),
+    vz=((4, 16, 256), F32),
+    pvb=((4, 8, 256), F32),
+    vss=((8, 24, 256), F32),
+    vt=((8, 24, 256), F32),
+)
+SEMS = 128
+INPUTS = (
+    "x",
+    "cot",
+    "prev",
+    "init",
+    "decay",
+    "first",
+    "ratio",
+    "gain",
+    "bias",
+    "h_att",
+    "h_out",
+    "h_rec",
+    "h_key",
+    "h_val",
+)
+OUTPUTS = (
+    "o_out",
+    "o_in",
+    "o_prev",
+    "o_init",
+    "o_vec",
+    "o_att",
+    "o_wout",
+    "o_wrec",
+    "o_key",
+    "o_val",
+)
+
+
+def fused(*refs):
+    names = INPUTS + OUTPUTS + tuple(SCRATCH) + ("ss", "rs", "ls")
+    r = types.SimpleNamespace(**dict(zip(names, refs)))
+    s = lax.axis_index("seg")
+    t = lax.axis_index("tok")
+    chip = t // 2
+    taken = [0]
+
+    def slots(n):
+        taken[0] += n
+        return taken[0] - n
+
+    def wire(src, dst, slot, seg, tok, arrive=None):
+        return pltpu.make_async_remote_copy(
+            src_ref=src,
+            dst_ref=dst,
+            send_sem=r.ss.at[slot],
+            recv_sem=r.rs.at[slot if arrive is None else arrive],
+            device_id=(seg, tok),
+            device_id_type=MESH,
+        )
+
+    sent = []
+
+    def send(*args, **kw):
+        copy = wire(*args, **kw)
+        copy.start()
+        sent.append(copy)
+        return copy
+
+    loads = []
+    for i, (src, dst) in enumerate(
+        [
+            (r.h_att, r.watt),
+            (r.h_out, r.wout),
+            (r.h_rec, r.wrec),
+            (r.h_key, r.wkey.at[:, pl.ds(0, HALF)]),
+            (r.h_val, r.wval.at[pl.ds(0, HALF), :]),
+        ]
+    ):
+        copy = pltpu.make_async_copy(src, dst, r.ls.at[i])
+        copy.start()
+        loads.append(copy)
+
+    barrier = pltpu.get_barrier_semaphore()
+    for x in range(1, 8):
+        pl.semaphore_signal(barrier, inc=1, device_id=(s, t ^ x), device_id_type=MESH)
+    for x in range(1, 4):
+        pl.semaphore_signal(barrier, inc=1, device_id=(s ^ x, t), device_id_type=MESH)
+
+    swap = swap_matrix()
+    r.xp[...] = dot_nn(swap, r.x[...]).astype(BF16)
+    r.cg[0] = dot_nn(swap, r.cot[...]).astype(BF16)
+
+    def first_norm(i):
+        i = 3 - i
+        for q in range(2):
+            rows = pl.ds(pl.multiple_of(q * SPAN + i * 16, 16), 16)
+            normed, scale = normalise(r.xp[rows, :].astype(F32))
+            r.n1[rows, :] = normed
+            r.r1[rows, :] = jnp.broadcast_to(scale, (16, 128))
+            r.fn[q, pl.ds(pl.multiple_of(8 + i * 16, 8), 16), :] = (
+                normed * r.gain[0:1, :] + r.bias[0:1, :]
+            )
+
+    each(4, first_norm)
+    for q in range(2):
+        r.hs1[q] = r.fn[q, 71:72, :]
+    pl.semaphore_wait(barrier, 10)
+    after = (t + 1) % 8
+    prior = (t + 7) % 8
+    halo1 = send(r.hs1, r.hr1, slots(1), s, after)
+    near = t ^ 1
+    key_in = send(r.h_key, r.wkey.at[:, pl.ds(HALF, HALF)], slots(1), s, near)
+    val_in = send(r.h_val, r.wval.at[pl.ds(HALF, HALF), :], slots(1), s, near)
+    cot_slot = slots(4)
+    for j in range(1, 4):
+        send(r.cg.at[0], r.cg.at[j], cot_slot + j, s, t ^ (2 * j))
+
+    row8 = lax.broadcasted_iota(jnp.int32, (8, 1024), 0)
+    halo1.wait_recv()
+    for q in range(2):
+        head = jnp.where(t == 0, r.prev[0, q : q + 1, :], r.hr1[q])
+        r.fn[q, 0:8, :] = jnp.where(row8 == 0, head, pltpu.roll(r.fn[q, 64:72, :], 1, 0))
+
+    def mix_one(i):
+        for q in range(2):
+            now = r.fn[q, pl.ds(pl.multiple_of(8 + i * 16, 8), 16), :]
+            back = r.fn[q, tile_of(i, 16), :]
+            rows = pl.ds(pl.multiple_of(q * SPAN + i * 16, 16), 16)
+            for m in range(3):
+                ratio = r.ratio[m : m + 1, :]
+                r.xs[m, rows, :] = (now * ratio + back * (1.0 - ratio)).astype(BF16)
+
+    each(4, mix_one)
+    for copy in loads[:1]:
+        copy.wait()
+
+    def product(get, weights, put, transposed=False, tile=TILE):
+        def step(n):
+            span = tile_of(n, tile)
+            if transposed:
+                put(span, dot_nt(get(), weights[span, :]))
+            else:
+                put(span, dot_nn(get(), weights[:, span]))
+
+        each(1024 // tile, step)
+
+    own = pl.ds(0, ROWS)
+
+    def keep(ref):
+        def put(span, part):
+            ref[:, span] = part
+
+        return put
+
+    def keep_gate(span, part):
+        r.sr[:, span] = jax.nn.sigmoid(part)
+
+    product(lambda: r.xs[0, own, :], r.watt.at[0], keep(r.kb))
+    product(lambda: r.xs[1, own, :], r.watt.at[1], keep(r.vb))
+
+    fade = -jnp.exp(r.decay[...])
+    r.vec[15:16, :] = fade
+    row_h = lax.broadcasted_iota(jnp.int32, (8, HALF), 0)
+    row_f = row_h.astype(F32)
+
+    def local_scan(n):
+        cols = tile_of(n, HALF)
+        w = r.vec[15:16, cols]
+        for q in range(2):
+            a = jnp.zeros((8, HALF), F32)
+            b = jnp.zeros((8, HALF), F32)
+            p = jnp.full((8, HALF), LOW, F32)
+            for i in range(8):
+                rows = pl.ds(q * SPAN + i * 8, 8)
+                kk = r.kb[rows, cols]
+                a, b, p = join(a, b, p + w, r.vb[rows, cols], 1.0, kk)
+            for d in (1, 2, 4):
+                pe = jnp.where(row_h >= d, pltpu.roll(p, d, 0) + (8.0 * d) * w, LOW)
+                a, b, p = join(a, b, p, pltpu.roll(a, d, 0), pltpu.roll(b, d, 0), pe)
+            for m, part in enumerate((a, b, p)):
+                r.ws[m, q : q + 1, cols] = part[7:8, :]
+            r.ea[q, :, cols] = jnp.where(row_h == 0, 0.0, pltpu.roll(a, 1, 0))
+            r.eb[q, :, cols] = jnp.where(row_h == 0, 0.0, pltpu.roll(b, 1, 0))
+            r.ep[q, :, cols] = jnp.where(row_h == 0, LOW, pltpu.roll(p, 1, 0))
+
+    each(2, local_scan)
+    r.wr[0] = r.ws[...]
+    state_slot = slots(8)
+    state_in = [
+        send(r.ws, r.wr.at[x], state_slot + x, s, t ^ x) for x in range(1, 8)
+    ]
+    product(lambda: r.xs[2, own, :], r.watt.at[2], keep_gate)
+    for copy in loads[1:]:
+        copy.wait()
+    near_x = [slots(1) for _ in range(5)]
+    near_g = [slots(1) for _ in range(5)]
+    far = pl.ds(ROWS, ROWS)
+
+    def share(ref, m, slot):
+        return send(ref.at[m, own, :], ref.at[m, far, :], slot, s, near)
+
+    x_in = [share(r.xs, m, near_x[m]) for m in range(3)]
+    for copy in state_in:
+        copy.wait_recv()
+
+    def far_state(ref, base_p, sel, steps):
+        peak = base_p
+        for j in range(8):
+            e = jnp.where(sel(j), ref[j ^ t, 2] + fade * steps(j), LOW)
+            peak = jnp.maximum(peak, e)
+        return peak
+
+    def far_sum(ref, peak, sel, steps, a, b):
+        for j in range(8):
+            e = jnp.exp(jnp.where(sel(j), ref[j ^ t, 2] + fade * steps(j), LOW) - peak)
+            a = a + ref[j ^ t, 0] * e
+            b = b + ref[j ^ t, 1] * e
+        return a, b
+
+    tf = t.astype(F32)
+    entry = r.init[2] + fade * (64.0 * tf)
+    before = lambda j: j < t
+    gap = lambda j: 64.0 * (tf - (1.0 + j))
+    peak = far_state(r.wr, entry, before, gap)
+    lead = jnp.exp(entry - peak)
+    a, b = far_sum(r.wr, peak, before, gap, r.init[0] * lead, r.init[1] * lead)
+    r.dev[0] = a
+    r.dev[1] = b
+    r.dev[2] = peak
+
+    def full_scan(n):
+        cols = tile_of(n, HALF)
+        w = r.vec[15:16, cols]
+        u = r.first[:, cols]
+        for q in range(2):
+            a, b, p = join(
+                r.ea[q, :, cols],
+                r.eb[q, :, cols],
+                r.ep[q, :, cols],
+                r.dev[0, q : q + 1, cols],
+                r.dev[1, q : q + 1, cols],
+                r.dev[2, q : q + 1, cols] + (8.0 * row_f) * w,
+            )
+            for i in range(8):
+                rows = pl.ds(q * SPAN + i * 8, 8)
+                kk = r.kb[rows, cols]
+                vv = r.vb[rows, cols]
+                r.sa[rows, cols] = a
+                r.sb[rows, cols] = b
+                r.sp[rows, cols] = p
+                num, den, top = join(a, b, p, vv, 1.0, u + kk)
+                inv = 1.0 / den
+                r.ou[rows, cols] = num * inv
+                r.rd[rows, cols] = inv
+                r.qq[rows, cols] = top
+                a, b, p = join(a, b, p + w, vv, 1.0, kk)
+
+    each(2, full_scan)
+
+    def weigh(i):
+        rows = tile_of(i, 16)
+        r.xs[3, rows, :] = (r.sr[rows, :] * r.ou[rows, :]).astype(BF16)
+
+    each(8, weigh)
+    x_in.append(share(r.xs, 3, near_x[3]))
+
+    def keep_middle(span, part):
+        r.mid[:, span] = r.xp[:, span].astype(F32) + part
+
+    product(lambda: r.xs[3, own, :], r.wout, keep_middle)
+
+    def second_norm(i):
+        rows = tile_of(i, 16)
+        normed, scale = normalise(r.mid[rows, :])
+        r.n2[rows, :] = normed
+        r.r2[rows, :] = jnp.broadcast_to(scale, (16, 128))
+        r.sng[0, rows, :] = (normed * r.gain[1:2, :] + r.bias[1:2, :]).astype(BF16)
+
+    each(8, second_norm)
+    for q in range(2):
+        last = r.n2[q * SPAN + 56 : q * SPAN + 64, :]
+        r.hs2[q] = (last * r.gain[1:2, :] + r.bias[1:2, :])[7:8, :]
+    halo_slot = slots(4)
+    halo2 = [
+        send(r.hs2, r.hr2.at[i], halo_slot + i, s, t ^ (2 * i + 1)) for i in range(4)
+    ]
+    sn_slot = slots(4)
+    for j in range(1, 4):
+        send(r.sng.at[0], r.sng.at[j], sn_slot + j, s, t ^ (2 * j))
+    key_in.wait_recv()
+    val_in.wait_recv()
+    for copy in halo2:
+        copy.wait_recv()
+    r.acc[...] = jnp.zeros_like(r.acc)
+    r.vec[5:7, :] = jnp.zeros((2, 1024), F32)
+
+    pv_slot = slots(4)
+    gs_slot = slots(4)
+    bt_slot = slots(4)
+    bt_home = slots(4)
+
+    def block(j):
+        b = t ^ (2 * j)
+        rows = tile_of(j, ROWS)
+
+        @pl.when(j > 0)
+        def _():
+            wire(r.sng.at[0], r.sng.at[j], sn_slot + j, s, b).wait_recv()
+            wire(r.cg.at[0], r.cg.at[j], cot_slot + j, s, b).wait_recv()
+
+        source = (((b + 7) % 8) ^ t) // 2
+        for q in range(2):
+            for i in range(4):
+                r.sf[q, pl.ds(8 + 16 * i, 16), :] = r.sng[
+                    j, pl.ds(q * SPAN + 16 * i, 16), :
+                ].astype(F32)
+            head = jnp.where(b == 0, r.prev[1, q : q + 1, :], r.hr2[source, q])
+            r.sf[q, 0:8, :] = jnp.where(
+                row8 == 0, head, pltpu.roll(r.sf[q, 64:72, :], 1, 0)
+            )
+
+        def mix_two(i):
+            for q in range(2):
+                now = r.sf[q, pl.ds(pl.multiple_of(8 + i * 16, 8), 16), :]
+                back = r.sf[q, tile_of(i, 16), :]
+                at = pl.multiple_of(q * SPAN + i * 16, 16)
+                r3 = r.ratio[3:4, :]
+                r4 = r.ratio[4:5, :]
+                r.mk[pl.ds(pl.multiple_of(j * ROWS + at, 16), 16), :] = (
+                    now * r3 + back * (1.0 - r3)
+                ).astype(BF16)
+                r.mg[pl.ds(at, 16), :] = (now * r4 + back * (1.0 - r4)).astype(BF16)
+
+        each(4, mix_two)
+
+        @pl.when(j == 0)
+        def _():
+            r.xs[4, own, :] = r.mg[...]
+
+        def put_gate(span, part):
+            sg = jax.nn.sigmoid(part)
+            top = r.cg[j, :, span].astype(F32) * sg
+            r.gv[rows, span] = top.astype(BF16)
+            r.cc[:, span] = top * (1.0 - sg)
+
+        product(lambda: r.mg[...], r.wrec, put_gate)
+
+        def put_hidden(span, part):
+            relu = jnp.maximum(part, 0.0)
+            r.rl[:, span] = relu
+            r.hid[rows, span] = (relu * relu).astype(BF16)
+
+        product(lambda: r.mk[rows, :], r.wkey, put_hidden)
+
+        def put_hidden_grad(span, part):
+            r.ghp[rows, span] = (part * 2.0 * r.rl[:, span]).astype(BF16)
+
+        product(lambda: r.gv[rows, :], r.wval, put_hidden_grad, transposed=True)
+
+        def put_value(span, part):
+            r.pvs[j, :, span] = part.astype(BF16)
+            r.gg[:, span] = (part * r.cc[:, span]).astype(BF16)
+
+        product(lambda: r.hid[rows, :], r.wval, put_value)
+
+        def mixed_back(m, first):
+            def put(span, part):
+                ratio = r.ratio[m : m + 1, span]
+                total = jnp.zeros((1, TILE), F32)
+                for q in range(2):
+                    here = part[q * SPAN : (q + 1) * SPAN, :]
+                    step = r.sf[q, 8:72, span] - r.sf[q, 0:64, span]
+                    total = total + jnp.sum(step * here, axis=0, keepdims=True)
+                    half = pl.ds(q * SPAN, SPAN)
+                    if first:
+                        r.ab[half, span] = here * ratio
+                        r.bb[q, 0:64, span] = here * (1.0 - ratio)
+                    else:
+                        r.ab[half, span] = r.ab[half, span] + here * ratio
+                        r.bb[q, 0:64, span] = r.bb[q, 0:64, span] + here * (1.0 - ratio)
+                r.vec[m + 2 : m + 3, span] = r.vec[m + 2 : m + 3, span] + total
+
+            return put
+
+        product(lambda: r.ghp[rows, :], r.wkey, mixed_back(3, True), transposed=True)
+        product(lambda: r.gg[...], r.wrec, mixed_back(4, False), transposed=True)
+        for q in range(2):
+            r.bts[j, q] = r.bb[q, 0:1, :]
+            r.bb[q, 64:72, :] = jnp.where(row8 == 7, 0.0, pltpu.roll(r.bb[q, 0:8, :], 7, 0))
+            for i in range(4):
+                at = pl.ds(q * SPAN + 16 * i, 16)
+                r.gss[j, at, :] = (r.ab[at, :] + r.bb[q, pl.ds(8 + 16 * i, 16), :]).astype(
+                    BF16
+                )
+        wire(r.bts.at[j], r.btr.at[chip], bt_slot + j, s, (b + 7) % 8, bt_home + chip).start()
+
+        @pl.when(j > 0)
+        def _():
+            wire(r.gss.at[j], r.gsr.at[j - 1], gs_slot + j, s, b).start()
+            wire(r.pvs.at[j], r.pvr.at[j - 1], pv_slot + j, s, b).start()
+
+    each(4, block)
+    x_in.append(share(r.xs, 4, near_x[4]))
+
+    def key_grad(half, ref):
+        def step(n):
+            rows = tile_of(n, 256)
+            ref[rows, :] = dot_tn(
+                r.mk[:, rows], r.ghp[:, pl.ds(half * HALF, HALF)]
+            ).astype(BF16)
+
+        each(4, step)
+
+    def value_grad(half, ref):
+        def step(n):
+            ref[n] = dot_tn(
+                r.hid[:, pl.ds(half * HALF, HALF)], r.gv[:, tile_of(n, 256)]
+            ).astype(BF16)
+
+        each(4, step)
+
+    key_grad(1, r.fks)
+    fk_in = send(r.fks, r.fkr, slots(1), s, near)
+    value_grad(1, r.fvs)
+    fv_in = send(r.fvs, r.fvr, slots(1), s, near)
+    key_grad(0, r.fkz)
+    value_grad(0, r.fvz)
+    fk_in.wait_recv()
+
+    def add_key(i):
+        rows = tile_of(i, 64)
+        r.fkz[rows, :] = (r.fkz[rows, :].astype(F32) + r.fkr[rows, :].astype(F32)).astype(BF16)
+
+    each(16, add_key)
+    fk_slot = slots(4)
+    fkz_in = [
+        send(r.fkz.at[tile_of(s ^ z, 256), :], r.fkt.at[z - 1], fk_slot + z, s ^ z, t)
+        for z in range(1, 4)
+    ]
+    fv_in.wait_recv()
+
+    def add_value(n):
+        for i in range(4):
+            rows = pl.ds(i * 128, 128)
+            r.fvz[n, rows, :] = (
+                r.fvz[n, rows, :].astype(F32) + r.fvr[n, rows, :].astype(F32)
+            ).astype(BF16)
+
+    each(4, add_value)
+    fv_slot = slots(4)
+    fvz_in = [
+        send(r.fvz.at[s ^ z], r.fvt.at[z - 1], fv_slot + z, s ^ z, t) for z in range(1, 4)
+    ]
+
+    for i in range(4):
+        wire(r.bts.at[0], r.btr.at[i], bt_slot, s, near, bt_home + i).wait_recv()
+    for j in range(1, 4):
+        wire(r.gss.at[j], r.gsr.at[j - 1], gs_slot + j, s, t ^ (2 * j)).wait_recv()
+    for q in range(2):
+        r.bsum[q] = r.btr[0, q] + r.btr[1, q] + (r.btr[2, q] + r.btr[3, q])
+    row16 = lax.broadcasted_iota(jnp.int32, (16, 1024), 0)
+
+    def fold(x):
+        return x[0:8, :] + x[8:16, :]
+
+    def back_two(i):
+        for q in range(2):
+            rows = pl.ds(pl.multiple_of(q * SPAN + i * 16, 16), 16)
+            grad = r.gss[0, rows, :].astype(F32)
+            for j in range(1, 4):
+                grad = grad + r.gsr[j - 1, rows, :].astype(F32)
+            is_last = (row16 + 16 * i == 63) & (t < 7)
+            grad = grad + jnp.where(is_last, r.bsum[q], 0.0)
+            normed = r.n2[rows, :]
+            r.acc[0] = r.acc[0] + fold(grad * normed)
+            r.acc[1] = r.acc[1] + fold(grad)
+            dz = unnormalise(grad, normed, r.r2[rows, 0:1], r.gain[1:2, :])
+            total = r.cg[0, rows, :].astype(F32) + dz
+            r.rl[rows, :] = total
+            r.gs[3, rows, :] = total.astype(BF16)
+
+    each(4, back_two)
+    g_in = {3: share(r.gs, 3, near_g[3])}
+
+    def put_branch(span, part):
+        sr = r.sr[:, span]
+        out = r.ou[:, span]
+        grad = part * sr
+        r.gs[2, own, span] = (grad * out * (1.0 - sr)).astype(BF16)
+        r.rd[:, span] = grad * r.rd[:, span]
+
+    product(lambda: r.gs[3, own, :], r.wout, put_branch, transposed=True)
+    g_in[2] = share(r.gs, 2, near_g[2])
+
+    def back_local(n):
+        cols = tile_of(n, HALF)
+        w = r.vec[15:16, cols]
+        for q in range(2):
+            a = jnp.zeros((8, HALF), F32)
+            b = jnp.zeros((8, HALF), F32)
+            p = jnp.full((8, HALF), LOW, F32)
+            for i in range(7, -1, -1):
+                rows = pl.ds(q * SPAN + i * 8, 8)
+                al = r.rd[rows, cols]
+                a, b, p = join(a, b, p + w, al, -al * r.ou[rows, cols], -r.qq[rows, cols])
+            for d in (1, 2, 4):
+                pe = jnp.where(row_h < 8 - d, pltpu.roll(p, 8 - d, 0) + (8.0 * d) * w, LOW)
+                a, b, p = join(a, b, p, pltpu.roll(a, 8 - d, 0), pltpu.roll(b, 8 - d, 0), pe)
+            for m, part in enumerate((a, b, p)):
+                r.bs[m, q : q + 1, cols] = part[0:1, :]
+            r.ea[q, :, cols] = jnp.where(row_h == 7, 0.0, pltpu.roll(a, 7, 0))
+            r.eb[q, :, cols] = jnp.where(row_h == 7, 0.0, pltpu.roll(b, 7, 0))
+            r.ep[q, :, cols] = jnp.where(row_h == 7, LOW, pltpu.roll(p, 7, 0))
+
+    each(2, back_local)
+    r.br[0] = r.bs[...]
+    back_slot = slots(8)
+    back_in = [send(r.bs, r.br.at[x], back_slot + x, s, t ^ x) for x in range(1, 8)]
+
+    for j in range(1, 4):
+        wire(r.pvs.at[j], r.pvr.at[j - 1], pv_slot + j, s, t ^ (2 * j)).wait_recv()
+
+    product_gate = lambda span, part: put_out(span, jax.nn.sigmoid(part))
+
+    def put_out(span, sg):
+        value = r.pvs[0, :, span].astype(F32)
+        for j in range(1, 4):
+            value = value + r.pvr[j - 1, :, span].astype(F32)
+        out = r.mid[:, span] + sg * value
+        top = r.cg[0, :, span].astype(F32)
+        r.gs[4, own, span] = (top * value * sg * (1.0 - sg)).astype(BF16)
+        r.o_out[:, span] = dot_nn(swap, out.astype(BF16)).astype(BF16)
+
+    product(lambda: r.xs[4, own, :], r.wrec, product_gate)
+    g_in[4] = share(r.gs, 4, near_g[4])
+
+    a_home = (r.wval, r.mk, r.wval, r.wkey, r.wkey)
+    a_base = (4, 0, 0, 0, 4)
+
+    def a_rows(m, j):
+        return tile_of(a_base[m] + j, ROWS)
+
+    def a_part(m, j):
+        return a_home[m].at[a_rows(m, j), :]
+
+    a_slot = [slots(4) for _ in range(5)]
+    z_slot = [slots(4) for _ in range(5)]
+
+    def weight_grad(m):
+        x_in[m].wait_recv()
+        g_in[m].wait_recv()
+
+        def step(j):
+            cols = tile_of(t ^ (2 * j), 128)
+            a_home[m][a_rows(m, j), :] = dot_tn(r.xs[m, :, cols], r.gs[m]).astype(BF16)
+
+            @pl.when(j > 0)
+            def _():
+                wire(
+                    a_part(m, j), r.arecv.at[m, j - 1], a_slot[m] + j, s, t ^ (2 * j)
+                ).start()
+
+        each(4, step)
+
+    weight_grad(3)
+    for copy in back_in:
+        copy.wait_recv()
+
+    later = lambda j: j > t
+    gap_back = lambda j: 64.0 * (j - 1.0 - tf)
+    nothing = jnp.full((2, 1024), LOW, F32)
+    peak = far_state(r.br, nothing, later, gap_back)
+    a, b = far_sum(r.br, peak, later, gap_back, 0.0 * fade, 0.0 * fade)
+    r.dev[0] = a
+    r.dev[1] = b
+    r.dev[2] = peak
+    always = lambda j: j >= 0
+    from_start = lambda j: 64.0 * j
+    peak = far_state(r.br, nothing, always, from_start)
+    a, b = far_sum(r.br, peak, always, from_start, 0.0 * fade, 0.0 * fade)
+    lift = jnp.exp(peak + r.init[2])
+    a = a * lift
+    b = b * lift
+    r.bs3[0] = a
+    r.bs3[1] = b
+    r.bs3[2] = a * r.init[0] + b * r.init[1]
+    r.o_init[...] = r.bs3[:, :, tile_of(t, 128)]
+
+    def back_full(n):
+        cols = tile_of(n, HALF)
+        w = r.vec[15:16, cols]
+        u = r.first[:, cols]
+        gu = jnp.zeros((8, HALF), F32)
+        gw = jnp.zeros((8, HALF), F32)
+        for q in range(2):
+            a, b, p = join(
+                r.ea[q, :, cols],
+                r.eb[q, :, cols],
+                r.ep[q, :, cols],
+                r.dev[0, q : q + 1, cols],
+                r.dev[1, q : q + 1, cols],
+                r.dev[2, q : q + 1, cols] + (8.0 * (7.0 - row_f)) * w,
+            )
+            for i in range(7, -1, -1):
+                rows = pl.ds(q * SPAN + i * 8, 8)
+                kk = r.kb[rows, cols]
+                vv = r.vb[rows, cols]
+                al = r.rd[rows, cols]
+                out = r.ou[rows, cols]
+                top = r.qq[rows, cols]
+                now = jnp.exp(u + kk - top) * al
+                ahead = jnp.exp(kk + p)
+                bonus = now * (vv - out)
+                gu = gu + bonus
+                gw = gw + jnp.exp(p + w + r.sp[rows, cols]) * (
+                    a * r.sa[rows, cols] + b * r.sb[rows, cols]
+                )
+                r.vb[rows, cols] = now + ahead * a
+                r.kb[rows, cols] = bonus + ahead * (a * vv + b)
+                a, b, p = join(a, b, p + w, al, -al * out, -top)
+        r.vec[0:1, cols] = jnp.sum(gw, axis=0, keepdims=True) * w
+        r.vec[1:2, cols] = jnp.sum(gu, axis=0, keepdims=True)
+
+    each(2, back_full)
+
+    def round_grads(i):
+        rows = tile_of(i, 16)
+        r.gs[0, rows, :] = r.kb[rows, :].astype(BF16)
+        r.gs[1, rows, :] = r.vb[rows, :].astype(BF16)
+
+    each(8, round_grads)
+    g_in[0] = share(r.gs, 0, near_g[0])
+    g_in[1] = share(r.gs, 1, near_g[1])
+
+    def mixed_first(m):
+        def put(span, part):
+            ratio = r.ratio[m : m + 1, span]
+            total = jnp.zeros((1, TILE), F32)
+            for q in range(2):
+                here = part[q * SPAN : (q + 1) * SPAN, :]
+                step = r.fn[q, 8:72, span] - r.fn[q, 0:64, span]
+                total = total + jnp.sum(step * here, axis=0, keepdims=True)
+                half = pl.ds(q * SPAN, SPAN)
+                if m == 0:
+                    r.ab[half, span] = here * ratio
+                    r.bb[q, 0:64, span] = here * (1.0 - ratio)
+                else:
+                    r.ab[half, span] = r.ab[half, span] + here * ratio
+                    r.bb[q, 0:64, span] = r.bb[q, 0:64, span] + here * (1.0 - ratio)
+            r.vec[m + 2 : m + 3, span] = total
+
+        return put
+
+    for m in range(3):
+        product(lambda: r.gs[m, own, :], r.watt.at[m], mixed_first(m), transposed=True)
+    for q in range(2):
+        r.hs3[q] = r.bb[q, 0:1, :]
+    halo3 = send(r.hs3, r.hr3, slots(1), s, prior)
+    weight_grad(4)
+    weight_grad(2)
+    weight_grad(0)
+    weight_grad(1)
+    halo3.wait_recv()
+    for q in range(2):
+        last = jnp.where(t < 7, r.hr3[q], 0.0)
+        r.bb[q, 64:72, :] = jnp.where(row8 == 7, last, pltpu.roll(r.bb[q, 0:8, :], 7, 0))
+
+    def back_one(i):
+        for q in range(2):
+            rows = pl.ds(pl.multiple_of(q * SPAN + i * 16, 16), 16)
+            grad = r.ab[rows, :] + r.bb[q, pl.ds(pl.multiple_of(8 + i * 16, 8), 16), :]
+            normed = r.n1[rows, :]
+            r.acc[2] = r.acc[2] + fold(grad * normed)
+            r.acc[3] = r.acc[3] + fold(grad)
+            dz = unnormalise(grad, normed, r.r1[rows, 0:1], r.gain[0:1, :])
+            r.rl[rows, :] = r.rl[rows, :] + dz
+
+    each(4, back_one)
+    for row, m in ((7, 2), (8, 0), (9, 3), (10, 1)):
+        r.vec[row : row + 1, :] = jnp.sum(r.acc[m], axis=0, keepdims=True)
+    r.vec[11:16, :] = jnp.zeros((5, 1024), F32)
+    vz_slot = slots(4)
+    vz_in = [
+        send(r.vec.at[:, tile_of(s ^ z, 256)], r.vz.at[z], vz_slot + z, s ^ z, t)
+        for z in range(1, 4)
+    ]
+
+    def put_in(n):
+        span = tile_of(n, TILE)
+        r.o_in[:, span] = swap_exact(swap, r.rl[:, span])
+
+    each(4, put_in)
+    r.pvb[...] = jnp.zeros_like(r.pvb)
+    for q in range(4):
+        span = pl.ds(q * 256, 256)
+        for i in range(2):
+            r.pvb[q, i : i + 1, :] = r.hr3[i, :, span]
+            r.pvb[q, 2 + i : 3 + i, :] = r.bsum[i, :, span]
+
+    def gather_plane(m):
+        for j in range(1, 4):
+            wire(
+                a_part(m, j), r.arecv.at[m, j - 1], a_slot[m] + j, s, t ^ (2 * j)
+            ).wait_recv()
+
+        def step(n):
+            span = tile_of(n, 256)
+            total = a_home[m][a_rows(m, 0), span].astype(F32)
+            for j in range(1, 4):
+                total = total + r.arecv[m, j - 1, :, span].astype(F32)
+            r.zsend[m, n] = total.astype(BF16)
+
+        each(4, step)
+        for z in range(1, 4):
+            send(r.zsend.at[m, s ^ z], r.zrecv.at[m, z - 1], z_slot[m] + z, s ^ z, t)
+
+    gather_plane(3)
+    for copy in vz_in:
+        copy.wait_recv()
+    mine = r.vec[:, tile_of(s, 256)] + r.vz[1] + (r.vz[2] + r.vz[3])
+    for x in range(8):
+        ref = r.vt if x == 0 else r.vss
+        ref[x, 0:16, :] = mine
+        ref[x, 16:24, :] = r.pvb[(t ^ x) // 2]
+    vt_slot = slots(8)
+    vt_in = [send(r.vss.at[x], r.vt.at[x], vt_slot + x, s, t ^ x) for x in range(1, 8)]
+    gather_plane(4)
+    gather_plane(2)
+    gather_plane(0)
+    gather_plane(1)
+    for copy in vt_in:
+        copy.wait_recv()
+    total = r.vt[0, 0:16, :]
+    for x in range(1, 8):
+        total = total + r.vt[x, 0:16, :]
+    r.o_vec[...] = total
+    r.o_prev[...] = r.vt[7 ^ t, 16:20, tile_of(t % 2, 128)]
+    for copy in fkz_in + fvz_in:
+        copy.wait_recv()
+
+    def out_key(i):
+        rows = tile_of(i, 64)
+        at = pl.ds(pl.multiple_of(s * 256 + i * 64, 64), 64)
+        total = r.fkz[at, :].astype(F32)
+        for z in range(1, 4):
+            total = total + r.fkt[z - 1, rows, :].astype(F32)
+        r.o_key[rows, :] = total
+
+    each(4, out_key)
+
+    def out_value(i):
+        rows = tile_of(i, 128)
+        total = r.fvz[s, rows, :].astype(F32)
+        for z in range(1, 4):
+            total = total + r.fvt[z - 1, rows, :].astype(F32)
+        r.o_val[rows, :] = total
+
+    each(4, out_value)
+    for m in (3, 4, 2, 0, 1):
+        for z in range(1, 4):
+            wire(
+                r.zsend.at[m, s ^ z], r.zrecv.at[m, z - 1], z_slot[m] + z, s ^ z, t
+            ).wait_recv()
+        total = r.zsend[m, s].astype(F32)
+        for z in range(1, 4):
+            total = total + r.zrecv[m, z - 1].astype(F32)
+        if m < 3:
+            r.o_att[m] = total
+        elif m == 3:
+            r.o_wout[...] = total
+        else:
+            r.o_wrec[...] = total
+
+    for j in range(1, 4):
+        for src, dst, slot in (
+            (r.pvs, r.pvr, pv_slot),
+            (r.gss, r.gsr, gs_slot),
+        ):
+            wire(src.at[j], dst.at[j - 1], slot + j, s, t ^ (2 * j)).wait_send()
+        for m in range(5):
+            wire(
+                a_part(m, j), r.arecv.at[m, j - 1], a_slot[m] + j, s, t ^ (2 * j)
+            ).wait_send()
+    for j in range(4):
+        wire(r.bts.at[j], r.btr.at[0], bt_slot + j, s, near, bt_home).wait_send()
+    for copy in sent:
+        copy.wait_send()
+    assert taken[0] <= SEMS
+
+
+SCRATCH["bs3"] = ((3, 2, 1024), F32)
+
+
+def fused_call(args):
+    (
+        layer_input,
+        prev_rows,
+        init_state,
+        time_decay,
+        time_first,
+        mix_ratios,
+        norm_gain,
+        norm_bias,
+        att_weights,
+        att_output,
+        ffn_receptance,
+        ffn_key,
+        ffn_value,
+        cotangent,
+    ) = args
+    vmem = pl.BlockSpec(memory_space=pltpu.VMEM)
+    anywhere = pl.BlockSpec(memory_space=pl.ANY)
+    shape = jax.ShapeDtypeStruct
+    out_shapes = [
+        shape((ROWS, 1024), BF16),
+        shape((ROWS, 1024), F32),
+        shape((4, 128), F32),
+        shape((3, 2, 128), F32),
+        shape((16, 256), F32),
+        shape((3, 128, 256), F32),
+        shape((128, 256), F32),
+        shape((128, 256), F32),
+        shape((256, 512), F32),
+        shape((512, 256), F32),
+    ]
+    outs = pl.pallas_call(
+        fused,
+        out_shape=out_shapes,
+        in_specs=[vmem] * 9 + [anywhere] * 5,
+        out_specs=[vmem] * 10,
+        scratch_shapes=[pltpu.VMEM(dims, kind) for dims, kind in SCRATCH.values()]
+        + [
+            pltpu.SemaphoreType.DMA((SEMS,)),
+            pltpu.SemaphoreType.DMA((SEMS,)),
+            pltpu.SemaphoreType.DMA((5,)),
+        ],
+        compiler_params=pltpu.CompilerParams(
+            collective_id=0, has_side_effects=True, vmem_limit_bytes=VMEM_LIMIT
+        ),
+    )(
+        layer_input.reshape(ROWS, 1024),
+        cotangent.reshape(ROWS, 1024),
+        prev_rows,
+        init_state,
+        time_decay.reshape(1, 1024),
+        time_first.reshape(1, 1024),
+        mix_ratios,
+        norm_gain,
+        norm_bias,
+        att_weights,
+        att_output,
+        ffn_receptance,
+        ffn_key,
+        ffn_value,
+    )
+    out, grad_in, prev, init, vec, att, wout, wrec, key, value = outs
+    mine = lax.dynamic_slice_in_dim(vec, lax.axis_index("tok") * 32, 32, 1)
+    return (
+        out.reshape(2, SPAN, 1024),
+        grad_in.reshape(2, SPAN, 1024),
+        prev.reshape(2, 2, 128),
+        init,
+        mine[0],
+        mine[1],
+        mine[2:7],
+        mine[7:9],
+        mine[9:11],
+        att,
+        wout,
+        wrec,
+        key,
+        value,
+    )
+
+
+VMEM_LIMIT = 62 * 2**20
+
+
 def solution(mesh):
+    def body(*args):
+        tok, seg = mesh.shape["tok"], mesh.shape["seg"]
+        seqs, length, width = args[0].shape
+        if (tok, seg, seqs, length, width, args[11].shape[1]) == (8, 4, 2, SPAN, 1024, HALF):
+            return fused_call(args)
+        return on_device(*args)
+
     return jax.shard_map(
-        on_device,
+        body,
         mesh=mesh,
         in_specs=(
             P("seg", "tok", None),

time: 1050 us -> 164 us (0.16)
  waiting for transfers between devices: 719 us -> 0 us
  Pallas kernels: 0 us -> 148 us
  other arithmetic: 124 us -> 0 us
  blocking collectives: 77.5 us -> 0 us
  matrix products: 53.4 us -> 0 us
  local copies, waits for them, and re-layouts: 41.9 us -> 14.9 us
  between operations: 18.1 us -> 0.7 us
    reduce_scatter x11 -> x0, waiting for transfers between devices: 489 us -> none  [the longest x1 110 us: on_device(): lax.psum_scatter(grad_att_w.astype(jnp.bfloat16), 'seg', scatter_dimensio...]
    unnamed x27 -> x0, waiting for transfers between devices: 170 us -> none
    pallas_call x0 -> x1, Pallas kernels: none -> 148 us  [fused_call(): pl.pallas_call(fused, out_shape=out_shapes, in_specs=[vmem] * 9 + [anywhe...]
    reduce_sum x109 -> x0, other arithmetic: 67.2 us -> none  [the longest x8 17.8 us: averaged_pair_segment(): jnp.where((earlier_position == later_position)[None, :, :, None], initial...]
    all_gather x2 -> x0, waiting for transfers between devices: 58 us -> none  [the longest x1 30.2 us: on_device(): rows_all = lax.all_gather(mix_key_two, 'tok', axis=1, tiled=True)]
    all_gather x6 -> x0, blocking collectives: 56.3 us -> none  [the longest x4 36.2 us: prefix(): lax.all_gather(part.astype(kind), axis)]
    dot_general x21 -> x0, matrix products: 53.4 us -> none  [the longest x7 19.9 us: project_back(): jnp.einsum('ste,de->std', grads_in, weight_mat, preferred_element_type=jn...]
    unnamed x2 -> x0, blocking collectives: 21.2 us -> none
  transfers between devices with their start and end apart: 24 -> 0, of which waited for: 21 -> 0; matrix products, arithmetic and copies ran while one was open for 5% -> 0% of each run, Pallas kernels for 0% -> 0%
where the time goes in v1:
time: 164 us; the launch traced here: 163 us
  Pallas kernels  148 us (90%)
  local copies, waits for them, and re-layouts  14.9 us (9%)
    pallas_call x1, Pallas kernels, fused_call(): pl.pallas_call(fused, out_shape=out_shapes, in_specs=[vmem] * 9 + [anywhe...  148 us
    unnamed x17, local copies, waits for them, and re-layouts  10.7 us

profile of v1, /device:TPU:0, one launch (start us, length us, event | category | flops | bytes accessed | tf_op | source)
XLA Modules:
  0.0 163.1 jit_solution(7270509426211534603)
XLA Ops:
  0.7 147.5 %shard_map.245 = (bf16[128,1024]{1,0:T(8,128)(2,1)}, f32[128,1024]{1,0:T(8,128)}, f32[4,128]{1,0:T(4,128)}, f32[3,2,128]{2,1,0:T(2,128)}, f32[16,256]{1,0:T(8,12...) custom-call(bf16[128,1024]{1,0:T(8,128)(2,1)} %bitcast.12, ...), custom_call_target="tpu_custom_call" | custom-call | tf_op jit(solution)/shard_map/pallas_call | solution.py:1403
  148.2 0.0 copy-start.3
  148.2 0.0 copy-start.2
  148.2 0.0 copy-start.1
  148.2 0.0 copy-start
  148.2 1.4 fusion
  149.7 1.3 dynamic-slice_bitcast_fusion
  151.0 1.3 dynamic-slice.2
  152.4 1.7 %copy.37 = bf16[2,64,1024]{2,1,0:T(8,128)(2,1)} copy(bf16[2,64,1024]{2,1,0:T(8,128)(2,1)} %bitcast.14) | data formatting | bytes 524288
  154.0 1.9 %copy.38 = f32[2,64,1024]{2,1,0:T(8,128)} copy(f32[2,64,1024]{2,1,0:T(8,128)} %bitcast.11) | data formatting | bytes 1048576
  155.9 1.2 copy.39
  157.2 1.2 copy.40
  158.4 1.8 %copy.41 = f32[3,128,256]{2,1,0:T(8,128)} copy(f32[3,128,256]{2,1,0:T(8,128)} %get-tuple-element.61) | data formatting | bytes 786432
  160.2 0.0 copy-done.3
  160.2 0.7 copy.42
  160.8 0.0 copy-done.2
  160.8 0.7 copy.43
  161.5 0.0 copy-done.1
  161.5 0.8 copy.44
  162.3 0.0 copy-done
  162.3 0.8 copy.45
Async XLA Ops:
  148.2 12.0 %copy-start.3 = (f32[128,256]{1,0:T(8,128)S(1)}, f32[128,256]{1,0:T(8,128)}, u32[]{:S(2)}) copy-start(f32[128,256]{1,0:T(8,128)} %get-tuple-element.62) | copy-start | bytes 393220
  148.2 12.6 %copy-start.2 = (f32[128,256]{1,0:T(8,128)S(1)}, f32[128,256]{1,0:T(8,128)}, u32[]{:S(2)}) copy-start(f32[128,256]{1,0:T(8,128)} %get-tuple-element.63) | copy-start | bytes 393220
  148.2 13.3 %copy-start.1 = (f32[256,512]{1,0:T(8,128)S(1)}, f32[256,512]{1,0:T(8,128)}, u32[]{:S(2)}) copy-start(f32[256,512]{1,0:T(8,128)} %get-tuple-element.64) | copy-start | bytes 1572868
  148.2 14.1 %copy-start = (f32[512,256]{1,0:T(8,128)S(1)}, f32[512,256]{1,0:T(8,128)}, u32[]{:S(2)}) copy-start(f32[512,256]{1,0:T(8,128)} %get-tuple-element.65) | copy-start | bytes 1572868

commit v2 on v1

--- a/solution.py
+++ b/solution.py
@@ -1,3 +1,4 @@
+import functools
 import types
 
 import jax
@@ -544,17 +545,17 @@
     sng=((4, ROWS, 1024), BF16),
     hs2=((2, 1, 1024), F32),
     hr2=((4, 2, 1, 1024), F32),
-    sf=((2, 72, 1024), F32),
+    sf=((4, 72, 1024), F32),
     mk=((4 * ROWS, 1024), BF16),
-    mg=((ROWS, 1024), BF16),
+    mg=((2 * ROWS, 1024), BF16),
     gv=((4 * ROWS, 1024), BF16),
     hid=((4 * ROWS, 1024), BF16),
     ghp=((4 * ROWS, 1024), BF16),
-    rl=((ROWS, 1024), F32),
-    cc=((ROWS, 1024), F32),
-    gg=((ROWS, 1024), BF16),
-    ab=((ROWS, 1024), F32),
-    bb=((2, 72, 1024), F32),
+    rl=((2 * ROWS, 1024), F32),
+    cc=((2 * ROWS, 1024), F32),
+    gg=((2 * ROWS, 1024), BF16),
+    ab=((2 * ROWS, 1024), F32),
+    bb=((4, 72, 1024), F32),
     pvs=((4, ROWS, 1024), BF16),
     pvr=((3, ROWS, 1024), BF16),
     gss=((4, ROWS, 1024), BF16),
@@ -565,24 +566,25 @@
     fks=((1024, 512), BF16),
     fkr=((1024, 512), BF16),
     fkz=((1024, 512), BF16),
-    fkt=((3, 256, 512), BF16),
+    fkt=((4, 256, 512), BF16),
     fvs=((4, 512, 256), BF16),
     fvr=((4, 512, 256), BF16),
     fvz=((4, 512, 256), BF16),
-    fvt=((3, 512, 256), BF16),
-    arecv=((5, 3, ROWS, 1024), BF16),
+    fvt=((4, 512, 256), BF16),
+    arecv=((3, 3, ROWS, 1024), BF16),
     zsend=((5, 4, ROWS, 256), BF16),
-    zrecv=((5, 3, ROWS, 256), BF16),
+    zrecv=((5, 4, ROWS, 256), BF16),
     hs3=((2, 1, 1024), F32),
     hr3=((2, 1, 1024), F32),
-    acc=((6, 8, 1024), F32),
+    acc=((9, 8, 1024), F32),
+    gm=((ROWS, 1024), F32),
     vec=((16, 1024), F32),
     vz=((4, 16, 256), F32),
     pvb=((4, 8, 256), F32),
     vss=((8, 24, 256), F32),
     vt=((8, 24, 256), F32),
 )
-SEMS = 128
+SEMS = 160
 INPUTS = (
     "x",
     "cot",
@@ -636,14 +638,25 @@
         )
 
     sent = []
-
-    def send(*args, **kw):
-        copy = wire(*args, **kw)
+    unread = {}
+
+    def track(copy):
+        sent.append(copy)
+        unread[id(copy)] = copy
+        return copy
+
+    def send(*args):
+        copy = track(wire(*args))
         copy.start()
-        sent.append(copy)
         return copy
 
+    def arrive(*copies):
+        for copy in copies:
+            copy.wait_recv()
+            del unread[id(copy)]
+
     loads = []
+    lines = {}
     for i, (src, dst) in enumerate(
         [
             (r.h_att, r.watt),
@@ -688,12 +701,21 @@
     near = t ^ 1
     key_in = send(r.h_key, r.wkey.at[:, pl.ds(HALF, HALF)], slots(1), s, near)
     val_in = send(r.h_val, r.wval.at[pl.ds(HALF, HALF), :], slots(1), s, near)
+    side_x, side_y, across = t ^ 2, t ^ 4, t ^ 6
+    upper, lower = pl.ds(0, SPAN), pl.ds(SPAN, SPAN)
     cot_slot = slots(4)
-    for j in range(1, 4):
-        send(r.cg.at[0], r.cg.at[j], cot_slot + j, s, t ^ (2 * j))
+    cot_in = [
+        send(r.cg.at[0], r.cg.at[1], cot_slot, s, side_x),
+        send(r.cg.at[0], r.cg.at[2], cot_slot + 1, s, side_y),
+    ]
 
     row8 = lax.broadcasted_iota(jnp.int32, (8, 1024), 0)
-    halo1.wait_recv()
+    row16 = lax.broadcasted_iota(jnp.int32, (16, 1024), 0)
+
+    def fold(x):
+        return x[0:8, :] + x[8:16, :]
+
+    arrive(halo1)
     for q in range(2):
         head = jnp.where(t == 0, r.prev[0, q : q + 1, :], r.hr1[q])
         r.fn[q, 0:8, :] = jnp.where(row8 == 0, head, pltpu.roll(r.fn[q, 64:72, :], 1, 0))
@@ -708,29 +730,25 @@
                 r.xs[m, rows, :] = (now * ratio + back * (1.0 - ratio)).astype(BF16)
 
     each(4, mix_one)
-    for copy in loads[:1]:
-        copy.wait()
-
-    def product(get, weights, put, transposed=False, tile=TILE):
+    loads.pop(0).wait()
+
+    def product(get, weights, put, transposed=False):
         def step(n):
-            span = tile_of(n, tile)
-            if transposed:
-                put(span, dot_nt(get(), weights[span, :]))
-            else:
-                put(span, dot_nn(get(), weights[:, span]))
-
-        each(1024 // tile, step)
+            dot = dot_nt if transposed else dot_nn
+            put(dot(get(), weights[...]))
+
+        each(1, step)
 
     own = pl.ds(0, ROWS)
 
     def keep(ref):
-        def put(span, part):
-            ref[:, span] = part
+        def put(part):
+            ref[...] = part
 
         return put
 
-    def keep_gate(span, part):
-        r.sr[:, span] = jax.nn.sigmoid(part)
+    def keep_gate(part):
+        r.sr[...] = jax.nn.sigmoid(part)
 
     product(lambda: r.xs[0, own, :], r.watt.at[0], keep(r.kb))
     product(lambda: r.xs[1, own, :], r.watt.at[1], keep(r.vb))
@@ -767,8 +785,8 @@
         send(r.ws, r.wr.at[x], state_slot + x, s, t ^ x) for x in range(1, 8)
     ]
     product(lambda: r.xs[2, own, :], r.watt.at[2], keep_gate)
-    for copy in loads[1:]:
-        copy.wait()
+    while loads:
+        loads.pop().wait()
     near_x = [slots(1) for _ in range(5)]
     near_g = [slots(1) for _ in range(5)]
     far = pl.ds(ROWS, ROWS)
@@ -777,8 +795,7 @@
         return send(ref.at[m, own, :], ref.at[m, far, :], slot, s, near)
 
     x_in = [share(r.xs, m, near_x[m]) for m in range(3)]
-    for copy in state_in:
-        copy.wait_recv()
+    arrive(*state_in)
 
     def far_state(ref, base_p, sel, steps):
         peak = base_p
@@ -833,6 +850,11 @@
                 a, b, p = join(a, b, p + w, vv, 1.0, kk)
 
     each(2, full_scan)
+    arrive(*cot_in)
+    cot_in = [
+        send(r.cg.at[2, upper, :], r.cg.at[3, upper, :], cot_slot + 2, s, side_x),
+        send(r.cg.at[1, lower, :], r.cg.at[3, lower, :], cot_slot + 3, s, side_y),
+    ]
 
     def weigh(i):
         rows = tile_of(i, 16)
@@ -841,8 +863,8 @@
     each(8, weigh)
     x_in.append(share(r.xs, 3, near_x[3]))
 
-    def keep_middle(span, part):
-        r.mid[:, span] = r.xp[:, span].astype(F32) + part
+    def keep_middle(part):
+        r.mid[...] = r.xp[...].astype(F32) + part
 
     product(lambda: r.xs[3, own, :], r.wout, keep_middle)
 
@@ -862,159 +884,258 @@
         send(r.hs2, r.hr2.at[i], halo_slot + i, s, t ^ (2 * i + 1)) for i in range(4)
     ]
     sn_slot = slots(4)
-    for j in range(1, 4):
-        send(r.sng.at[0], r.sng.at[j], sn_slot + j, s, t ^ (2 * j))
-    key_in.wait_recv()
-    val_in.wait_recv()
-    for copy in halo2:
-        copy.wait_recv()
+    sn_in = [
+        send(r.sng.at[0], r.sng.at[j], sn_slot + j, s, t ^ (2 * j)) for j in range(1, 3)
+    ]
+    arrive(key_in, val_in, *halo2)
     r.acc[...] = jnp.zeros_like(r.acc)
-    r.vec[5:7, :] = jnp.zeros((2, 1024), F32)
-
-    pv_slot = slots(4)
     gs_slot = slots(4)
     bt_slot = slots(4)
     bt_home = slots(4)
 
-    def block(j):
-        b = t ^ (2 * j)
-        rows = tile_of(j, ROWS)
-
-        @pl.when(j > 0)
-        def _():
-            wire(r.sng.at[0], r.sng.at[j], sn_slot + j, s, b).wait_recv()
-            wire(r.cg.at[0], r.cg.at[j], cot_slot + j, s, b).wait_recv()
-
-        source = (((b + 7) % 8) ^ t) // 2
-        for q in range(2):
+    def block(js):
+        count = len(js)
+        rows = pl.ds(js[0] * ROWS, count * ROWS)
+        top_rows = pl.ds(0, count * ROWS)
+        groups = [(n, j, q, 2 * n + q) for n, j in enumerate(js) for q in range(2)]
+        for n, j, q, g in groups:
+            b = t ^ (2 * j)
+            source = (((b + 7) % 8) ^ t) // 2
             for i in range(4):
-                r.sf[q, pl.ds(8 + 16 * i, 16), :] = r.sng[
+                r.sf[g, pl.ds(8 + 16 * i, 16), :] = r.sng[
                     j, pl.ds(q * SPAN + 16 * i, 16), :
                 ].astype(F32)
             head = jnp.where(b == 0, r.prev[1, q : q + 1, :], r.hr2[source, q])
-            r.sf[q, 0:8, :] = jnp.where(
-                row8 == 0, head, pltpu.roll(r.sf[q, 64:72, :], 1, 0)
+            r.sf[g, 0:8, :] = jnp.where(
+                row8 == 0, head, pltpu.roll(r.sf[g, 64:72, :], 1, 0)
             )
 
         def mix_two(i):
-            for q in range(2):
-                now = r.sf[q, pl.ds(pl.multiple_of(8 + i * 16, 8), 16), :]
-                back = r.sf[q, tile_of(i, 16), :]
-                at = pl.multiple_of(q * SPAN + i * 16, 16)
+            for n, j, q, g in groups:
+                now = r.sf[g, pl.ds(pl.multiple_of(8 + i * 16, 8), 16), :]
+                back = r.sf[g, tile_of(i, 16), :]
+                at = pl.multiple_of(i * 16, 16)
                 r3 = r.ratio[3:4, :]
                 r4 = r.ratio[4:5, :]
-                r.mk[pl.ds(pl.multiple_of(j * ROWS + at, 16), 16), :] = (
+                r.mk[pl.ds(j * ROWS + q * SPAN + at, 16), :] = (
                     now * r3 + back * (1.0 - r3)
                 ).astype(BF16)
-                r.mg[pl.ds(at, 16), :] = (now * r4 + back * (1.0 - r4)).astype(BF16)
+                r.mg[pl.ds(n * ROWS + q * SPAN + at, 16), :] = (
+                    now * r4 + back * (1.0 - r4)
+                ).astype(BF16)
 
         each(4, mix_two)
-
-        @pl.when(j == 0)
-        def _():
-            r.xs[4, own, :] = r.mg[...]
-
-        def put_gate(span, part):
+        if js[0] == 0:
+            r.xs[4, own, :] = r.mg[own, :]
+
+        def put_gate(part):
             sg = jax.nn.sigmoid(part)
-            top = r.cg[j, :, span].astype(F32) * sg
-            r.gv[rows, span] = top.astype(BF16)
-            r.cc[:, span] = top * (1.0 - sg)
-
-        product(lambda: r.mg[...], r.wrec, put_gate)
-
-        def put_hidden(span, part):
+            for n, j in enumerate(js):
+                here = sg[n * ROWS : (n + 1) * ROWS, :]
+                top = r.cg[j].astype(F32) * here
+                r.gv[pl.ds(j * ROWS, ROWS), :] = top.astype(BF16)
+                r.cc[pl.ds(n * ROWS, ROWS), :] = top * (1.0 - here)
+
+        product(lambda: r.mg[top_rows, :], r.wrec, put_gate)
+
+        def put_hidden(part):
             relu = jnp.maximum(part, 0.0)
-            r.rl[:, span] = relu
-            r.hid[rows, span] = (relu * relu).astype(BF16)
+            r.rl[top_rows, :] = relu
+            r.hid[rows, :] = (relu * relu).astype(BF16)
 
         product(lambda: r.mk[rows, :], r.wkey, put_hidden)
 
-        def put_hidden_grad(span, part):
-            r.ghp[rows, span] = (part * 2.0 * r.rl[:, span]).astype(BF16)
+        def put_hidden_grad(part):
+            r.ghp[rows, :] = (part * 2.0 * r.rl[top_rows, :]).astype(BF16)
 
         product(lambda: r.gv[rows, :], r.wval, put_hidden_grad, transposed=True)
 
-        def put_value(span, part):
-            r.pvs[j, :, span] = part.astype(BF16)
-            r.gg[:, span] = (part * r.cc[:, span]).astype(BF16)
+        def put_value(part):
+            for n, j in enumerate(js):
+                r.pvs[j] = part[n * ROWS : (n + 1) * ROWS, :].astype(BF16)
+            r.gg[top_rows, :] = (part * r.cc[top_rows, :]).astype(BF16)
 
         product(lambda: r.hid[rows, :], r.wval, put_value)
 
-        def mixed_back(m, first):
-            def put(span, part):
-                ratio = r.ratio[m : m + 1, span]
-                total = jnp.zeros((1, TILE), F32)
-                for q in range(2):
-                    here = part[q * SPAN : (q + 1) * SPAN, :]
-                    step = r.sf[q, 8:72, span] - r.sf[q, 0:64, span]
-                    total = total + jnp.sum(step * here, axis=0, keepdims=True)
-                    half = pl.ds(q * SPAN, SPAN)
-                    if first:
-                        r.ab[half, span] = here * ratio
-                        r.bb[q, 0:64, span] = here * (1.0 - ratio)
-                    else:
-                        r.ab[half, span] = r.ab[half, span] + here * ratio
-                        r.bb[q, 0:64, span] = r.bb[q, 0:64, span] + here * (1.0 - ratio)
-                r.vec[m + 2 : m + 3, span] = r.vec[m + 2 : m + 3, span] + total
-
-            return put
-
-        product(lambda: r.ghp[rows, :], r.wkey, mixed_back(3, True), transposed=True)
-        product(lambda: r.gg[...], r.wrec, mixed_back(4, False), transposed=True)
-        for q in range(2):
-            r.bts[j, q] = r.bb[q, 0:1, :]
-            r.bb[q, 64:72, :] = jnp.where(row8 == 7, 0.0, pltpu.roll(r.bb[q, 0:8, :], 7, 0))
-            for i in range(4):
-                at = pl.ds(q * SPAN + 16 * i, 16)
-                r.gss[j, at, :] = (r.ab[at, :] + r.bb[q, pl.ds(8 + 16 * i, 16), :]).astype(
-                    BF16
-                )
-        wire(r.bts.at[j], r.btr.at[chip], bt_slot + j, s, (b + 7) % 8, bt_home + chip).start()
-
-        @pl.when(j > 0)
-        def _():
-            wire(r.gss.at[j], r.gsr.at[j - 1], gs_slot + j, s, b).start()
-            wire(r.pvs.at[j], r.pvr.at[j - 1], pv_slot + j, s, b).start()
-
-    each(4, block)
+        def put_key_back(part):
+            r.ab[top_rows, :] = part
+
+        def put_gate_back(part):
+            r.rl[top_rows, :] = part
+
+        product(lambda: r.ghp[rows, :], r.wkey, put_key_back, transposed=True)
+        product(lambda: r.gg[top_rows, :], r.wrec, put_gate_back, transposed=True)
+
+        def mixed_back(i):
+            r3 = r.ratio[3:4, :]
+            r4 = r.ratio[4:5, :]
+            for n, j, q, g in groups:
+                now = r.sf[g, pl.ds(pl.multiple_of(8 + i * 16, 8), 16), :]
+                step = now - r.sf[g, tile_of(i, 16), :]
+                at = pl.ds(pl.multiple_of(g * SPAN + i * 16, 16), 16)
+                gk = r.ab[at, :]
+                gm = r.rl[at, :]
+                r.acc[4] = r.acc[4] + fold(step * gk)
+                r.acc[5] = r.acc[5] + fold(step * gm)
+                r.ab[at, :] = gk * r3 + gm * r4
+                r.bb[g, tile_of(i, 16), :] = gk * (1.0 - r3) + gm * (1.0 - r4)
+
+        each(4, mixed_back)
+        for n, j, q, g in groups:
+            r.bts[j, q] = r.bb[g, 0:1, :]
+            r.bb[g, 64:72, :] = jnp.where(row8 == 7, 0.0, pltpu.roll(r.bb[g, 0:8, :], 7, 0))
+
+        def shifted(i):
+            for n, j, q, g in groups:
+                at = pl.ds(pl.multiple_of(g * SPAN + i * 16, 16), 16)
+                r.gss[j, pl.ds(pl.multiple_of(q * SPAN + i * 16, 16), 16), :] = (
+                    r.ab[at, :] + r.bb[g, pl.ds(pl.multiple_of(8 + i * 16, 8), 16), :]
+                ).astype(BF16)
+
+        each(4, shifted)
+        for j in js:
+            b = t ^ (2 * j)
+            copy = wire(
+                r.bts.at[j], r.btr.at[chip], bt_slot + j, s, (b + 7) % 8, bt_home + chip
+            )
+            copy.start()
+            sent.append(copy)
+            if j:
+                gs_in.append(send(r.gss.at[j], r.gsr.at[j - 1], gs_slot + j, s, b))
+
+    gs_in = []
+    block((0,))
+    sn_in.append(send(r.sng.at[0], r.sng.at[3], sn_slot + 3, s, across))
+    arrive(*sn_in[:2])
+    block((1, 2))
+    arrive(*cot_in, *sn_in[2:])
+    block((3,))
+    bt_in = [
+        wire(r.bts.at[i], r.btr.at[i], bt_slot + i, s, near, bt_home + i) for i in range(4)
+    ]
+    for copy in bt_in:
+        unread[id(copy)] = copy
+
+    class PlaneSum:
+        def __init__(self, part, landing):
+            self.part, self.landing = part, landing
+            self.slot = slots(6)
+
+        def go(self, n, j, half, tok, place):
+            return send(
+                self.part(j, half), self.landing(place, half), self.slot + n, s, tok
+            )
+
+        def first(self):
+            self.hop = [self.go(0, 3, upper, side_x, 2), self.go(1, 3, lower, side_y, 2)]
+            self.last = [self.go(2, 1, upper, side_x, 0)]
+
+        def second(self):
+            self.last.append(self.go(3, 2, lower, side_y, 1))
+
+        def pump(self):
+            for copy, n, j, half, tok, place in (
+                (self.hop[0], 4, 2, upper, side_y, 1),
+                (self.hop[1], 5, 1, lower, side_x, 0),
+            ):
+                arrive(copy)
+                ref, more = self.part(j, half), self.landing(2, half)
+                ref[...] = (ref[...].astype(F32) + more[...].astype(F32)).astype(BF16)
+                self.last.append(self.go(n, j, half, tok, place))
+
+        def finish(self):
+            arrive(*self.last)
+
+    value_sum = PlaneSum(
+        lambda j, half: r.pvs.at[j, half, :], lambda n, half: r.pvr.at[n, half, :]
+    )
+    value_sum.first()
+    value_sum.second()
     x_in.append(share(r.xs, 4, near_x[4]))
 
     def key_grad(half, ref):
         def step(n):
-            rows = tile_of(n, 256)
+            rows = tile_of(n, 512)
             ref[rows, :] = dot_tn(
                 r.mk[:, rows], r.ghp[:, pl.ds(half * HALF, HALF)]
             ).astype(BF16)
 
-        each(4, step)
+        each(2, step)
 
     def value_grad(half, ref):
         def step(n):
-            ref[n] = dot_tn(
-                r.hid[:, pl.ds(half * HALF, HALF)], r.gv[:, tile_of(n, 256)]
-            ).astype(BF16)
-
-        each(4, step)
-
+            part = dot_tn(r.hid[:, pl.ds(half * HALF, HALF)], r.gv[:, tile_of(n, 512)])
+            ref[2 * n] = part[:, 0:256].astype(BF16)
+            ref[2 * n + 1] = part[:, 256:512].astype(BF16)
+
+        each(2, step)
+
+    middle_seg = (s == 1) | (s == 2)
+    end_seg = (s == 0) | (s == 3)
+
+    class LineSum:
+        def __init__(self, part, landing):
+            self.part, self.landing = part, landing
+            self.slot = slots(4)
+            lines[id(self)] = self
+            self.pumped = False
+
+        def copy(self, chunk, place, seg):
+            return wire(
+                self.part(chunk), self.landing(place), self.slot + place, seg, t
+            )
+
+        def first(self):
+            @pl.when(end_seg)
+            def _():
+                self.copy(s ^ 3, 3, s ^ 1).start()
+
+            self.copy(s ^ 1, 0, s ^ 1).start()
+
+            @pl.when(end_seg)
+            def _():
+                self.copy(s ^ 2, 1, s ^ 2).start()
+
+            @pl.when(middle_seg)
+            def _():
+                self.copy(s ^ 3, 2, s ^ 3).start()
+
+        def pump(self):
+            self.pumped = True
+
+            @pl.when(middle_seg)
+            def _():
+                self.copy(s ^ 3, 3, s ^ 1).wait_recv()
+                ref, more = self.part(s ^ 2), self.landing(3)
+                ref[...] = (ref[...].astype(F32) + more[...].astype(F32)).astype(BF16)
+                self.copy(s ^ 2, 1, s ^ 2).start()
+
+        def finish(self):
+            del lines[id(self)]
+            self.copy(s ^ 1, 0, s ^ 1).wait()
+            self.copy(s ^ 2, 1, s ^ 2).wait()
+
+            @pl.when(middle_seg)
+            def _():
+                self.copy(s ^ 3, 2, s ^ 3).wait()
+
+            @pl.when(end_seg)
+            def _():
+                self.copy(s ^ 3, 3, s ^ 1).wait_send()
+
+        def total(self, rows):
+            out = self.part(s)[rows, :].astype(F32)
+            out = out + self.landing(0)[rows, :].astype(F32)
+            out = out + self.landing(1)[rows, :].astype(F32)
+            more = self.landing(2)[rows, :].astype(F32)
+            return out + jnp.where(middle_seg, more, 0.0)
+
+    value_grad(1, r.fvs)
+    fv_in = send(r.fvs, r.fvr, slots(1), s, near)
     key_grad(1, r.fks)
     fk_in = send(r.fks, r.fkr, slots(1), s, near)
-    value_grad(1, r.fvs)
-    fv_in = send(r.fvs, r.fvr, slots(1), s, near)
-    key_grad(0, r.fkz)
     value_grad(0, r.fvz)
-    fk_in.wait_recv()
-
-    def add_key(i):
-        rows = tile_of(i, 64)
-        r.fkz[rows, :] = (r.fkz[rows, :].astype(F32) + r.fkr[rows, :].astype(F32)).astype(BF16)
-
-    each(16, add_key)
-    fk_slot = slots(4)
-    fkz_in = [
-        send(r.fkz.at[tile_of(s ^ z, 256), :], r.fkt.at[z - 1], fk_slot + z, s ^ z, t)
-        for z in range(1, 4)
-    ]
-    fv_in.wait_recv()
+    arrive(fv_in)
 
     def add_value(n):
         for i in range(4):
@@ -1024,21 +1145,23 @@
             ).astype(BF16)
 
     each(4, add_value)
-    fv_slot = slots(4)
-    fvz_in = [
-        send(r.fvz.at[s ^ z], r.fvt.at[z - 1], fv_slot + z, s ^ z, t) for z in range(1, 4)
-    ]
-
-    for i in range(4):
-        wire(r.bts.at[0], r.btr.at[i], bt_slot, s, near, bt_home + i).wait_recv()
-    for j in range(1, 4):
-        wire(r.gss.at[j], r.gsr.at[j - 1], gs_slot + j, s, t ^ (2 * j)).wait_recv()
+    value_line = LineSum(lambda n: r.fvz.at[n], lambda n: r.fvt.at[n])
+    value_line.first()
+    key_grad(0, r.fkz)
+    arrive(fk_in)
+
+    def add_key(i):
+        rows = tile_of(i, 128)
+        r.fkz[rows, :] = (r.fkz[rows, :].astype(F32) + r.fkr[rows, :].astype(F32)).astype(BF16)
+
+    each(8, add_key)
+    key_line = LineSum(lambda n: r.fkz.at[tile_of(n, 256), :], lambda n: r.fkt.at[n])
+    key_line.first()
+    value_sum.pump()
+
+    arrive(*bt_in, *gs_in)
     for q in range(2):
         r.bsum[q] = r.btr[0, q] + r.btr[1, q] + (r.btr[2, q] + r.btr[3, q])
-    row16 = lax.broadcasted_iota(jnp.int32, (16, 1024), 0)
-
-    def fold(x):
-        return x[0:8, :] + x[8:16, :]
 
     def back_two(i):
         for q in range(2):
@@ -1053,18 +1176,17 @@
             r.acc[1] = r.acc[1] + fold(grad)
             dz = unnormalise(grad, normed, r.r2[rows, 0:1], r.gain[1:2, :])
             total = r.cg[0, rows, :].astype(F32) + dz
-            r.rl[rows, :] = total
+            r.gm[rows, :] = total
             r.gs[3, rows, :] = total.astype(BF16)
 
     each(4, back_two)
     g_in = {3: share(r.gs, 3, near_g[3])}
 
-    def put_branch(span, part):
-        sr = r.sr[:, span]
-        out = r.ou[:, span]
+    def put_branch(part):
+        sr = r.sr[...]
         grad = part * sr
-        r.gs[2, own, span] = (grad * out * (1.0 - sr)).astype(BF16)
-        r.rd[:, span] = grad * r.rd[:, span]
+        r.gs[2, own, :] = (grad * r.ou[...] * (1.0 - sr)).astype(BF16)
+        r.rd[...] = grad * r.rd[...]
 
     product(lambda: r.gs[3, own, :], r.wout, put_branch, transposed=True)
     g_in[2] = share(r.gs, 2, near_g[2])
@@ -1094,21 +1216,17 @@
     back_slot = slots(8)
     back_in = [send(r.bs, r.br.at[x], back_slot + x, s, t ^ x) for x in range(1, 8)]
 
-    for j in range(1, 4):
-        wire(r.pvs.at[j], r.pvr.at[j - 1], pv_slot + j, s, t ^ (2 * j)).wait_recv()
-
-    product_gate = lambda span, part: put_out(span, jax.nn.sigmoid(part))
-
-    def put_out(span, sg):
-        value = r.pvs[0, :, span].astype(F32)
-        for j in range(1, 4):
-            value = value + r.pvr[j - 1, :, span].astype(F32)
-        out = r.mid[:, span] + sg * value
-        top = r.cg[0, :, span].astype(F32)
-        r.gs[4, own, span] = (top * value * sg * (1.0 - sg)).astype(BF16)
-        r.o_out[:, span] = dot_nn(swap, out.astype(BF16)).astype(BF16)
-
-    product(lambda: r.xs[4, own, :], r.wrec, product_gate)
+    value_sum.finish()
+
+    def put_out(part):
+        sg = jax.nn.sigmoid(part)
+        value = r.pvs[0].astype(F32) + r.pvr[0].astype(F32) + r.pvr[1].astype(F32)
+        out = r.mid[...] + sg * value
+        top = r.cg[0].astype(F32)
+        r.gs[4, own, :] = (top * value * sg * (1.0 - sg)).astype(BF16)
+        r.o_out[...] = dot_nn(swap, out.astype(BF16)).astype(BF16)
+
+    product(lambda: r.xs[4, own, :], r.wrec, put_out)
     g_in[4] = share(r.gs, 4, near_g[4])
 
     a_home = (r.wval, r.mk, r.wval, r.wkey, r.wkey)
@@ -1117,31 +1235,43 @@
     def a_rows(m, j):
         return tile_of(a_base[m] + j, ROWS)
 
-    def a_part(m, j):
-        return a_home[m].at[a_rows(m, j), :]
-
-    a_slot = [slots(4) for _ in range(5)]
-    z_slot = [slots(4) for _ in range(5)]
+    land_home = (r.hid, r.ghp, r.arecv.at[0], r.arecv.at[1], r.arecv.at[2])
+
+    def a_landing(m, n, half):
+        if m < 2:
+            return land_home[m].at[pl.ds(n * ROWS + half.start, SPAN), :]
+        return land_home[m].at[n, half, :]
+
+    def a_piece(m, j, half):
+        return a_home[m].at[
+            pl.ds((a_base[m] + j) * ROWS + half.start, SPAN), :
+        ]
+
+    plane_sums = {}
+    line_sums = {}
 
     def weight_grad(m):
-        x_in[m].wait_recv()
-        g_in[m].wait_recv()
-
-        def step(j):
-            cols = tile_of(t ^ (2 * j), 128)
-            a_home[m][a_rows(m, j), :] = dot_tn(r.xs[m, :, cols], r.gs[m]).astype(BF16)
-
-            @pl.when(j > 0)
-            def _():
-                wire(
-                    a_part(m, j), r.arecv.at[m, j - 1], a_slot[m] + j, s, t ^ (2 * j)
-                ).start()
-
-        each(4, step)
+        arrive(x_in[m], g_in[m])
+        plane_sums[m] = PlaneSum(functools.partial(a_piece, m), functools.partial(a_landing, m))
+
+        def pair(j, j2):
+            cols = [r.xs[m, :, tile_of(t ^ (2 * i), 128)] for i in (j, j2)]
+            both = dot_tn(jnp.concatenate(cols, axis=1), r.gs[m]).astype(BF16)
+            a_home[m][a_rows(m, j), :] = both[0:ROWS, :]
+            a_home[m][a_rows(m, j2), :] = both[ROWS : 2 * ROWS, :]
+
+        each(1, lambda i: pair(3, 1))
+        plane_sums[m].first()
+        each(1, lambda i: pair(2, 0))
+        plane_sums[m].second()
 
     weight_grad(3)
-    for copy in back_in:
-        copy.wait_recv()
+    weight_grad(2)
+    weight_grad(4)
+    value_line.pump()
+    plane_sums[3].pump()
+    plane_sums[2].pump()
+    arrive(*back_in)
 
     later = lambda j: j > t
     gap_back = lambda j: 64.0 * (j - 1.0 - tf)
@@ -1209,35 +1339,38 @@
     g_in[0] = share(r.gs, 0, near_g[0])
     g_in[1] = share(r.gs, 1, near_g[1])
 
-    def mixed_first(m):
-        def put(span, part):
-            ratio = r.ratio[m : m + 1, span]
-            total = jnp.zeros((1, TILE), F32)
-            for q in range(2):
-                here = part[q * SPAN : (q + 1) * SPAN, :]
-                step = r.fn[q, 8:72, span] - r.fn[q, 0:64, span]
-                total = total + jnp.sum(step * here, axis=0, keepdims=True)
-                half = pl.ds(q * SPAN, SPAN)
-                if m == 0:
-                    r.ab[half, span] = here * ratio
-                    r.bb[q, 0:64, span] = here * (1.0 - ratio)
-                else:
-                    r.ab[half, span] = r.ab[half, span] + here * ratio
-                    r.bb[q, 0:64, span] = r.bb[q, 0:64, span] + here * (1.0 - ratio)
-            r.vec[m + 2 : m + 3, span] = total
-
-        return put
-
-    for m in range(3):
-        product(lambda: r.gs[m, own, :], r.watt.at[m], mixed_first(m), transposed=True)
+    for m, ref in enumerate((r.ab, r.rl, r.cc)):
+
+        def put_mixed(part):
+            ref[own, :] = part
+
+        product(lambda: r.gs[m, own, :], r.watt.at[m], put_mixed, transposed=True)
+
+    def mixed_first(i):
+        for q in range(2):
+            now = r.fn[q, pl.ds(pl.multiple_of(8 + i * 16, 8), 16), :]
+            step = now - r.fn[q, tile_of(i, 16), :]
+            at = pl.ds(pl.multiple_of(q * SPAN + i * 16, 16), 16)
+            here = jnp.zeros((16, 1024), F32)
+            ahead = jnp.zeros((16, 1024), F32)
+            for m, ref in enumerate((r.ab, r.rl, r.cc)):
+                part = ref[at, :]
+                ratio = r.ratio[m : m + 1, :]
+                r.acc[6 + m] = r.acc[6 + m] + fold(step * part)
+                here = here + part * ratio
+                ahead = ahead + part * (1.0 - ratio)
+            r.ab[at, :] = here
+            r.bb[q, tile_of(i, 16), :] = ahead
+
+    each(4, mixed_first)
     for q in range(2):
         r.hs3[q] = r.bb[q, 0:1, :]
     halo3 = send(r.hs3, r.hr3, slots(1), s, prior)
-    weight_grad(4)
-    weight_grad(2)
     weight_grad(0)
     weight_grad(1)
-    halo3.wait_recv()
+    plane_sums[4].pump()
+    key_line.pump()
+    arrive(halo3)
     for q in range(2):
         last = jnp.where(t < 7, r.hr3[q], 0.0)
         r.bb[q, 64:72, :] = jnp.where(row8 == 7, last, pltpu.roll(r.bb[q, 0:8, :], 7, 0))
@@ -1250,10 +1383,12 @@
             r.acc[2] = r.acc[2] + fold(grad * normed)
             r.acc[3] = r.acc[3] + fold(grad)
             dz = unnormalise(grad, normed, r.r1[rows, 0:1], r.gain[0:1, :])
-            r.rl[rows, :] = r.rl[rows, :] + dz
+            r.gm[rows, :] = r.gm[rows, :] + dz
 
     each(4, back_one)
-    for row, m in ((7, 2), (8, 0), (9, 3), (10, 1)):
+    for row, m in (
+        (2, 6), (3, 7), (4, 8), (5, 4), (6, 5), (7, 2), (8, 0), (9, 3), (10, 1)
+    ):
         r.vec[row : row + 1, :] = jnp.sum(r.acc[m], axis=0, keepdims=True)
     r.vec[11:16, :] = jnp.zeros((5, 1024), F32)
     vz_slot = slots(4)
@@ -1263,10 +1398,9 @@
     ]
 
     def put_in(n):
-        span = tile_of(n, TILE)
-        r.o_in[:, span] = swap_exact(swap, r.rl[:, span])
-
-    each(4, put_in)
+        r.o_in[...] = swap_exact(swap, r.gm[...])
+
+    each(1, put_in)
     r.pvb[...] = jnp.zeros_like(r.pvb)
     for q in range(4):
         span = pl.ds(q * 256, 256)
@@ -1275,25 +1409,30 @@
             r.pvb[q, 2 + i : 3 + i, :] = r.bsum[i, :, span]
 
     def gather_plane(m):
-        for j in range(1, 4):
-            wire(
-                a_part(m, j), r.arecv.at[m, j - 1], a_slot[m] + j, s, t ^ (2 * j)
-            ).wait_recv()
+        plane_sums[m].finish()
 
         def step(n):
             span = tile_of(n, 256)
             total = a_home[m][a_rows(m, 0), span].astype(F32)
-            for j in range(1, 4):
-                total = total + r.arecv[m, j - 1, :, span].astype(F32)
+            for k in range(2):
+                if m < 2:
+                    more = land_home[m][pl.ds(k * ROWS, ROWS), span]
+                else:
+                    more = land_home[m][k, :, span]
+                total = total + more.astype(F32)
             r.zsend[m, n] = total.astype(BF16)
 
         each(4, step)
-        for z in range(1, 4):
-            send(r.zsend.at[m, s ^ z], r.zrecv.at[m, z - 1], z_slot[m] + z, s ^ z, t)
+        line_sums[m] = LineSum(lambda n: r.zsend.at[m, n], lambda n: r.zrecv.at[m, n])
+        line_sums[m].first()
 
     gather_plane(3)
-    for copy in vz_in:
-        copy.wait_recv()
+    plane_sums[0].pump()
+    gather_plane(2)
+    plane_sums[1].pump()
+    line_sums[3].pump()
+    gather_plane(4)
+    arrive(*vz_in)
     mine = r.vec[:, tile_of(s, 256)] + r.vz[1] + (r.vz[2] + r.vz[3])
     for x in range(8):
         ref = r.vt if x == 0 else r.vss
@@ -1301,46 +1440,35 @@
         ref[x, 16:24, :] = r.pvb[(t ^ x) // 2]
     vt_slot = slots(8)
     vt_in = [send(r.vss.at[x], r.vt.at[x], vt_slot + x, s, t ^ x) for x in range(1, 8)]
-    gather_plane(4)
-    gather_plane(2)
+    line_sums[2].pump()
     gather_plane(0)
+    line_sums[4].pump()
     gather_plane(1)
-    for copy in vt_in:
-        copy.wait_recv()
+    line_sums[0].pump()
+    line_sums[1].pump()
+    arrive(*vt_in)
     total = r.vt[0, 0:16, :]
     for x in range(1, 8):
         total = total + r.vt[x, 0:16, :]
     r.o_vec[...] = total
     r.o_prev[...] = r.vt[7 ^ t, 16:20, tile_of(t % 2, 128)]
-    for copy in fkz_in + fvz_in:
-        copy.wait_recv()
+    value_line.finish()
+    key_line.finish()
 
     def out_key(i):
         rows = tile_of(i, 64)
-        at = pl.ds(pl.multiple_of(s * 256 + i * 64, 64), 64)
-        total = r.fkz[at, :].astype(F32)
-        for z in range(1, 4):
-            total = total + r.fkt[z - 1, rows, :].astype(F32)
-        r.o_key[rows, :] = total
+        r.o_key[rows, :] = key_line.total(rows)
 
     each(4, out_key)
 
     def out_value(i):
         rows = tile_of(i, 128)
-        total = r.fvz[s, rows, :].astype(F32)
-        for z in range(1, 4):
-            total = total + r.fvt[z - 1, rows, :].astype(F32)
-        r.o_val[rows, :] = total
+        r.o_val[rows, :] = value_line.total(rows)
 
     each(4, out_value)
-    for m in (3, 4, 2, 0, 1):
-        for z in range(1, 4):
-            wire(
-                r.zsend.at[m, s ^ z], r.zrecv.at[m, z - 1], z_slot[m] + z, s ^ z, t
-            ).wait_recv()
-        total = r.zsend[m, s].astype(F32)
-        for z in range(1, 4):
-            total = total + r.zrecv[m, z - 1].astype(F32)
+    for m in (3, 2, 4, 0, 1):
+        line_sums[m].finish()
+        total = line_sums[m].total(pl.ds(0, ROWS))
         if m < 3:
             r.o_att[m] = total
         elif m == 3:
@@ -1348,21 +1476,9 @@
         else:
             r.o_wrec[...] = total
 
-    for j in range(1, 4):
-        for src, dst, slot in (
-            (r.pvs, r.pvr, pv_slot),
-            (r.gss, r.gsr, gs_slot),
-        ):
-            wire(src.at[j], dst.at[j - 1], slot + j, s, t ^ (2 * j)).wait_send()
-        for m in range(5):
-            wire(
-                a_part(m, j), r.arecv.at[m, j - 1], a_slot[m] + j, s, t ^ (2 * j)
-            ).wait_send()
-    for j in range(4):
-        wire(r.bts.at[j], r.btr.at[0], bt_slot + j, s, near, bt_home).wait_send()
     for copy in sent:
         copy.wait_send()
-    assert taken[0] <= SEMS
+    assert not unread and not lines and taken[0] <= SEMS
 
 
 SCRATCH["bs3"] = ((3, 2, 1024), F32)
@@ -1430,24 +1546,48 @@
         ffn_key,
         ffn_value,
     )
-    out, grad_in, prev, init, vec, att, wout, wrec, key, value = outs
-    mine = lax.dynamic_slice_in_dim(vec, lax.axis_index("tok") * 32, 32, 1)
+    big = [outs[i] for i in (0, 1, 5, 6, 7, 8, 9)]
+    small = [outs[i] for i in (2, 3, 4)]
+    done = pl.pallas_call(
+        hand_over,
+        out_shape=[shape(x.shape, x.dtype) for x in big + small[:2]]
+        + [shape((n, 32), F32) for n in (1, 1, 5, 2, 2)],
+        in_specs=[vmem] * 10,
+        out_specs=[vmem] * 14,
+    )(*big, *small)
+    out, grad_in, att, wout, wrec, key, value, prev, init = done[:9]
+    decay, first, ratios, gains, biases = done[9:]
     return (
         out.reshape(2, SPAN, 1024),
         grad_in.reshape(2, SPAN, 1024),
         prev.reshape(2, 2, 128),
         init,
-        mine[0],
-        mine[1],
-        mine[2:7],
-        mine[7:9],
-        mine[9:11],
+        decay.reshape(32),
+        first.reshape(32),
+        ratios,
+        gains,
+        biases,
         att,
         wout,
         wrec,
         key,
         value,
     )
+
+
+def hand_over(*refs):
+    given, made = refs[:10], refs[10:24]
+    for old, new in zip(given[:9], made):
+        new[...] = old[...]
+    place = lax.axis_index("tok")
+    rows = given[9][...]
+    mine = jnp.zeros((16, 32), F32)
+    for k in range(8):
+        mine = mine + jnp.where(place == k, rows[:, 32 * k : 32 * k + 32], 0.0)
+    at = 0
+    for ref in made[9:14]:
+        ref[...] = mine[at : at + ref.shape[0], :]
+        at += ref.shape[0]
 
 
 VMEM_LIMIT = 62 * 2**20

time: 164 us -> 119 us (0.73)
  Pallas kernels: 148 us -> 118 us
  local copies, waits for them, and re-layouts: 14.9 us -> 0 us
    pallas_call x1, Pallas kernels: 148 us -> 115 us  [fused_call(): pl.pallas_call(fused, out_shape=out_shapes, in_specs=[vmem] * 9 + [anywhe...]
    unnamed x17 -> x0, local copies, waits for them, and re-layouts: 10.7 us -> none
    pallas_call x0 -> x1, Pallas kernels: none -> 3.17 us  [fused_call(): pl.pallas_call(hand_over, out_shape=[shape(x.shape, x.dtype) for x in big...]
    slice x2 -> x0, local copies, waits for them, and re-layouts: 2.79 us -> none  [the longest x1 1.45 us: fused_call(): mine[9:11]]
where the time goes in v2:
time: 119 us
  Pallas kernels  118 us (99%)
    pallas_call x1, Pallas kernels, fused_call(): pl.pallas_call(fused, out_shape=out_shapes, in_specs=[vmem] * 9 + [anywhe...  115 us
    pallas_call x1, Pallas kernels, fused_call(): pl.pallas_call(hand_over, out_shape=[shape(x.shape, x.dtype) for x in big...  3.17 us

profile of v2, /device:TPU:0, one launch (start us, length us, event | category | flops | bytes accessed | tf_op | source)
XLA Modules:
  0.0 119.1 jit_solution(8455126004206649679)
XLA Ops:
  0.7 115.2 %shard_map.245 = (bf16[128,1024]{1,0:T(8,128)(2,1)}, f32[128,1024]{1,0:T(8,128)}, f32[4,128]{1,0:T(4,128)}, f32[3,2,128]{2,1,0:T(2,128)}, f32[16,256]{1,0:T(8,12...) custom-call(bf16[128,1024]{1,0:T(8,128)(2,1)} %bitcast.9, ...), custom_call_target="tpu_custom_call" | custom-call | tf_op jit(solution)/shard_map/pallas_call | solution.py:1519
  115.8 3.2 %shard_map.246 = (bf16[128,1024]{1,0:T(8,128)(2,1)}, f32[128,1024]{1,0:T(8,128)}, f32[3,128,256]{2,1,0:T(8,128)}, f32[128,256]{1,0:T(8,128)}, f32[128,256]{1,0:T...) custom-call(bf16[128,1024]{1,0:T(8,128)(2,1)} %get-tuple-element.38., ...), custom_call_target="tpu_custom_call" | custom-call | tf_op jit(solution)/shard_map/pallas_call | solution.py:1551

commit v3 on v2

--- a/solution.py
+++ b/solution.py
@@ -520,8 +520,17 @@
     fn=((2, 72, 1024), F32),
     hs1=((2, 1, 1024), F32),
     hr1=((2, 1, 1024), F32),
-    xs=((5, 2 * ROWS, 1024), BF16),
-    gs=((5, 2 * ROWS, 1024), BF16),
+    xk=((2, ROWS, 1024), BF16),
+    xs=((3, 2 * ROWS, 1024), BF16),
+    gk=((2, ROWS, 1024), BF16),
+    gs=((3, 2 * ROWS, 1024), BF16),
+    fnb=((ROWS + 16, 1024), BF16),
+    nz=((3, ROWS + 16, 1024), BF16),
+    gz=((2, 4 * ROWS, 256), BF16),
+    kvp=((2, 4, 2, ROWS, 256), BF16),
+    kvr=((2, 4, ROWS, 256), BF16),
+    kvs=((2, 4, ROWS, 256), BF16),
+    kvl=((2, 3, ROWS, 256), BF16),
     kb=((ROWS, 1024), F32),
     vb=((ROWS, 1024), F32),
     sr=((ROWS, 1024), F32),
@@ -572,52 +581,58 @@
     fvz=((4, 512, 256), BF16),
     fvt=((4, 512, 256), BF16),
     arecv=((3, 3, ROWS, 1024), BF16),
-    zsend=((5, 4, ROWS, 256), BF16),
-    zrecv=((5, 4, ROWS, 256), BF16),
+    zsend=((3, 4, ROWS, 256), BF16),
+    zrecv=((3, 4, ROWS, 256), BF16),
     hs3=((2, 1, 1024), F32),
     hr3=((2, 1, 1024), F32),
     acc=((9, 8, 1024), F32),
-    gm=((ROWS, 1024), F32),
     vec=((16, 1024), F32),
     vz=((4, 16, 256), F32),
     pvb=((4, 8, 256), F32),
     vss=((8, 24, 256), F32),
     vt=((8, 24, 256), F32),
+    bs3=((3, 2, 1024), F32),
 )
 SEMS = 160
-INPUTS = (
-    "x",
-    "cot",
-    "prev",
-    "init",
-    "decay",
-    "first",
-    "ratio",
-    "gain",
-    "bias",
-    "h_att",
-    "h_out",
-    "h_rec",
-    "h_key",
-    "h_val",
+SMALL_IN = dict(
+    x=((ROWS, 1024), BF16),
+    cot=((ROWS, 1024), BF16),
+    prev=((2, 2, 1024), F32),
+    init=((3, 2, 1024), F32),
+    decay=((1, 1024), F32),
+    first=((1, 1024), F32),
+    ratio=((5, 1024), F32),
+    gain=((2, 1024), F32),
+    bias=((2, 1024), F32),
 )
-OUTPUTS = (
-    "o_out",
-    "o_in",
-    "o_prev",
-    "o_init",
-    "o_vec",
-    "o_att",
-    "o_wout",
-    "o_wrec",
-    "o_key",
-    "o_val",
+RESULTS = dict(
+    o_out=((ROWS, 1024), BF16),
+    o_in=((ROWS, 1024), F32),
+    o_prev=((4, 128), F32),
+    o_init=((3, 2, 128), F32),
+    o_vec=((16, 256), F32),
+    o_att=((3, 128, 256), F32),
+    o_wout=((128, 256), F32),
+    o_wrec=((128, 256), F32),
+    o_key=((256, 512), F32),
+    o_val=((512, 256), F32),
 )
+STAGED = {name: spec for name, spec in RESULTS.items() if name != "o_in"}
+WEIGHTS = ("h_att", "h_out", "h_rec", "h_key", "h_val")
+NAMES = (
+    tuple("h_" + name for name in SMALL_IN)
+    + WEIGHTS
+    + tuple("h_" + name for name in RESULTS)
+    + tuple(SCRATCH)
+    + tuple(SMALL_IN)
+    + tuple(STAGED)
+    + ("ss", "rs", "ls")
+)
 
 
 def fused(*refs):
-    names = INPUTS + OUTPUTS + tuple(SCRATCH) + ("ss", "rs", "ls")
-    r = types.SimpleNamespace(**dict(zip(names, refs)))
+    r = types.SimpleNamespace(**dict(zip(NAMES, refs)))
+    r.o_in, r.gm = r.kb, r.n2
     s = lax.axis_index("seg")
     t = lax.axis_index("tok")
     chip = t // 2
@@ -655,10 +670,18 @@
             copy.wait_recv()
             del unread[id(copy)]
 
+    barrier = pltpu.get_barrier_semaphore()
+    for x in range(1, 8):
+        pl.semaphore_signal(barrier, inc=1, device_id=(s, t ^ x), device_id_type=MESH)
+    for x in range(1, 4):
+        pl.semaphore_signal(barrier, inc=1, device_id=(s ^ x, t), device_id_type=MESH)
+
     loads = []
     lines = {}
+    names = tuple(SMALL_IN)
     for i, (src, dst) in enumerate(
-        [
+        [(getattr(r, "h_" + name), getattr(r, name)) for name in names]
+        + [
             (r.h_att, r.watt),
             (r.h_out, r.wout),
             (r.h_rec, r.wrec),
@@ -670,12 +693,17 @@
         copy.start()
         loads.append(copy)
 
-    barrier = pltpu.get_barrier_semaphore()
-    for x in range(1, 8):
-        pl.semaphore_signal(barrier, inc=1, device_id=(s, t ^ x), device_id_type=MESH)
-    for x in range(1, 4):
-        pl.semaphore_signal(barrier, inc=1, device_id=(s ^ x, t), device_id_type=MESH)
-
+    handed = []
+
+    def hand_out(name):
+        copy = pltpu.make_async_copy(
+            getattr(r, name), getattr(r, "h_" + name), r.ls.at[14 + len(handed)]
+        )
+        copy.start()
+        handed.append(copy)
+
+    for _ in names:
+        loads.pop(0).wait()
     swap = swap_matrix()
     r.xp[...] = dot_nn(swap, r.x[...]).astype(BF16)
     r.cg[0] = dot_nn(swap, r.cot[...]).astype(BF16)
@@ -727,9 +755,27 @@
             rows = pl.ds(pl.multiple_of(q * SPAN + i * 16, 16), 16)
             for m in range(3):
                 ratio = r.ratio[m : m + 1, :]
-                r.xs[m, rows, :] = (now * ratio + back * (1.0 - ratio)).astype(BF16)
+                mixed = (now * ratio + back * (1.0 - ratio)).astype(BF16)
+                if m < 2:
+                    r.xk[m, rows, :] = mixed
+                else:
+                    r.xs[0, rows, :] = mixed
 
     each(4, mix_one)
+
+    def narrow(i):
+        for q in range(2):
+            at = pl.ds(pl.multiple_of(q * SPAN + i * 16, 16), 16)
+            r.fnb[at, :] = r.fn[q, pl.ds(pl.multiple_of(8 + i * 16, 8), 16), :].astype(BF16)
+
+    each(4, narrow)
+    heads = jnp.where(row16 == 0, r.fn[0, 0:1, :], 0.0)
+    heads = jnp.where(row16 == 1, r.fn[1, 0:1, :], heads)
+    r.fnb[pl.ds(ROWS, 16), :] = heads.astype(BF16)
+    nz_slot = slots(3)
+    nz_in = [
+        send(r.fnb, r.nz.at[z - 1], nz_slot + z - 1, s ^ z, t) for z in range(1, 4)
+    ]
     loads.pop(0).wait()
 
     def product(get, weights, put, transposed=False):
@@ -750,8 +796,8 @@
     def keep_gate(part):
         r.sr[...] = jax.nn.sigmoid(part)
 
-    product(lambda: r.xs[0, own, :], r.watt.at[0], keep(r.kb))
-    product(lambda: r.xs[1, own, :], r.watt.at[1], keep(r.vb))
+    product(lambda: r.xk[0], r.watt.at[0], keep(r.kb))
+    product(lambda: r.xk[1], r.watt.at[1], keep(r.vb))
 
     fade = -jnp.exp(r.decay[...])
     r.vec[15:16, :] = fade
@@ -784,7 +830,7 @@
     state_in = [
         send(r.ws, r.wr.at[x], state_slot + x, s, t ^ x) for x in range(1, 8)
     ]
-    product(lambda: r.xs[2, own, :], r.watt.at[2], keep_gate)
+    product(lambda: r.xs[0, own, :], r.watt.at[2], keep_gate)
     while loads:
         loads.pop().wait()
     near_x = [slots(1) for _ in range(5)]
@@ -792,10 +838,15 @@
     far = pl.ds(ROWS, ROWS)
 
     def share(ref, m, slot):
-        return send(ref.at[m, own, :], ref.at[m, far, :], slot, s, near)
-
-    x_in = [share(r.xs, m, near_x[m]) for m in range(3)]
+        return send(ref.at[m - 2, own, :], ref.at[m - 2, far, :], slot, s, near)
+
+    x_in = {2: share(r.xs, 2, near_x[2])}
     arrive(*state_in)
+    arrive(*cot_in)
+    cot_in = [
+        send(r.cg.at[2, upper, :], r.cg.at[3, upper, :], cot_slot + 2, s, side_x),
+        send(r.cg.at[1, lower, :], r.cg.at[3, lower, :], cot_slot + 3, s, side_y),
+    ]
 
     def far_state(ref, base_p, sel, steps):
         peak = base_p
@@ -850,23 +901,18 @@
                 a, b, p = join(a, b, p + w, vv, 1.0, kk)
 
     each(2, full_scan)
-    arrive(*cot_in)
-    cot_in = [
-        send(r.cg.at[2, upper, :], r.cg.at[3, upper, :], cot_slot + 2, s, side_x),
-        send(r.cg.at[1, lower, :], r.cg.at[3, lower, :], cot_slot + 3, s, side_y),
-    ]
 
     def weigh(i):
         rows = tile_of(i, 16)
-        r.xs[3, rows, :] = (r.sr[rows, :] * r.ou[rows, :]).astype(BF16)
+        r.xs[1, rows, :] = (r.sr[rows, :] * r.ou[rows, :]).astype(BF16)
 
     each(8, weigh)
-    x_in.append(share(r.xs, 3, near_x[3]))
+    x_in[3] = share(r.xs, 3, near_x[3])
 
     def keep_middle(part):
         r.mid[...] = r.xp[...].astype(F32) + part
 
-    product(lambda: r.xs[3, own, :], r.wout, keep_middle)
+    product(lambda: r.xs[1, own, :], r.wout, keep_middle)
 
     def second_norm(i):
         rows = tile_of(i, 16)
@@ -893,7 +939,7 @@
     bt_slot = slots(4)
     bt_home = slots(4)
 
-    def block(js):
+    def block(js, between=None):
         count = len(js)
         rows = pl.ds(js[0] * ROWS, count * ROWS)
         top_rows = pl.ds(0, count * ROWS)
@@ -926,7 +972,7 @@
 
         each(4, mix_two)
         if js[0] == 0:
-            r.xs[4, own, :] = r.mg[own, :]
+            r.xs[2, own, :] = r.mg[own, :]
 
         def put_gate(part):
             sg = jax.nn.sigmoid(part)
@@ -944,6 +990,8 @@
             r.hid[rows, :] = (relu * relu).astype(BF16)
 
         product(lambda: r.mk[rows, :], r.wkey, put_hidden)
+        if between is not None:
+            between()
 
         def put_hidden_grad(part):
             r.ghp[rows, :] = (part * 2.0 * r.rl[top_rows, :]).astype(BF16)
@@ -1003,13 +1051,110 @@
             if j:
                 gs_in.append(send(r.gss.at[j], r.gsr.at[j - 1], gs_slot + j, s, b))
 
+    def key_grad(half, ref):
+        def step(n):
+            rows = tile_of(n, 512)
+            ref[rows, :] = dot_tn(
+                r.mk[:, rows], r.ghp[:, pl.ds(half * HALF, HALF)]
+            ).astype(BF16)
+
+        each(2, step)
+
+    def value_grad(half, ref):
+        def step(n):
+            part = dot_tn(r.hid[:, pl.ds(half * HALF, HALF)], r.gv[:, tile_of(n, 512)])
+            ref[2 * n] = part[:, 0:256].astype(BF16)
+            ref[2 * n + 1] = part[:, 256:512].astype(BF16)
+
+        each(2, step)
+
+    middle_seg = (s == 1) | (s == 2)
+    end_seg = (s == 0) | (s == 3)
+
+    class LineSum:
+        def __init__(self, part, landing):
+            self.part, self.landing = part, landing
+            self.slot = slots(4)
+            lines[id(self)] = self
+            self.pumped = False
+
+        def copy(self, chunk, place, seg):
+            return wire(
+                self.part(chunk), self.landing(place), self.slot + place, seg, t
+            )
+
+        def first(self):
+            @pl.when(end_seg)
+            def _():
+                self.copy(s ^ 3, 3, s ^ 1).start()
+
+            self.copy(s ^ 1, 0, s ^ 1).start()
+
+            @pl.when(end_seg)
+            def _():
+                self.copy(s ^ 2, 1, s ^ 2).start()
+
+            @pl.when(middle_seg)
+            def _():
+                self.copy(s ^ 3, 2, s ^ 3).start()
+
+        def pump(self):
+            self.pumped = True
+
+            @pl.when(middle_seg)
+            def _():
+                self.copy(s ^ 3, 3, s ^ 1).wait_recv()
+                ref, more = self.part(s ^ 2), self.landing(3)
+                ref[...] = (ref[...].astype(F32) + more[...].astype(F32)).astype(BF16)
+                self.copy(s ^ 2, 1, s ^ 2).start()
+
+        def finish(self):
+            del lines[id(self)]
+            self.copy(s ^ 1, 0, s ^ 1).wait()
+            self.copy(s ^ 2, 1, s ^ 2).wait()
+
+            @pl.when(middle_seg)
+            def _():
+                self.copy(s ^ 3, 2, s ^ 3).wait()
+
+            @pl.when(end_seg)
+            def _():
+                self.copy(s ^ 3, 3, s ^ 1).wait_send()
+
+        def total(self, rows):
+            out = self.part(s)[rows, :].astype(F32)
+            out = out + self.landing(0)[rows, :].astype(F32)
+            out = out + self.landing(1)[rows, :].astype(F32)
+            more = self.landing(2)[rows, :].astype(F32)
+            return out + jnp.where(middle_seg, more, 0.0)
+
+    value_lines = []
+
+    def value_first():
+        value_grad(1, r.fvs)
+        fv_in = send(r.fvs, r.fvr, slots(1), s, near)
+        value_grad(0, r.fvz)
+        arrive(fv_in)
+
+        def add_value(n):
+            for i in range(4):
+                rows = pl.ds(i * 128, 128)
+                r.fvz[n, rows, :] = (
+                    r.fvz[n, rows, :].astype(F32) + r.fvr[n, rows, :].astype(F32)
+                ).astype(BF16)
+
+        each(4, add_value)
+        value_lines.append(LineSum(lambda n: r.fvz.at[n], lambda n: r.fvt.at[n]))
+        value_lines[0].first()
+
     gs_in = []
     block((0,))
     sn_in.append(send(r.sng.at[0], r.sng.at[3], sn_slot + 3, s, across))
     arrive(*sn_in[:2])
     block((1, 2))
     arrive(*cot_in, *sn_in[2:])
-    block((3,))
+    block((3,), value_first)
+    value_line = value_lines[0]
     bt_in = [
         wire(r.bts.at[i], r.btr.at[i], bt_slot + i, s, near, bt_home + i) for i in range(4)
     ]
@@ -1051,102 +1196,10 @@
     )
     value_sum.first()
     value_sum.second()
-    x_in.append(share(r.xs, 4, near_x[4]))
-
-    def key_grad(half, ref):
-        def step(n):
-            rows = tile_of(n, 512)
-            ref[rows, :] = dot_tn(
-                r.mk[:, rows], r.ghp[:, pl.ds(half * HALF, HALF)]
-            ).astype(BF16)
-
-        each(2, step)
-
-    def value_grad(half, ref):
-        def step(n):
-            part = dot_tn(r.hid[:, pl.ds(half * HALF, HALF)], r.gv[:, tile_of(n, 512)])
-            ref[2 * n] = part[:, 0:256].astype(BF16)
-            ref[2 * n + 1] = part[:, 256:512].astype(BF16)
-
-        each(2, step)
-
-    middle_seg = (s == 1) | (s == 2)
-    end_seg = (s == 0) | (s == 3)
-
-    class LineSum:
-        def __init__(self, part, landing):
-            self.part, self.landing = part, landing
-            self.slot = slots(4)
-            lines[id(self)] = self
-            self.pumped = False
-
-        def copy(self, chunk, place, seg):
-            return wire(
-                self.part(chunk), self.landing(place), self.slot + place, seg, t
-            )
-
-        def first(self):
-            @pl.when(end_seg)
-            def _():
-                self.copy(s ^ 3, 3, s ^ 1).start()
-
-            self.copy(s ^ 1, 0, s ^ 1).start()
-
-            @pl.when(end_seg)
-            def _():
-                self.copy(s ^ 2, 1, s ^ 2).start()
-
-            @pl.when(middle_seg)
-            def _():
-                self.copy(s ^ 3, 2, s ^ 3).start()
-
-        def pump(self):
-            self.pumped = True
-
-            @pl.when(middle_seg)
-            def _():
-                self.copy(s ^ 3, 3, s ^ 1).wait_recv()
-                ref, more = self.part(s ^ 2), self.landing(3)
-                ref[...] = (ref[...].astype(F32) + more[...].astype(F32)).astype(BF16)
-                self.copy(s ^ 2, 1, s ^ 2).start()
-
-        def finish(self):
-            del lines[id(self)]
-            self.copy(s ^ 1, 0, s ^ 1).wait()
-            self.copy(s ^ 2, 1, s ^ 2).wait()
-
-            @pl.when(middle_seg)
-            def _():
-                self.copy(s ^ 3, 2, s ^ 3).wait()
-
-            @pl.when(end_seg)
-            def _():
-                self.copy(s ^ 3, 3, s ^ 1).wait_send()
-
-        def total(self, rows):
-            out = self.part(s)[rows, :].astype(F32)
-            out = out + self.landing(0)[rows, :].astype(F32)
-            out = out + self.landing(1)[rows, :].astype(F32)
-            more = self.landing(2)[rows, :].astype(F32)
-            return out + jnp.where(middle_seg, more, 0.0)
-
-    value_grad(1, r.fvs)
-    fv_in = send(r.fvs, r.fvr, slots(1), s, near)
+    x_in[4] = share(r.xs, 4, near_x[4])
+
     key_grad(1, r.fks)
     fk_in = send(r.fks, r.fkr, slots(1), s, near)
-    value_grad(0, r.fvz)
-    arrive(fv_in)
-
-    def add_value(n):
-        for i in range(4):
-            rows = pl.ds(i * 128, 128)
-            r.fvz[n, rows, :] = (
-                r.fvz[n, rows, :].astype(F32) + r.fvr[n, rows, :].astype(F32)
-            ).astype(BF16)
-
-    each(4, add_value)
-    value_line = LineSum(lambda n: r.fvz.at[n], lambda n: r.fvt.at[n])
-    value_line.first()
     key_grad(0, r.fkz)
     arrive(fk_in)
 
@@ -1158,6 +1211,36 @@
     key_line = LineSum(lambda n: r.fkz.at[tile_of(n, 256), :], lambda n: r.fkt.at[n])
     key_line.first()
     value_sum.pump()
+
+    spread = (r.wval, r.mk)
+    spread_base = (4, 0)
+    arrive(*nz_in)
+    for z in range(4):
+        if z:
+            for q in range(2):
+                for i in range(4):
+                    r.sf[q, pl.ds(8 + 16 * i, 16), :] = r.nz[
+                        z - 1, pl.ds(q * SPAN + 16 * i, 16), :
+                    ].astype(F32)
+                head = r.nz[z - 1, pl.ds(ROWS, 16), :].astype(F32)[q : q + 1, :]
+                r.sf[q, 0:8, :] = jnp.where(
+                    row8 == 0, head, pltpu.roll(r.sf[q, 64:72, :], 1, 0)
+                )
+
+        def mix_far(i):
+            for q in range(2):
+                at = pl.multiple_of(q * SPAN + i * 16, 16)
+                for m in range(2):
+                    to = pl.ds(pl.multiple_of((spread_base[m] + z) * ROWS + at, 16), 16)
+                    if z:
+                        now = r.sf[q, pl.ds(pl.multiple_of(8 + i * 16, 8), 16), :]
+                        back = r.sf[q, tile_of(i, 16), :]
+                        ratio = r.ratio[m : m + 1, :]
+                        spread[m][to, :] = (now * ratio + back * (1.0 - ratio)).astype(BF16)
+                    else:
+                        spread[m][to, :] = r.xk[m, pl.ds(at, 16), :]
+
+        each(4, mix_far)
 
     arrive(*bt_in, *gs_in)
     for q in range(2):
@@ -1177,7 +1260,7 @@
             dz = unnormalise(grad, normed, r.r2[rows, 0:1], r.gain[1:2, :])
             total = r.cg[0, rows, :].astype(F32) + dz
             r.gm[rows, :] = total
-            r.gs[3, rows, :] = total.astype(BF16)
+            r.gs[1, rows, :] = total.astype(BF16)
 
     each(4, back_two)
     g_in = {3: share(r.gs, 3, near_g[3])}
@@ -1185,10 +1268,10 @@
     def put_branch(part):
         sr = r.sr[...]
         grad = part * sr
-        r.gs[2, own, :] = (grad * r.ou[...] * (1.0 - sr)).astype(BF16)
+        r.gs[0, own, :] = (grad * r.ou[...] * (1.0 - sr)).astype(BF16)
         r.rd[...] = grad * r.rd[...]
 
-    product(lambda: r.gs[3, own, :], r.wout, put_branch, transposed=True)
+    product(lambda: r.gs[1, own, :], r.wout, put_branch, transposed=True)
     g_in[2] = share(r.gs, 2, near_g[2])
 
     def back_local(n):
@@ -1223,24 +1306,21 @@
         value = r.pvs[0].astype(F32) + r.pvr[0].astype(F32) + r.pvr[1].astype(F32)
         out = r.mid[...] + sg * value
         top = r.cg[0].astype(F32)
-        r.gs[4, own, :] = (top * value * sg * (1.0 - sg)).astype(BF16)
+        r.gs[2, own, :] = (top * value * sg * (1.0 - sg)).astype(BF16)
         r.o_out[...] = dot_nn(swap, out.astype(BF16)).astype(BF16)
 
-    product(lambda: r.xs[4, own, :], r.wrec, put_out)
+    product(lambda: r.xs[2, own, :], r.wrec, put_out)
+    hand_out("o_out")
     g_in[4] = share(r.gs, 4, near_g[4])
 
-    a_home = (r.wval, r.mk, r.wval, r.wkey, r.wkey)
+    a_home = (None, None, r.wval, r.wkey, r.wkey)
     a_base = (4, 0, 0, 0, 4)
 
     def a_rows(m, j):
         return tile_of(a_base[m] + j, ROWS)
 
-    land_home = (r.hid, r.ghp, r.arecv.at[0], r.arecv.at[1], r.arecv.at[2])
-
     def a_landing(m, n, half):
-        if m < 2:
-            return land_home[m].at[pl.ds(n * ROWS + half.start, SPAN), :]
-        return land_home[m].at[n, half, :]
+        return r.arecv.at[m - 2, n, half, :]
 
     def a_piece(m, j, half):
         return a_home[m].at[
@@ -1255,8 +1335,8 @@
         plane_sums[m] = PlaneSum(functools.partial(a_piece, m), functools.partial(a_landing, m))
 
         def pair(j, j2):
-            cols = [r.xs[m, :, tile_of(t ^ (2 * i), 128)] for i in (j, j2)]
-            both = dot_tn(jnp.concatenate(cols, axis=1), r.gs[m]).astype(BF16)
+            cols = [r.xs[m - 2, :, tile_of(t ^ (2 * i), 128)] for i in (j, j2)]
+            both = dot_tn(jnp.concatenate(cols, axis=1), r.gs[m - 2]).astype(BF16)
             a_home[m][a_rows(m, j), :] = both[0:ROWS, :]
             a_home[m][a_rows(m, j2), :] = both[ROWS : 2 * ROWS, :]
 
@@ -1292,6 +1372,7 @@
     r.bs3[1] = b
     r.bs3[2] = a * r.init[0] + b * r.init[1]
     r.o_init[...] = r.bs3[:, :, tile_of(t, 128)]
+    hand_out("o_init")
 
     def back_full(n):
         cols = tile_of(n, HALF)
@@ -1332,19 +1413,38 @@
 
     def round_grads(i):
         rows = tile_of(i, 16)
-        r.gs[0, rows, :] = r.kb[rows, :].astype(BF16)
-        r.gs[1, rows, :] = r.vb[rows, :].astype(BF16)
+        r.gk[0, rows, :] = r.kb[rows, :].astype(BF16)
+        r.gk[1, rows, :] = r.vb[rows, :].astype(BF16)
 
     each(8, round_grads)
-    g_in[0] = share(r.gs, 0, near_g[0])
-    g_in[1] = share(r.gs, 1, near_g[1])
+    gz_slot = slots(6)
+    gz_in = [
+        [
+            send(
+                r.gk.at[m, :, tile_of(s ^ z, 256)],
+                r.gz.at[m, pl.ds(z * ROWS, ROWS), :],
+                gz_slot + 3 * m + z - 1,
+                s ^ z,
+                t,
+            )
+            for z in range(1, 4)
+        ]
+        for m in range(2)
+    ]
+    for m in range(2):
+        r.gz[m, own, :] = r.gk[m, :, tile_of(s, 256)]
 
     for m, ref in enumerate((r.ab, r.rl, r.cc)):
 
         def put_mixed(part):
             ref[own, :] = part
 
-        product(lambda: r.gs[m, own, :], r.watt.at[m], put_mixed, transposed=True)
+        product(
+            lambda: r.gk[m] if m < 2 else r.gs[0, own, :],
+            r.watt.at[m],
+            put_mixed,
+            transposed=True,
+        )
 
     def mixed_first(i):
         for q in range(2):
@@ -1363,13 +1463,67 @@
             r.bb[q, tile_of(i, 16), :] = ahead
 
     each(4, mixed_first)
+    def gather_plane(m):
+        plane_sums[m].finish()
+
+        def step(n):
+            span = tile_of(n, 256)
+            total = a_home[m][a_rows(m, 0), span].astype(F32)
+            for k in range(2):
+                total = total + r.arecv[m - 2, k, :, span].astype(F32)
+            r.zsend[m - 2, n] = total.astype(BF16)
+
+        each(4, step)
+        line_sums[m] = LineSum(lambda n: r.zsend.at[m - 2, n], lambda n: r.zrecv.at[m - 2, n])
+        line_sums[m].first()
+
+    kv_slot = slots(8)
+    kv_near = {}
+    kv_in = {}
+
+    def kv_start(m):
+        arrive(*gz_in[m])
+
+        def step(i):
+            part = dot_tn(
+                spread[m][pl.ds(spread_base[m] * ROWS, 4 * ROWS), :], r.gz[m]
+            ).astype(BF16)
+            for c in range(4):
+                for k in range(2):
+                    at = (2 * c + k) * ROWS
+                    r.kvp[m, c, k] = part[at : at + ROWS, :]
+
+        each(1, step)
+        kv_near[m] = send(r.kvp.at[m, :, lax.rem(near, 2)], r.kvr.at[m], kv_slot + 4 * m, s, near)
+
+    def kv_next(m):
+        arrive(kv_near[m])
+        for j in range(4):
+            c = chip ^ j
+            r.kvs[m, j] = (
+                r.kvp[m, c, lax.rem(t, 2)].astype(F32) + r.kvr[m, c].astype(F32)
+            ).astype(BF16)
+        kv_in[m] = [
+            send(r.kvs.at[m, j], r.kvl.at[m, j - 1], kv_slot + 4 * m + j, s, t ^ (2 * j))
+            for j in range(1, 4)
+        ]
+
+    def kv_finish(m):
+        arrive(*kv_in[m])
+        total = r.kvs[m, 0].astype(F32)
+        for j in range(3):
+            total = total + r.kvl[m, j].astype(F32)
+        r.o_att[m] = total
+
     for q in range(2):
         r.hs3[q] = r.bb[q, 0:1, :]
     halo3 = send(r.hs3, r.hr3, slots(1), s, prior)
-    weight_grad(0)
-    weight_grad(1)
     plane_sums[4].pump()
+    gather_plane(3)
     key_line.pump()
+    kv_start(0)
+    gather_plane(2)
+    kv_start(1)
     arrive(halo3)
     for q in range(2):
         last = jnp.where(t < 7, r.hr3[q], 0.0)
@@ -1401,6 +1555,7 @@
         r.o_in[...] = swap_exact(swap, r.gm[...])
 
     each(1, put_in)
+    hand_out("o_in")
     r.pvb[...] = jnp.zeros_like(r.pvb)
     for q in range(4):
         span = pl.ds(q * 256, 256)
@@ -1408,29 +1563,9 @@
             r.pvb[q, i : i + 1, :] = r.hr3[i, :, span]
             r.pvb[q, 2 + i : 3 + i, :] = r.bsum[i, :, span]
 
-    def gather_plane(m):
-        plane_sums[m].finish()
-
-        def step(n):
-            span = tile_of(n, 256)
-            total = a_home[m][a_rows(m, 0), span].astype(F32)
-            for k in range(2):
-                if m < 2:
-                    more = land_home[m][pl.ds(k * ROWS, ROWS), span]
-                else:
-                    more = land_home[m][k, :, span]
-                total = total + more.astype(F32)
-            r.zsend[m, n] = total.astype(BF16)
-
-        each(4, step)
-        line_sums[m] = LineSum(lambda n: r.zsend.at[m, n], lambda n: r.zrecv.at[m, n])
-        line_sums[m].first()
-
-    gather_plane(3)
-    plane_sums[0].pump()
-    gather_plane(2)
-    plane_sums[1].pump()
+    kv_next(0)
     line_sums[3].pump()
+    kv_next(1)
     gather_plane(4)
     arrive(*vz_in)
     mine = r.vec[:, tile_of(s, 256)] + r.vz[1] + (r.vz[2] + r.vz[3])
@@ -1441,18 +1576,40 @@
     vt_slot = slots(8)
     vt_in = [send(r.vss.at[x], r.vt.at[x], vt_slot + x, s, t ^ x) for x in range(1, 8)]
     line_sums[2].pump()
-    gather_plane(0)
     line_sums[4].pump()
-    gather_plane(1)
-    line_sums[0].pump()
-    line_sums[1].pump()
+    kv_finish(0)
+    kv_finish(1)
     arrive(*vt_in)
     total = r.vt[0, 0:16, :]
     for x in range(1, 8):
         total = total + r.vt[x, 0:16, :]
     r.o_vec[...] = total
     r.o_prev[...] = r.vt[7 ^ t, 16:20, tile_of(t % 2, 128)]
+    hand_out("o_vec")
+    hand_out("o_prev")
+    def square_out(m):
+        line_sums[m].finish()
+        total = line_sums[m].total(pl.ds(0, ROWS))
+        if m == 2:
+            r.o_att[2] = total
+            hand_out("o_att")
+        elif m == 3:
+            r.o_wout[...] = total
+            hand_out("o_wout")
+        else:
+            r.o_wrec[...] = total
+            hand_out("o_wrec")
+
     value_line.finish()
+
+    def out_value(i):
+        rows = tile_of(i, 128)
+        r.o_val[rows, :] = value_line.total(rows)
+
+    each(4, out_value)
+    hand_out("o_val")
+    square_out(3)
+    square_out(2)
     key_line.finish()
 
     def out_key(i):
@@ -1460,28 +1617,15 @@
         r.o_key[rows, :] = key_line.total(rows)
 
     each(4, out_key)
-
-    def out_value(i):
-        rows = tile_of(i, 128)
-        r.o_val[rows, :] = value_line.total(rows)
-
-    each(4, out_value)
-    for m in (3, 2, 4, 0, 1):
-        line_sums[m].finish()
-        total = line_sums[m].total(pl.ds(0, ROWS))
-        if m < 3:
-            r.o_att[m] = total
-        elif m == 3:
-            r.o_wout[...] = total
-        else:
-            r.o_wrec[...] = total
+    hand_out("o_key")
+    square_out(4)
 
     for copy in sent:
         copy.wait_send()
+    for copy in handed:
+        copy.wait()
+    assert len(handed) == len(RESULTS)
     assert not unread and not lines and taken[0] <= SEMS
-
-
-SCRATCH["bs3"] = ((3, 2, 1024), F32)
 
 
 def fused_call(args):
@@ -1504,28 +1648,21 @@
     vmem = pl.BlockSpec(memory_space=pltpu.VMEM)
     anywhere = pl.BlockSpec(memory_space=pl.ANY)
     shape = jax.ShapeDtypeStruct
-    out_shapes = [
-        shape((ROWS, 1024), BF16),
-        shape((ROWS, 1024), F32),
-        shape((4, 128), F32),
-        shape((3, 2, 128), F32),
-        shape((16, 256), F32),
-        shape((3, 128, 256), F32),
-        shape((128, 256), F32),
-        shape((128, 256), F32),
-        shape((256, 512), F32),
-        shape((512, 256), F32),
-    ]
+    out_shapes = [shape(dims, kind) for dims, kind in RESULTS.values()]
     outs = pl.pallas_call(
         fused,
         out_shape=out_shapes,
-        in_specs=[vmem] * 9 + [anywhere] * 5,
-        out_specs=[vmem] * 10,
-        scratch_shapes=[pltpu.VMEM(dims, kind) for dims, kind in SCRATCH.values()]
+        in_specs=[anywhere] * 14,
+        out_specs=[anywhere] * 10,
+        scratch_shapes=[
+            pltpu.VMEM(dims, kind)
+            for group in (SCRATCH, SMALL_IN, STAGED)
+            for dims, kind in group.values()
+        ]
         + [
             pltpu.SemaphoreType.DMA((SEMS,)),
             pltpu.SemaphoreType.DMA((SEMS,)),
-            pltpu.SemaphoreType.DMA((5,)),
+            pltpu.SemaphoreType.DMA((24,)),
         ],
         compiler_params=pltpu.CompilerParams(
             collective_id=0, has_side_effects=True, vmem_limit_bytes=VMEM_LIMIT

time: 119 us -> 113 us (0.950)
  Pallas kernels: 118 us -> 112 us
    pallas_call x1, Pallas kernels: 115 us -> 109 us  [fused_call(): pl.pallas_call(fused, out_shape=out_shapes, in_specs=[anywhere] * 14, out...]
where the time goes in v3:
time: 113 us
  Pallas kernels  112 us (99%)
    pallas_call x1, Pallas kernels, fused_call(): pl.pallas_call(fused, out_shape=out_shapes, in_specs=[anywhere] * 14, out...  109 us
    pallas_call x1, Pallas kernels, fused_call(): pl.pallas_call(hand_over, out_shape=[shape(x.shape, x.dtype) for x in big...  3.17 us

profile of v3, /device:TPU:0, one launch (start us, length us, event | category | flops | bytes accessed | tf_op | source)
XLA Modules:
  0.0 113.2 jit_solution(17532044846588443152)
XLA Ops:
  0.7 109.2 %shard_map.245 = (bf16[128,1024]{1,0:T(8,128)(2,1)}, f32[128,1024]{1,0:T(8,128)}, f32[4,128]{1,0:T(4,128)}, f32[3,2,128]{2,1,0:T(2,128)}, f32[16,256]{1,0:T(8,12...) custom-call(bf16[128,1024]{1,0:T(8,128)(2,1)} %bitcast.9, ...), custom_call_target="tpu_custom_call" | custom-call | tf_op jit(solution)/shard_map/pallas_call | solution.py:1652
  109.9 3.2 %shard_map.246 = (bf16[128,1024]{1,0:T(8,128)(2,1)}, f32[128,1024]{1,0:T(8,128)}, f32[3,128,256]{2,1,0:T(8,128)}, f32[128,256]{1,0:T(8,128)}, f32[128,256]{1,0:T...) custom-call(bf16[128,1024]{1,0:T(8,128)(2,1)} %get-tuple-element.38., ...), custom_call_target="tpu_custom_call" | custom-call | tf_op jit(solution)/shard_map/pallas_call | solution.py:1688

commit v4 on v3

--- a/solution.py
+++ b/solution.py
@@ -560,8 +560,9 @@
     gv=((4 * ROWS, 1024), BF16),
     hid=((4 * ROWS, 1024), BF16),
     ghp=((4 * ROWS, 1024), BF16),
-    rl=((2 * ROWS, 1024), F32),
-    cc=((2 * ROWS, 1024), F32),
+    rl=((4 * ROWS, 1024), BF16),
+    cc=((4 * ROWS, 1024), BF16),
+    gb=((2 * ROWS, 1024), F32),
     gg=((2 * ROWS, 1024), BF16),
     ab=((2 * ROWS, 1024), F32),
     bb=((4, 72, 1024), F32),
@@ -617,14 +618,15 @@
     o_key=((256, 512), F32),
     o_val=((512, 256), F32),
 )
-STAGED = {name: spec for name, spec in RESULTS.items() if name != "o_in"}
+HELD = {name: spec for name, spec in SMALL_IN.items() if name != "cot"}
+STAGED = {name: spec for name, spec in RESULTS.items() if name not in ("o_in", "o_out")}
 WEIGHTS = ("h_att", "h_out", "h_rec", "h_key", "h_val")
 NAMES = (
     tuple("h_" + name for name in SMALL_IN)
     + WEIGHTS
     + tuple("h_" + name for name in RESULTS)
     + tuple(SCRATCH)
-    + tuple(SMALL_IN)
+    + tuple(HELD)
     + tuple(STAGED)
     + ("ss", "rs", "ls")
 )
@@ -632,7 +634,8 @@
 
 def fused(*refs):
     r = types.SimpleNamespace(**dict(zip(NAMES, refs)))
-    r.o_in, r.gm = r.kb, r.n2
+    r.o_in, r.gm, r.o_out = r.kb, r.n2, r.x
+    r.cot = r.gk.at[0]
     s = lax.axis_index("seg")
     t = lax.axis_index("tok")
     chip = t // 2
@@ -929,22 +932,29 @@
     halo2 = [
         send(r.hs2, r.hr2.at[i], halo_slot + i, s, t ^ (2 * i + 1)) for i in range(4)
     ]
-    sn_slot = slots(4)
-    sn_in = [
-        send(r.sng.at[0], r.sng.at[j], sn_slot + j, s, t ^ (2 * j)) for j in range(1, 3)
-    ]
+    sn_slot = slots(6)
+
+    def pass_on(n, j, place, half, tok):
+        return send(
+            r.sng.at[j, half, :], r.sng.at[place, half, :], sn_slot + n, s, tok
+        )
+
+    sn_early = [pass_on(0, 0, 1, lower, side_x), pass_on(1, 0, 2, upper, side_y)]
+    sn_in = [pass_on(2, 0, 1, upper, side_x), pass_on(3, 0, 2, lower, side_y)]
     arrive(key_in, val_in, *halo2)
     r.acc[...] = jnp.zeros_like(r.acc)
     gs_slot = slots(4)
     bt_slot = slots(4)
     bt_home = slots(4)
 
-    def block(js, between=None):
-        count = len(js)
-        rows = pl.ds(js[0] * ROWS, count * ROWS)
-        top_rows = pl.ds(0, count * ROWS)
-        groups = [(n, j, q, 2 * n + q) for n, j in enumerate(js) for q in range(2)]
-        for n, j, q, g in groups:
+    def span_of(js):
+        return pl.ds(js[0] * ROWS, len(js) * ROWS)
+
+    def groups_of(js):
+        return [(n, j, q, 2 * n + q) for n, j in enumerate(js) for q in range(2)]
+
+    def widen(js):
+        for n, j, q, g in groups_of(js):
             b = t ^ (2 * j)
             source = (((b + 7) % 8) ^ t) // 2
             for i in range(4):
@@ -956,8 +966,14 @@
                 row8 == 0, head, pltpu.roll(r.sf[g, 64:72, :], 1, 0)
             )
 
+    def block_in(js):
+        count = len(js)
+        rows = span_of(js)
+        top_rows = pl.ds(0, count * ROWS)
+        widen(js)
+
         def mix_two(i):
-            for n, j, q, g in groups:
+            for n, j, q, g in groups_of(js):
                 now = r.sf[g, pl.ds(pl.multiple_of(8 + i * 16, 8), 16), :]
                 back = r.sf[g, tile_of(i, 16), :]
                 at = pl.multiple_of(i * 16, 16)
@@ -980,28 +996,31 @@
                 here = sg[n * ROWS : (n + 1) * ROWS, :]
                 top = r.cg[j].astype(F32) * here
                 r.gv[pl.ds(j * ROWS, ROWS), :] = top.astype(BF16)
-                r.cc[pl.ds(n * ROWS, ROWS), :] = top * (1.0 - here)
+                r.cc[pl.ds(j * ROWS, ROWS), :] = (top * (1.0 - here)).astype(BF16)
 
         product(lambda: r.mg[top_rows, :], r.wrec, put_gate)
 
         def put_hidden(part):
             relu = jnp.maximum(part, 0.0)
-            r.rl[top_rows, :] = relu
+            r.rl[rows, :] = relu.astype(BF16)
             r.hid[rows, :] = (relu * relu).astype(BF16)
 
         product(lambda: r.mk[rows, :], r.wkey, put_hidden)
-        if between is not None:
-            between()
+
+    def block_out(js):
+        rows = span_of(js)
+        top_rows = pl.ds(0, len(js) * ROWS)
+        widen(js)
 
         def put_hidden_grad(part):
-            r.ghp[rows, :] = (part * 2.0 * r.rl[top_rows, :]).astype(BF16)
+            r.ghp[rows, :] = (part * 2.0 * r.rl[rows, :].astype(F32)).astype(BF16)
 
         product(lambda: r.gv[rows, :], r.wval, put_hidden_grad, transposed=True)
 
         def put_value(part):
             for n, j in enumerate(js):
                 r.pvs[j] = part[n * ROWS : (n + 1) * ROWS, :].astype(BF16)
-            r.gg[top_rows, :] = (part * r.cc[top_rows, :]).astype(BF16)
+            r.gg[top_rows, :] = (part * r.cc[rows, :].astype(F32)).astype(BF16)
 
         product(lambda: r.hid[rows, :], r.wval, put_value)
 
@@ -1009,7 +1028,7 @@
             r.ab[top_rows, :] = part
 
         def put_gate_back(part):
-            r.rl[top_rows, :] = part
+            r.gb[top_rows, :] = part
 
         product(lambda: r.ghp[rows, :], r.wkey, put_key_back, transposed=True)
         product(lambda: r.gg[top_rows, :], r.wrec, put_gate_back, transposed=True)
@@ -1017,31 +1036,31 @@
         def mixed_back(i):
             r3 = r.ratio[3:4, :]
             r4 = r.ratio[4:5, :]
-            for n, j, q, g in groups:
+            for n, j, q, g in groups_of(js):
                 now = r.sf[g, pl.ds(pl.multiple_of(8 + i * 16, 8), 16), :]
                 step = now - r.sf[g, tile_of(i, 16), :]
                 at = pl.ds(pl.multiple_of(g * SPAN + i * 16, 16), 16)
                 gk = r.ab[at, :]
-                gm = r.rl[at, :]
+                gm = r.gb[at, :]
                 r.acc[4] = r.acc[4] + fold(step * gk)
                 r.acc[5] = r.acc[5] + fold(step * gm)
                 r.ab[at, :] = gk * r3 + gm * r4
                 r.bb[g, tile_of(i, 16), :] = gk * (1.0 - r3) + gm * (1.0 - r4)
 
         each(4, mixed_back)
-        for n, j, q, g in groups:
+        for n, j, q, g in groups_of(js):
             r.bts[j, q] = r.bb[g, 0:1, :]
             r.bb[g, 64:72, :] = jnp.where(row8 == 7, 0.0, pltpu.roll(r.bb[g, 0:8, :], 7, 0))
 
         def shifted(i):
-            for n, j, q, g in groups:
+            for n, j, q, g in groups_of(js):
                 at = pl.ds(pl.multiple_of(g * SPAN + i * 16, 16), 16)
                 r.gss[j, pl.ds(pl.multiple_of(q * SPAN + i * 16, 16), 16), :] = (
                     r.ab[at, :] + r.bb[g, pl.ds(pl.multiple_of(8 + i * 16, 8), 16), :]
                 ).astype(BF16)
 
         each(4, shifted)
-        for j in js:
+        for j in js[::-1]:
             b = t ^ (2 * j)
             copy = wire(
                 r.bts.at[j], r.btr.at[chip], bt_slot + j, s, (b + 7) % 8, bt_home + chip
@@ -1060,14 +1079,6 @@
 
         each(2, step)
 
-    def value_grad(half, ref):
-        def step(n):
-            part = dot_tn(r.hid[:, pl.ds(half * HALF, HALF)], r.gv[:, tile_of(n, 512)])
-            ref[2 * n] = part[:, 0:256].astype(BF16)
-            ref[2 * n + 1] = part[:, 256:512].astype(BF16)
-
-        each(2, step)
-
     middle_seg = (s == 1) | (s == 2)
     end_seg = (s == 0) | (s == 3)
 
@@ -1083,20 +1094,28 @@
                 self.part(chunk), self.landing(place), self.slot + place, seg, t
             )
 
+        def chunk(self, k):
+            if k == 1:
+                self.copy(s ^ 1, 0, s ^ 1).start()
+            if k == 2:
+
+                @pl.when(end_seg)
+                def _():
+                    self.copy(s ^ 2, 1, s ^ 2).start()
+
+            if k == 3:
+
+                @pl.when(end_seg)
+                def _():
+                    self.copy(s ^ 3, 3, s ^ 1).start()
+
+                @pl.when(middle_seg)
+                def _():
+                    self.copy(s ^ 3, 2, s ^ 3).start()
+
         def first(self):
-            @pl.when(end_seg)
-            def _():
-                self.copy(s ^ 3, 3, s ^ 1).start()
-
-            self.copy(s ^ 1, 0, s ^ 1).start()
-
-            @pl.when(end_seg)
-            def _():
-                self.copy(s ^ 2, 1, s ^ 2).start()
-
-            @pl.when(middle_seg)
-            def _():
-                self.copy(s ^ 3, 2, s ^ 3).start()
+            for k in (3, 1, 2):
+                self.chunk(k)
 
         def pump(self):
             self.pumped = True
@@ -1131,30 +1150,57 @@
     value_lines = []
 
     def value_first():
-        value_grad(1, r.fvs)
-        fv_in = send(r.fvs, r.fvr, slots(1), s, near)
-        value_grad(0, r.fvz)
-        arrive(fv_in)
-
-        def add_value(n):
-            for i in range(4):
-                rows = pl.ds(i * 128, 128)
-                r.fvz[n, rows, :] = (
-                    r.fvz[n, rows, :].astype(F32) + r.fvr[n, rows, :].astype(F32)
+        slot = slots(4)
+        line = LineSum(lambda n: r.fvz.at[n], lambda n: r.fvt.at[n])
+        value_lines.append(line)
+        fv_in = {}
+
+        def piece(half, k, ref):
+            def step(i):
+                cols = tile_of(s ^ k, 256)
+                ref[s ^ k] = dot_tn(
+                    r.hid[:, pl.ds(half * HALF, HALF)], r.gv[:, cols]
                 ).astype(BF16)
 
-        each(4, add_value)
-        value_lines.append(LineSum(lambda n: r.fvz.at[n], lambda n: r.fvt.at[n]))
-        value_lines[0].first()
+            each(1, step)
+
+        def to_sibling(k):
+            piece(1, k, r.fvs)
+            fv_in[k] = send(r.fvs.at[s ^ k], r.fvr.at[s ^ k], slot + k, s, near)
+
+        def settle(k):
+            arrive(fv_in[k])
+
+            def add(i):
+                rows = tile_of(i, 256)
+                r.fvz[s ^ k, rows, :] = (
+                    r.fvz[s ^ k, rows, :].astype(F32) + r.fvr[s ^ k, rows, :].astype(F32)
+                ).astype(BF16)
+
+            each(2, add)
+            line.chunk(k)
+
+        order = (3, 1, 2, 0)
+        to_sibling(3)
+        piece(0, 3, r.fvz)
+        for last, k in zip(order, order[1:]):
+            to_sibling(k)
+            settle(last)
+            piece(0, k, r.fvz)
+        settle(0)
 
     gs_in = []
-    block((0,))
-    sn_in.append(send(r.sng.at[0], r.sng.at[3], sn_slot + 3, s, across))
-    arrive(*sn_in[:2])
-    block((1, 2))
-    arrive(*cot_in, *sn_in[2:])
-    block((3,), value_first)
+    block_in((0,))
+    arrive(*sn_early)
+    sn_far = [pass_on(4, 1, 3, lower, side_y), pass_on(5, 2, 3, upper, side_x)]
+    arrive(*sn_in)
+    block_in((1, 2))
+    arrive(*cot_in, *sn_far)
+    block_in((3,))
+    value_first()
     value_line = value_lines[0]
+    block_out((2, 3))
+    block_out((0, 1))
     bt_in = [
         wire(r.bts.at[i], r.btr.at[i], bt_slot + i, s, near, bt_home + i) for i in range(4)
     ]
@@ -1434,7 +1480,8 @@
     for m in range(2):
         r.gz[m, own, :] = r.gk[m, :, tile_of(s, 256)]
 
-    for m, ref in enumerate((r.ab, r.rl, r.cc)):
+    thirds = (r.ab, r.gb, r.sr)
+    for m, ref in enumerate(thirds):
 
         def put_mixed(part):
             ref[own, :] = part
@@ -1453,7 +1500,7 @@
             at = pl.ds(pl.multiple_of(q * SPAN + i * 16, 16), 16)
             here = jnp.zeros((16, 1024), F32)
             ahead = jnp.zeros((16, 1024), F32)
-            for m, ref in enumerate((r.ab, r.rl, r.cc)):
+            for m, ref in enumerate(thirds):
                 part = ref[at, :]
                 ratio = r.ratio[m : m + 1, :]
                 r.acc[6 + m] = r.acc[6 + m] + fold(step * part)
@@ -1656,7 +1703,7 @@
         out_specs=[anywhere] * 10,
         scratch_shapes=[
             pltpu.VMEM(dims, kind)
-            for group in (SCRATCH, SMALL_IN, STAGED)
+            for group in (SCRATCH, HELD, STAGED)
             for dims, kind in group.values()
         ]
         + [
@@ -1689,8 +1736,9 @@
         hand_over,
         out_shape=[shape(x.shape, x.dtype) for x in big + small[:2]]
         + [shape((n, 32), F32) for n in (1, 1, 5, 2, 2)],
-        in_specs=[vmem] * 10,
-        out_specs=[vmem] * 14,
+        grid=(PARTS,),
+        in_specs=[part_spec(x.shape) for x in big] + [vmem] * 3,
+        out_specs=[part_spec(x.shape) for x in big] + [vmem] * 7,
     )(*big, *small)
     out, grad_in, att, wout, wrec, key, value, prev, init = done[:9]
     decay, first, ratios, gains, biases = done[9:]
@@ -1712,6 +1760,14 @@
     )
 
 
+PARTS = 2
+
+
+def part_spec(dims):
+    block = dims[:-2] + (dims[-2] // PARTS, dims[-1])
+    return pl.BlockSpec(block, lambda i: (0,) * (len(dims) - 2) + (i, 0))
+
+
 def hand_over(*refs):
     given, made = refs[:10], refs[10:24]
     for old, new in zip(given[:9], made):
@@ -1727,7 +1783,7 @@
         at += ref.shape[0]
 
 
-VMEM_LIMIT = 62 * 2**20
+VMEM_LIMIT = 63 * 2**20
 
 
 def solution(mesh):

time: 113 us -> 113 us (level)
  no operation moved by 1% of the time
where the time goes in v4:
time: 113 us
  Pallas kernels  112 us (99%)
    pallas_call x1, Pallas kernels, fused_call(): pl.pallas_call(fused, out_shape=out_shapes, in_specs=[anywhere] * 14, out...  109 us
    pallas_call x1, Pallas kernels, fused_call(): pl.pallas_call(hand_over, out_shape=[shape(x.shape, x.dtype) for x in big...  2.92 us

profile of v4, /device:TPU:0, one launch (start us, length us, event | category | flops | bytes accessed | tf_op | source)
XLA Modules:
  0.0 112.7 jit_solution(14824324166448901502)
XLA Ops:
  0.7 109.0 %shard_map.245 = (bf16[128,1024]{1,0:T(8,128)(2,1)}, f32[128,1024]{1,0:T(8,128)}, f32[4,128]{1,0:T(4,128)}, f32[3,2,128]{2,1,0:T(2,128)}, f32[16,256]{1,0:T(8,12...) custom-call(bf16[128,1024]{1,0:T(8,128)(2,1)} %bitcast.9, ...), custom_call_target="tpu_custom_call" | custom-call | tf_op jit(solution)/shard_map/pallas_call | solution.py:1699
  109.6 2.9 %shard_map.246 = (bf16[128,1024]{1,0:T(8,128)(2,1)}, f32[128,1024]{1,0:T(8,128)}, f32[3,128,256]{2,1,0:T(8,128)}, f32[128,256]{1,0:T(8,128)}, f32[128,256]{1,0:T...) custom-call(bf16[128,1024]{1,0:T(8,128)(2,1)} %get-tuple-element.38., ...), custom_call_target="tpu_custom_call" | custom-call | tf_op jit(solution)/shard_map/pallas_call | solution.py:1735

commit v5 on v4

--- a/solution.py
+++ b/solution.py
@@ -1257,6 +1257,7 @@
     key_line = LineSum(lambda n: r.fkz.at[tile_of(n, 256), :], lambda n: r.fkt.at[n])
     key_line.first()
     value_sum.pump()
+    value_line.pump()
 
     spread = (r.wval, r.mk)
     spread_base = (4, 0)
@@ -1394,7 +1395,7 @@
     weight_grad(3)
     weight_grad(2)
     weight_grad(4)
-    value_line.pump()
+    key_line.pump()
     plane_sums[3].pump()
     plane_sums[2].pump()
     arrive(*back_in)
@@ -1567,7 +1568,6 @@
     halo3 = send(r.hs3, r.hr3, slots(1), s, prior)
     plane_sums[4].pump()
     gather_plane(3)
-    key_line.pump()
     kv_start(0)
     gather_plane(2)
     kv_start(1)

time: 113 us -> 108 us (0.956)
  Pallas kernels: 112 us -> 107 us
    pallas_call x1, Pallas kernels: 109 us -> 104 us  [fused_call(): pl.pallas_call(fused, out_shape=out_shapes, in_specs=[anywhere] * 14, out...]
where the time goes in v5:
time: 108 us
  Pallas kernels  107 us (99%)
    pallas_call x1, Pallas kernels, fused_call(): pl.pallas_call(fused, out_shape=out_shapes, in_specs=[anywhere] * 14, out...  104 us
    pallas_call x1, Pallas kernels, fused_call(): pl.pallas_call(hand_over, out_shape=[shape(x.shape, x.dtype) for x in big...  2.92 us

profile of v5, /device:TPU:0, one launch (start us, length us, event | category | flops | bytes accessed | tf_op | source)
XLA Modules:
  0.0 107.6 jit_solution(12643327105713224244)
XLA Ops:
  0.7 103.9 %shard_map.245 = (bf16[128,1024]{1,0:T(8,128)(2,1)}, f32[128,1024]{1,0:T(8,128)}, f32[4,128]{1,0:T(4,128)}, f32[3,2,128]{2,1,0:T(2,128)}, f32[16,256]{1,0:T(8,12...) custom-call(bf16[128,1024]{1,0:T(8,128)(2,1)} %bitcast.9, ...), custom_call_target="tpu_custom_call" | custom-call | tf_op jit(solution)/shard_map/pallas_call | solution.py:1699
  104.5 2.9 %shard_map.246 = (bf16[128,1024]{1,0:T(8,128)(2,1)}, f32[128,1024]{1,0:T(8,128)}, f32[3,128,256]{2,1,0:T(8,128)}, f32[128,256]{1,0:T(8,128)}, f32[128,256]{1,0:T...) custom-call(bf16[128,1024]{1,0:T(8,128)(2,1)} %get-tuple-element.38., ...), custom_call_target="tpu_custom_call" | custom-call | tf_op jit(solution)/shard_map/pallas_call | solution.py:1735

commit v6 on v5

--- a/solution.py
+++ b/solution.py
@@ -1610,8 +1610,9 @@
             r.pvb[q, i : i + 1, :] = r.hr3[i, :, span]
             r.pvb[q, 2 + i : 3 + i, :] = r.bsum[i, :, span]
 
+    line_sums[3].pump()
     kv_next(0)
-    line_sums[3].pump()
+    line_sums[2].pump()
     kv_next(1)
     gather_plane(4)
     arrive(*vz_in)
@@ -1622,7 +1623,6 @@
         ref[x, 16:24, :] = r.pvb[(t ^ x) // 2]
     vt_slot = slots(8)
     vt_in = [send(r.vss.at[x], r.vt.at[x], vt_slot + x, s, t ^ x) for x in range(1, 8)]
-    line_sums[2].pump()
     line_sums[4].pump()
     kv_finish(0)
     kv_finish(1)

time: 108 us -> 108 us (level)
  no operation moved by 1% of the time
where the time goes in v6:
time: 108 us
  Pallas kernels  107 us (99%)
    pallas_call x1, Pallas kernels, fused_call(): pl.pallas_call(fused, out_shape=out_shapes, in_specs=[anywhere] * 14, out...  104 us
    pallas_call x1, Pallas kernels, fused_call(): pl.pallas_call(hand_over, out_shape=[shape(x.shape, x.dtype) for x in big...  2.92 us

profile of v6, /device:TPU:0, one launch (start us, length us, event | category | flops | bytes accessed | tf_op | source)
XLA Modules:
  0.0 107.6 jit_solution(3445993901440337273)
XLA Ops:
  0.7 103.8 %shard_map.245 = (bf16[128,1024]{1,0:T(8,128)(2,1)}, f32[128,1024]{1,0:T(8,128)}, f32[4,128]{1,0:T(4,128)}, f32[3,2,128]{2,1,0:T(2,128)}, f32[16,256]{1,0:T(8,12...) custom-call(bf16[128,1024]{1,0:T(8,128)(2,1)} %bitcast.9, ...), custom_call_target="tpu_custom_call" | custom-call | tf_op jit(solution)/shard_map/pallas_call | solution.py:1699
  104.5 2.9 %shard_map.246 = (bf16[128,1024]{1,0:T(8,128)(2,1)}, f32[128,1024]{1,0:T(8,128)}, f32[3,128,256]{2,1,0:T(8,128)}, f32[128,256]{1,0:T(8,128)}, f32[128,256]{1,0:T...) custom-call(bf16[128,1024]{1,0:T(8,128)(2,1)} %get-tuple-element.38., ...), custom_call_target="tpu_custom_call" | custom-call | tf_op jit(solution)/shard_map/pallas_call | solution.py:1735
